TPU v7x, 512 devices: a whole 4x4x16 slice. The times are simulated.
512 devices in a mesh: grp: 16 (over z), shard: 32 (over x, y, core).
Axes of the slice: x: 4, y: 4, z: 16, core: 2. Of those that a mesh axis runs over, the one named last changes fastest.
Arguments:
- owner_shard: int32 [2, 65536, 16, 1], P(None, ('grp', 'shard')), may hold values from 0 to 31; in each aligned block of 2048 rows (0 to 2047, 2048 to 4095, ..., all dimensions but the last counted through in order) at most 128 rows name the same one
- local_row: int32 [2, 65536, 16], P(None, ('grp', 'shard')), may hold values from 0 to 511
- click_label: int32 [2, 65536], P(None, ('grp', 'shard')), may hold values 0 or 1
- row_table: float32 [16384, 128], P('shard'), may hold values from -3 to 3
- squared_sums: float32 [16384, 128], P('shard'), may hold values from 0.01 to 1
- w_input: bfloat16 [512, 1024], replicated, may hold values from -0.25 to 0.25
- w_hidden: bfloat16 [1024, 1024], replicated, may hold values from -0.1875 to 0.1875
- w_output: bfloat16 [1024], replicated, may hold values from -0.1875 to 0.1875
Outputs:
- new_table: float32 [16384, 128], P('shard')
- logits: float32 [2, 65536], P(None, ('grp', 'shard'))
- input_grad: float32 [524288], P(('grp', 'shard'))
Inputs may be any that keep to these rules, and one draw needn't show every extreme that they name: `owner_shard`: within the ids of one device in one minibatch (aligned blocks of 2048 ids), at most 128 name the same owner shard, and that many do in some block.
All inputs are finite; a program needn't handle non-finite values. No bound on the sum of `click_label` on one device may be relied on, other than what follows from the above.
Results may differ from a plain program's by a relative error of at most 0.0039.
The roundings to bfloat16 on the way count: a program that leaves them out, or rounds other values in their place, can miss the bound.
Values may be sent and summed in bfloat16 or wider, within the bound.
No kernel may reach another device: no remote copies, remote signals or barrier semaphores. Data moves between devices by JAX's collectives and lax.ppermute only.
A program may use at most 64 MiB of HBM per device.

v0:
```python
import jax
import jax.numpy as jnp
from jax import lax
from jax.sharding import PartitionSpec as P

SLOTS = 4
HOT = 4


learn_rate = 0.1


def mlp_pass(rows, labels, w_input, w_hidden, w_output):
    count = rows.shape[0]
    width = rows.shape[2]
    pooled = jnp.sum(rows.reshape(count, SLOTS, HOT, width), axis=2, dtype=jnp.float32)
    pooled = pooled.astype(jnp.bfloat16).reshape(count, SLOTS * width)
    pre_one = jnp.dot(pooled, w_input, preferred_element_type=jnp.float32)
    act_one = jnp.maximum(pre_one, 0.0).astype(jnp.bfloat16)
    pre_two = jnp.dot(act_one, w_hidden, preferred_element_type=jnp.float32)
    act_two = jnp.maximum(pre_two, 0.0).astype(jnp.bfloat16)
    logits = jnp.dot(act_two, w_output, preferred_element_type=jnp.float32)
    slope = jax.nn.sigmoid(logits) - labels
    back_two = jnp.where(
        pre_two > 0, slope[:, None] * w_output.astype(jnp.float32)[None, :], 0.0
    ).astype(jnp.bfloat16)
    back_one = lax.dot_general(
        back_two, w_hidden, (((1,), (1,)), ((), ())), preferred_element_type=jnp.float32
    )
    back_one = jnp.where(pre_one > 0, back_one, 0.0).astype(jnp.bfloat16)
    back_in = lax.dot_general(
        back_one, w_input, (((1,), (1,)), ((), ())), preferred_element_type=jnp.float32
    )
    back_in = back_in.astype(jnp.bfloat16)
    weight_term = lax.dot_general(
        pooled, back_one, (((0,), (0,)), ((), ())), preferred_element_type=jnp.float32
    )
    lookup_grad = jnp.broadcast_to(
        back_in.reshape(count, SLOTS, 1, width), (count, SLOTS, HOT, width)
    )
    return (logits, lookup_grad.reshape(count * SLOTS * HOT, width), weight_term)


def place_slots(owner_ids, shards, capacity):
    batches = owner_ids.shape[0]
    onehot = (owner_ids[:, :, None] == jnp.arange(shards, dtype=jnp.int32)[None, None, :]).astype(
        jnp.int32
    )
    position = jnp.sum((jnp.cumsum(onehot, axis=1) - 1) * onehot, axis=2)
    offsets = jnp.arange(batches, dtype=jnp.int32)[:, None] * capacity
    return owner_ids * (batches * capacity) + offsets + position


def window_pass(owner_ids, row_ids, labels, table_low, w_input, w_hidden, w_output):
    batches, samples, looks = row_ids.shape
    shards = lax.axis_size("shard")
    row_count = table_low.shape[0]
    width = table_low.shape[1]
    capacity = 2 * samples * looks // shards
    flat_owner = owner_ids.reshape(batches, samples * looks)
    flat_row = row_ids.reshape(batches, samples * looks)
    slots = place_slots(flat_owner, shards, capacity).reshape(-1)
    columns = batches * capacity
    request = (
        jnp.zeros((shards * columns,), jnp.int32)
        .at[slots]
        .set(flat_row.reshape(-1))
        .reshape(shards, columns)
    )
    asked = lax.all_to_all(request, "shard", split_axis=0, concat_axis=0, tiled=True)
    served = lax.all_to_all(table_low[asked], "shard", split_axis=0, concat_axis=0, tiled=True)
    looked = served.reshape(shards * columns, width)[slots]
    logits, lookup_grad, weight_term = mlp_pass(
        looked.reshape(batches * samples, looks, width),
        labels.reshape(-1),
        w_input,
        w_hidden,
        w_output,
    )
    outgoing = (
        jnp.zeros((shards * columns, width), jnp.bfloat16)
        .at[slots]
        .set(lookup_grad)
        .reshape(shards, columns, width)
    )
    incoming = lax.all_to_all(outgoing, "shard", split_axis=0, concat_axis=0, tiled=True)
    row_grad = jax.ops.segment_sum(
        incoming.reshape(-1, width).astype(jnp.float32), asked.reshape(-1), num_segments=row_count
    )
    return (logits.reshape(batches, samples), row_grad, weight_term)


def adagrad_step(table_part, sums_part, grad_part):
    new_sums = sums_part + grad_part * grad_part
    return table_part - learn_rate * grad_part / jnp.sqrt(new_sums)


def local(
    owner_shard, local_row, click_label, row_table, squared_sums, w_input, w_hidden, w_output
):
    table_low = row_table.astype(jnp.bfloat16)
    owner_ids = owner_shard[..., 0]
    labels = click_label.astype(jnp.float32)
    logit_parts = []
    row_grad = jnp.zeros(row_table.shape, jnp.float32)
    weight_sum = jnp.zeros(w_input.shape, jnp.float32)
    for batch in range(local_row.shape[0]):
        part_logits, part_grad, part_weight = window_pass(
            owner_ids[batch : batch + 1],
            local_row[batch : batch + 1],
            labels[batch : batch + 1],
            table_low,
            w_input,
            w_hidden,
            w_output,
        )
        logit_parts.append(part_logits)
        row_grad = row_grad + part_grad
        weight_sum = weight_sum + part_weight
    logits = jnp.concatenate(logit_parts, axis=0)
    input_grad = lax.psum_scatter(
        weight_sum.reshape(-1), ("grp", "shard"), scatter_dimension=0, tiled=True
    )
    total = lax.psum(row_grad.astype(jnp.bfloat16), "grp").astype(jnp.float32)
    new_table = adagrad_step(row_table, squared_sums, total)
    return (new_table, logits, input_grad)


def solution(mesh):
    in_specs = (
        P(None, ("grp", "shard"), None, None),
        P(None, ("grp", "shard"), None),
        P(None, ("grp", "shard")),
        P("shard", None),
        P("shard", None),
        P(),
        P(),
        P(),
    )
    out_specs = (P("shard", None), P(None, ("grp", "shard")), P(("grp", "shard")))
    return jax.shard_map(local, mesh=mesh, in_specs=in_specs, out_specs=out_specs, check_vma=False)
```

profile of v0, /device:TPU:2, one launch (start us, length us, event | category | flops | bytes accessed | tf_op | source)
XLA Modules:
  0.0 805.7 jit_solution(14773861811707289974)
XLA Ops:
  8.4 9.1 %reduce-window.14 = s32[1,32,16,128]{3,2,1,0:T(8,128)S(1)} reduce-window(s32[1,32,16,128]{3,2,1,0:T(8,128)S(1)} %bitcast.139, s32[]{:T(128)} %constant.10.clone.1), window={size=1x1x1x128 pad=0_0x0_0x0_0x127_0}, to_apply=%region_0.0 | reduce-window | flops 8323072 | bytes 524292 | tf_op jit(solution)/shard_map/reduce-window
  18.8 8.6 %scatter_custom_fusion = s32[4096]{0:T(1024)} fusion(s32[2048]{0:T(1024)S(1)} %bitcast.151, s32[2048]{0:T(1024)S(1)} %reshape.501, s32[]{:T(128)} %constant.10.clone.1), kind=kCustom, calls=%fused_computation.85 | custom fusion | bytes 16388 | tf_op jit(solution)/shard_map/scatter | solution.py:67
  27.4 9.4 %all-to-all-start = ((s32[32,1,128]{2,1,0:T(1,128)}), s32[32,1,128]{2,1,0:T(1,128)S(1)}, u32[]{:S(2)}, u32[]{:S(2)}) async-start(s32[32,1,128]{2,1,0:T(1,128)} %bitcast.6), calls=%async_computation | async-start | bytes 32768 | tf_op jit(solution)/shard_map/all_to_all | solution.py:70
  37.1 9.1 %reduce-window.16 = s32[1,32,16,128]{3,2,1,0:T(8,128)S(1)} reduce-window(s32[1,32,16,128]{3,2,1,0:T(8,128)S(1)} %bitcast.140, s32[]{:T(128)} %constant.10.clone.1), window={size=1x1x1x128 pad=0_0x0_0x0_0x127_0}, to_apply=%region_7.8 | reduce-window | flops 8323072 | bytes 524292 | tf_op jit(solution)/shard_map/reduce-window.2
  47.5 8.6 %scatter_custom_fusion.3 = s32[4096]{0:T(1024)} fusion(s32[2048]{0:T(1024)S(1)} %bitcast.154, s32[2048]{0:T(1024)S(1)} %reshape.525, s32[]{:T(128)} %constant.10.clone.1), kind=kCustom, calls=%fused_computation.83 | custom fusion | bytes 16388 | tf_op jit(solution)/shard_map/scatter | solution.py:67
  56.1 7.4 all-to-all-start.3
  63.6 14.9 %gather_fusion = bf16[4096,128]{1,0:T(8,128)(2,1)} fusion(bf16[512,128]{1,0:T(8,128)(2,1)S(1)} %convert_element_type.80, s32[4096]{0:T(1024)S(1)} %fusion.44), kind=kCustom, calls=%fused_computation | custom fusion | bytes 2113536 | tf_op jit(solution)/shard_map/gather | solution.py:71
  78.5 7.4 all-to-all-start.1
  85.9 14.9 %gather_fusion.2 = bf16[4096,128]{1,0:T(8,128)(2,1)} fusion(bf16[512,128]{1,0:T(8,128)(2,1)S(1)} %convert_element_type.80, s32[4096]{0:T(1024)S(1)} %fusion.46), kind=kCustom, calls=%fused_computation.2 | custom fusion | bytes 2113536 | tf_op jit(solution)/shard_map/gather | solution.py:71
  100.8 7.6 all-to-all-start.4
  109.1 8.0 gather_fusion.1
  118.8 4.1 all-to-all-done.4
  122.9 9.1 %gather_fusion.3 = bf16[2048,128]{1,0:T(8,128)(2,1)} fusion(bf16[4096,128]{1,0:T(8,128)(2,1)} %bitcast.29, s32[2048]{0:T(1024)S(1)} %broadcast_clamp_fusion), kind=kCustom, calls=%fused_computation.3 | custom fusion | bytes 1056768 | tf_op jit(solution)/shard_map/gather | solution.py:72
  142.3 7.1 scatter_custom_fusion.1
  149.5 6.9 all-to-all-start.2
  156.4 2.1 fusion.5
  161.4 7.0 scatter_custom_fusion.4
  168.4 2.7 fusion.33
  171.1 7.6 all-to-all-start.5
  178.8 2.0 add_bitcast_fusion
  182.9 27.2 %scatter_custom_fusion.2 = f32[512,128]{1,0:T(8,128)} fusion(s32[4096]{0:T(1024)S(1)} %bitcast.144, bf16[4096,128]{1,0:T(8,128)(2,1)} %bitcast.36, f32[]{:T(128)} %constant.9.clone.1), kind=kCustom, calls=%fused_computation.12 | custom fusion | flops 1048576 | bytes 1310724 | tf_op jit(solution)/shard_map/scatter-add | solution.py:87
  210.1 26.8 %scatter_custom_fusion.5 = f32[512,128]{1,0:T(8,128)} fusion(s32[4096]{0:T(1024)} %bitcast.146, bf16[4096,128]{1,0:T(8,128)(2,1)S(1)} %bitcast.131, f32[]{:T(128)} %constant.9.clone.1), kind=kCustom, calls=%fused_computation.10 | custom fusion | flops 1048576 | bytes 1311232 | tf_op jit(solution)/shard_map/scatter-add | solution.py:87
  239.3 423.6 %all-reduce.6.cloned.1.call-done = f32[524288]{0:T(1024)} async-done(((f32[524288]{0:T(1024)}), f32[524288]{0:T(1024)}) %all-reduce.6.cloned.1.call-update) | async-done | bytes 2097168
  664.1 133.0 %all-reduce.4.cloned.1.call-done = bf16[512,128]{1,0:T(8,128)(2,1)} async-done(((bf16[512,128]{1,0:T(8,128)(2,1)}), bf16[512,128]{1,0:T(8,128)(2,1)}) %all-reduce.4.cloned.1.call-update) | async-done | bytes 131088 | tf_op jit(solution)/shard_map/psum | solution.py:124
  (113 shorter events, 26.9 us)
Async XLA Ops:
  7.2 127.2 %copy-start = (bf16[1024,1024]{1,0:T(8,128)(2,1)S(1)}, bf16[1024,1024]{1,0:T(8,128)(2,1)}, u32[]{:S(2)}) copy-start(bf16[1024,1024]{1,0:T(8,128)(2,1)} %param.14) | copy-start | bytes 6291460
  7.2 11.3 %copy-start.13 = (s32[2,128,16]{1,2,0:T(8,128)S(1)}, s32[2,128,16]{1,2,0:T(8,128)}, u32[]{:S(2)}) copy-start(s32[2,128,16]{1,2,0:T(8,128)} %param.9) | copy-start | bytes 49156
  18.8 90.3 %copy-start.11 = (s32[2048,1]{0,1:T(1,128)}, s32[2048,1]{0,1:T(1,128)S(1)}, u32[]{:S(2)}) copy-start(s32[2048,1]{0,1:T(1,128)S(1)} %compare_select_fusion.1) | copy-start | bytes 24580
  27.4 28.8 %all-to-all-start = ((s32[32,1,128]{2,1,0:T(1,128)}), s32[32,1,128]{2,1,0:T(1,128)S(1)}, u32[]{:S(2)}, u32[]{:S(2)}) async-start(s32[32,1,128]{2,1,0:T(1,128)} %bitcast.6), calls=%async_computation | async-start | bytes 32768 | tf_op jit(solution)/shard_map/all_to_all | solution.py:70
  37.0 10.3 %copy-start.7 = (f32[512,128]{1,0:T(8,128)S(1)}, f32[512,128]{1,0:T(8,128)}, u32[]{:S(2)}) copy-start(f32[512,128]{1,0:T(8,128)} %param.11) | copy-start | bytes 786436
  47.3 61.8 %copy-start.12 = (s32[2048,1]{0,1:T(1,128)}, s32[2048,1]{0,1:T(1,128)S(1)}, u32[]{:S(2)}) copy-start(s32[2048,1]{0,1:T(1,128)S(1)} %compare_select_fusion) | copy-start | bytes 24580
  56.1 22.4 %all-to-all-start.3 = ((s32[32,1,128]{2,1,0:T(1,128)}), s32[32,1,128]{2,1,0:T(1,128)S(1)}, u32[]{:S(2)}, u32[]{:S(2)}) async-start(s32[32,1,128]{2,1,0:T(1,128)} %bitcast.24), calls=%async_computation.3 | async-start | bytes 32768 | tf_op jit(solution)/shard_map/all_to_all | solution.py:70
  78.5 22.3 %copy-start.9 = (s32[32,1,128]{2,1,0:T(1,128)}, s32[32,1,128]{2,1,0:T(1,128)S(1)}, u32[]{:S(2)}) copy-start(s32[32,1,128]{2,1,0:T(1,128)S(1)} %all-to-all-done.3) | copy-start | bytes 49156
  78.5 22.3 %all-to-all-start.1 = ((bf16[32,128,128]{2,1,0:T(8,128)(2,1)}), bf16[32,128,128]{2,1,0:T(8,128)(2,1)S(1)}, u32[]{:S(2)}, u32[]{:S(2)}) async-start(bf16[32,128,128]{2,1,0:T(8,128)(2,1)} %bitcast.130), calls=%async_computation.1 | async-start | bytes 2097152 | tf_op jit(solution)/shard_map/all_to_all | solution.py:71
  100.8 7.6 copy-start.14
  100.8 8.2 %copy-start.18 = (s32[2,128]{1,0:T(2,128)S(1)}, s32[2,128]{1,0:T(2,128)}, u32[]{:S(2)}) copy-start(s32[2,128]{1,0:T(2,128)} %param.10) | copy-start | bytes 3076
  100.8 22.1 %all-to-all-start.4 = ((bf16[32,128,128]{2,1,0:T(8,128)(2,1)}), bf16[32,128,128]{2,1,0:T(8,128)(2,1)}, u32[]{:S(2)}, u32[]{:S(2)}) async-start(bf16[32,128,128]{2,1,0:T(8,128)(2,1)} %bitcast.129), calls=%async_computation.4 | async-start | bytes 2097152 | tf_op jit(solution)/shard_map/all_to_all | solution.py:71
  118.8 14.9 %copy-start.6 = (bf16[128,4,128]{2,1,0:T(4,128)(2,1)}, bf16[128,4,128]{2,1,0:T(4,128)(2,1)S(1)}, u32[]{:S(2)}) copy-start(bf16[128,4,128]{2,1,0:T(4,128)(2,1)S(1)} %reduce_sum.48) | copy-start | bytes 393220
  122.9 10.8 %copy-start.1 = (bf16[512,1024]{1,0:T(8,128)(2,1)S(1)}, bf16[512,1024]{1,0:T(8,128)(2,1)}, u32[]{:S(2)}) copy-start(bf16[512,1024]{1,0:T(8,128)(2,1)} %param.13) | copy-start | bytes 3145732
  134.4 0.9 copy-start.2
  134.9 2.0 copy-start.10
  149.5 21.6 %all-to-all-start.2 = ((bf16[32,128,128]{2,1,0:T(8,128)(2,1)}), bf16[32,128,128]{2,1,0:T(8,128)(2,1)}, u32[]{:S(2)}, u32[]{:S(2)}) async-start(bf16[32,128,128]{2,1,0:T(8,128)(2,1)} %bitcast.132), calls=%async_computation.2 | async-start | bytes 2097152 | tf_op jit(solution)/shard_map/all_to_all | solution.py:86
  171.1 7.6 copy-start.5
  171.1 39.0 %all-to-all-start.5 = ((bf16[32,128,128]{2,1,0:T(8,128)(2,1)}), bf16[32,128,128]{2,1,0:T(8,128)(2,1)S(1)}, u32[]{:S(2)}, u32[]{:S(2)}) async-start(bf16[32,128,128]{2,1,0:T(8,128)(2,1)} %bitcast.34), calls=%async_computation.5 | async-start | bytes 2097152 | tf_op jit(solution)/shard_map/all_to_all | solution.py:86
  178.7 484.1 %all-reduce.6.cloned.1.call-start = ((), (), s32[]{:S(2)}) async-start(), calls=%async_computation.7 | async-start | bytes 4194304
  182.6 56.1 %copy-start.16 = (f32[1,128]{1,0:T(1,128)S(1)}, f32[1,128]{1,0:T(1,128)}, u32[]{:S(2)}) copy-start(f32[1,128]{1,0:T(1,128)} %copy-done.15) | copy-start | bytes 1540
  182.6 56.1 %copy-start.17 = (f32[1,128]{1,0:T(1,128)S(1)}, f32[1,128]{1,0:T(1,128)}, u32[]{:S(2)}) copy-start(f32[1,128]{1,0:T(1,128)} %get-tuple-element.11) | copy-start | bytes 1540
  182.6 614.4 %copy-start.8 = (f32[512,128]{1,0:T(8,128)S(1)}, f32[512,128]{1,0:T(8,128)}, u32[]{:S(2)}) copy-start(f32[512,128]{1,0:T(8,128)} %param.11) | copy-start | bytes 786436
  182.6 614.4 %all-reduce.4.cloned.1.call-start = ((), (), s32[]{:S(2)}) async-start(), calls=%async_computation.6 | async-start | bytes 262144 | tf_op jit(solution)/shard_map/psum | solution.py:124
  (3 other events, 2.2 us)
Sparse Core Ops, SparseCore 0:
  184.9 477.8 all-reduce.5
  665.1 131.9 all-reduce.3
where the time goes:
time: 807 us; the launch traced here: 806 us
  waiting for transfers between devices  561 us (70%)
  local copies, waits for them, and re-layouts  89.7 us (11%)
  other arithmetic  81.8 us (10%)
  starting transfers between devices  46.6 us (6%)
  between operations  14.6 us (2%)
  matrix products  12.4 us (2%)
    unnamed x3, waiting for transfers between devices  424 us
    psum x1, waiting for transfers between devices, local(): total = lax.psum(row_grad.astype(jnp.bfloat16), 'grp').astype(jnp.float32)  133 us
    scatter-add x2, other arithmetic, window_pass(): jax.ops.segment_sum(incoming.reshape(-1, width).astype(jnp.float32), aske...  54 us
    gather x2, local copies, waits for them, and re-layouts, window_pass(): table_low[asked]  29.8 us
    another operation x4, other arithmetic  18.5 us
    scatter x2, local copies, waits for them, and re-layouts, window_pass(): request = jnp.zeros((shards * columns,), jnp.int32).at[slots].set(flat_ro...  17.2 us
    gather x2, local copies, waits for them, and re-layouts, window_pass(): looked = served.reshape(shards * columns, width)[slots]  17 us
    all_to_all x2, starting transfers between devices, window_pass(): lax.all_to_all(request, 'shard', split_axis=0, concat_axis=0, tiled=True)  16.9 us
  transfers between devices with their start and end apart: 8, of which 3 were waited for; matrix products, arithmetic and copies ran while one was open for 17% of the time, Pallas kernels for 0%

commit v1 on v0

v1 whole, which is shorter than its diff:
```python
import jax
import jax.numpy as jnp
from jax import lax
from jax.experimental import pallas as pl
from jax.experimental.pallas import tpu as pltpu
from jax.sharding import PartitionSpec as P

bf16 = jnp.bfloat16
f32 = jnp.float32
learn_rate = 0.1

SLOTS = 4
HOT = 4
LOOK = 16
SHARDS = 32
CAP = 128
BATCHES = 2
GRAD_ROWS = BATCHES * CAP
TERM_ROWS = 128
ID_ROWS = 16
SENT_ROWS = GRAD_ROWS + TERM_ROWS + ID_ROWS

FIRST = [[x * 8 + y * 2 for x in range(4)] for y in range(4)] + [
    [x * 8 + y * 2 + 1 for y in range(4)] for x in range(4)
]
SECOND = [[x * 8 + y * 2 for y in range(4)] for x in range(4)] + [
    [x * 8 + y * 2 + 1 for x in range(4)] for y in range(4)
]
SWAP = [(i, i ^ 1) for i in range(SHARDS)]
NEAR = [[4 * i + j for j in range(4)] for i in range(4)]
FAR = [[4 * i + j for i in range(4)] for j in range(4)]


def exchange(value, axis, groups=None):
    return lax.all_to_all(
        value, axis, split_axis=0, concat_axis=0, tiled=True, axis_index_groups=groups
    )


def spread(value, axis, groups):
    return exchange(jnp.broadcast_to(value[None], (4,) + value.shape), axis, groups)


def gather_table(table_low):
    rows, width = table_low.shape
    line = spread(table_low, "shard", FIRST).reshape(4 * rows, width)
    own = spread(line, "shard", SECOND).reshape(16 * rows, width)
    other = lax.ppermute(own, "shard", SWAP)
    return own, other


def dot(a, b, dims):
    return lax.dot_general(a, b, (dims, ((), ())), preferred_element_type=f32)


def column(row):
    return jnp.transpose(jnp.broadcast_to(row, (128, 128)))[:, 0:1]


def main_kernel(
    index_ref,
    place_ref,
    own_ref,
    other_ref,
    label_ref,
    w_input_ref,
    w_hidden_ref,
    w_output_ref,
    ids_ref,
    sent_ref,
    logit_ref,
    table_ref,
    pooled_ref,
    slot_ref,
    term_ref,
):
    half = own_ref.shape[0]
    samples = pooled_ref.shape[0] // SLOTS

    def widen(step, carry):
        at = pl.multiple_of(step * 256, 256)
        table_ref[pl.ds(at, 256), :] = own_ref[pl.ds(at, 256), :].astype(f32)
        table_ref[pl.ds(half + at, 256), :] = other_ref[pl.ds(at, 256), :].astype(f32)
        return carry

    lax.fori_loop(0, half // 256, widen, 0)

    def look(sample, carry):
        for slot in range(SLOTS):
            first = sample * LOOK + slot * HOT
            total = table_ref[pl.ds(index_ref[first], 1), :]
            for hot in range(1, HOT):
                total = total + table_ref[pl.ds(index_ref[first + hot], 1), :]
            pooled_ref[pl.ds(slot * samples + sample, 1), :] = total
        return carry

    lax.fori_loop(0, samples, look, 0, unroll=4)

    def clear(step, carry):
        slot_ref[pl.ds(pl.multiple_of(step * 256, 256), 256), :] = jnp.zeros((256, 128), f32)
        return carry

    lax.fori_loop(0, slot_ref.shape[0] // 256, clear, 0)

    pooled = jnp.concatenate(
        [pooled_ref[slot * samples : (slot + 1) * samples, :].astype(bf16) for slot in range(SLOTS)],
        axis=1,
    )
    w_input = w_input_ref[...]
    w_hidden = w_hidden_ref[...]
    w_output = w_output_ref[...].astype(f32)
    labels = jnp.concatenate([column(label_ref[b : b + 1, :]) for b in range(BATCHES)], axis=0)
    pre_one = dot(pooled, w_input, ((1,), (0,)))
    act_one = jnp.maximum(pre_one, 0.0).astype(bf16)
    pre_two = dot(act_one, w_hidden, ((1,), (0,)))
    act_two = jnp.maximum(pre_two, 0.0).astype(bf16).astype(f32)
    logits = jnp.sum(act_two * w_output, axis=1, keepdims=True)
    for b in range(BATCHES):
        part = jnp.broadcast_to(logits[b * 128 : (b + 1) * 128], (128, 128))
        logit_ref[b : b + 1, :] = jnp.transpose(part)[0:1, :]
    slope = jax.nn.sigmoid(logits) - labels
    back_two = jnp.where(pre_two > 0, slope * w_output, 0.0).astype(bf16)
    back_one = dot(back_two, w_hidden, ((1,), (1,)))
    back_one = jnp.where(pre_one > 0, back_one, 0.0).astype(bf16)
    back_in = dot(back_one, w_input, ((1,), (1,))).astype(bf16).astype(f32)
    for slot in range(SLOTS):
        pooled_ref[slot * samples : (slot + 1) * samples, :] = back_in[:, slot * 128 : (slot + 1) * 128]
    inner = pooled.shape[1]
    for j in range(term_ref.shape[0] // inner):
        term_ref[j * inner : (j + 1) * inner, :] = dot(
            pooled, back_one[:, j * 128 : (j + 1) * 128], ((0,), (0,))
        )

    def scatter(sample, carry):
        for slot in range(SLOTS):
            first = sample * LOOK + slot * HOT
            row = pooled_ref[pl.ds(slot * samples + sample, 1), :]
            for hot in range(HOT):
                slot_ref[pl.ds(place_ref[first + hot], 1), :] = row
        return carry

    lax.fori_loop(0, samples, scatter, 0, unroll=4)

    def pack(owner, carry):
        at = pl.multiple_of(owner * GRAD_ROWS, GRAD_ROWS)
        sent_ref[owner, 0:GRAD_ROWS, :] = slot_ref[pl.ds(at, GRAD_ROWS), :].astype(bf16)
        sent_ref[owner, GRAD_ROWS : GRAD_ROWS + TERM_ROWS, :] = term_ref[
            pl.ds(owner, TERM_ROWS, stride=SHARDS), :
        ].astype(bf16)
        sent_ref[owner, GRAD_ROWS + TERM_ROWS : SENT_ROWS, :] = ids_ref[owner]
        return carry

    lax.fori_loop(0, SHARDS, pack, 0)


def run_main(index, place, own, other, labels, w_input, w_hidden, w_output, ids):
    width = own.shape[1]
    samples = index.shape[0] // LOOK
    smem = pl.BlockSpec(memory_space=pltpu.SMEM)
    vmem = pl.BlockSpec(memory_space=pltpu.VMEM)
    return pl.pallas_call(
        main_kernel,
        out_shape=(
            jax.ShapeDtypeStruct((SHARDS, SENT_ROWS, width), bf16),
            jax.ShapeDtypeStruct((BATCHES, samples // BATCHES), f32),
        ),
        in_specs=[smem, smem] + [vmem] * 7,
        out_specs=(vmem, vmem),
        scratch_shapes=[
            pltpu.VMEM((2 * own.shape[0], width), f32),
            pltpu.VMEM((samples * SLOTS, width), f32),
            pltpu.VMEM((SHARDS * GRAD_ROWS, width), f32),
            pltpu.VMEM((SHARDS * TERM_ROWS, width), f32),
        ],
        compiler_params=pltpu.CompilerParams(vmem_limit_bytes=50 * 1024 * 1024),
        cost_estimate=pl.CostEstimate(
            flops=2_000_000_000, bytes_accessed=12_000_000, transcendentals=256
        ),
    )(index, place, own, other, labels, w_input, w_hidden, w_output, ids)


def owner_kernel(got_ref, out_ref, sum_ref, term_ref):
    step = pl.program_id(0)

    @pl.when(step == 0)
    def _():
        sum_ref[...] = jnp.zeros_like(sum_ref)
        term_ref[...] = jnp.zeros_like(term_ref)

    names = lax.broadcasted_iota(jnp.int32, (sum_ref.shape[0], CAP), 0).astype(f32) + 1.0
    total = sum_ref[...]
    term = term_ref[...]
    for source in range(got_ref.shape[0]):
        coded = got_ref[source, GRAD_ROWS + TERM_ROWS : SENT_ROWS, :].astype(f32)
        picks = []
        for b in range(BATCHES):
            named = coded[b : b + 1] * 256.0 + coded[BATCHES + b : BATCHES + b + 1]
            picks.append(jnp.where(names == named, 1.0, 0.0).astype(bf16))
        pick = jnp.concatenate(picks, axis=1)
        total = total + dot(pick, got_ref[source, 0:GRAD_ROWS, :], ((1,), (0,)))
        term = term + got_ref[source, GRAD_ROWS : GRAD_ROWS + TERM_ROWS, :].astype(f32)
    sum_ref[...] = total
    term_ref[...] = term

    @pl.when(step == pl.num_programs(0) - 1)
    def _():
        for k in range(4):
            out_ref[k, 0:128, :] = sum_ref[k * 128 : (k + 1) * 128, :].astype(bf16)
            part = term_ref[pl.ds(k, 32, stride=4), :]
            high = part.astype(bf16)
            out_ref[k, 128:160, :] = high
            out_ref[k, 160:192, :] = (part - high.astype(f32)).astype(bf16)


def run_owner(got, rows):
    width = got.shape[2]
    return pl.pallas_call(
        owner_kernel,
        grid=(8,),
        out_shape=jax.ShapeDtypeStruct((4, 192, width), bf16),
        in_specs=[pl.BlockSpec((SHARDS // 8, SENT_ROWS, width), lambda i: (i, 0, 0))],
        out_specs=pl.BlockSpec((4, 192, width), lambda i: (0, 0, 0)),
        scratch_shapes=[
            pltpu.VMEM((rows, width), f32),
            pltpu.VMEM((TERM_ROWS, width), f32),
        ],
        compiler_params=pltpu.CompilerParams(vmem_limit_bytes=32 * 1024 * 1024),
        cost_estimate=pl.CostEstimate(
            flops=1_100_000_000, bytes_accessed=3_500_000, transcendentals=0
        ),
    )(got)


def plan_slots(owner, row):
    batches, samples, looks = owner.shape
    names = jnp.arange(SHARDS, dtype=jnp.int32)
    hit = (owner[..., None] == names).astype(bf16).reshape(batches, samples, looks * SHARDS)
    steps = jnp.arange(samples)
    before = (steps[None, :] < steps[:, None]).astype(bf16)
    rank = jnp.einsum("ts,bsn->btn", before, hit, preferred_element_type=f32)
    counts = jnp.sum(hit.astype(f32), axis=1).reshape(batches, looks, SHARDS)
    turn = jnp.arange(looks)
    base = jnp.sum(
        jnp.where((turn[None, :] < turn[:, None])[None, :, :, None], counts[:, None], 0.0), axis=2
    ).reshape(batches, 1, looks * SHARDS)
    spot = jnp.sum(
        (hit.astype(f32) * (rank + base)).reshape(batches, samples, looks, SHARDS), axis=3
    ).astype(jnp.int32)
    batch = jnp.arange(batches, dtype=jnp.int32)[:, None, None]
    place = owner * GRAD_ROWS + batch * CAP + spot
    code = row + 1
    high = (code >> 8).astype(bf16)
    low = (code & 255).astype(bf16)
    flat_hit = hit.reshape(batches, samples * looks, SHARDS)
    coded = jnp.concatenate(
        [flat_hit * high.reshape(batches, -1, 1), flat_hit * low.reshape(batches, -1, 1)], axis=2
    )
    where = (spot.reshape(batches, -1, 1) == jnp.arange(CAP, dtype=jnp.int32)).astype(bf16)
    ids = jnp.einsum("bin,bip->bnp", coded, where, preferred_element_type=f32).astype(bf16)
    ids = ids.reshape(batches, 2, SHARDS, CAP).transpose(2, 1, 0, 3).reshape(SHARDS, 2 * batches, CAP)
    ids = jnp.pad(ids, ((0, 0), (0, ID_ROWS - 2 * batches), (0, 0)))
    return place.reshape(-1), ids


def table_index(owner, row, rows):
    core = lax.axis_index("shard") & 1
    x, y, c = owner >> 3, (owner >> 1) & 3, owner & 1
    chip = jnp.where(c == 0, y * 4 + x, x * 4 + y)
    return (((c ^ core) * 16 + chip) * rows + row).reshape(-1)


def adagrad_step(table_part, sums_part, grad_part):
    new_sums = sums_part + grad_part * grad_part
    return table_part - learn_rate * grad_part / jnp.sqrt(new_sums)


def local(
    owner_shard, local_row, click_label, row_table, squared_sums, w_input, w_hidden, w_output
):
    rows, width = row_table.shape
    owner = owner_shard[..., 0]
    own, other = gather_table(row_table.astype(bf16))
    index = table_index(owner, local_row, rows)
    place, ids = plan_slots(owner, local_row)
    sent, logits = run_main(
        index,
        place,
        own,
        other,
        click_label.astype(f32),
        w_input,
        w_hidden,
        w_output.reshape(1, -1),
        ids,
    )
    near = exchange(run_owner(exchange(sent, "shard"), rows), "grp", NEAR).astype(f32)
    grads = jnp.sum(near[:, 0:128], axis=0).astype(bf16)
    term = jnp.sum(near[:, 128:160] + near[:, 160:192], axis=0)
    term = term.reshape(8, 4, width).transpose(1, 0, 2)
    high = term.astype(bf16)
    low = (term - high.astype(f32)).astype(bf16)
    far = jnp.concatenate([jnp.broadcast_to(grads[None], (4, 128, width)), high, low], axis=1)
    far = exchange(far, "grp", FAR).astype(f32)
    input_grad = jnp.sum(far[:, 128:136] + far[:, 136:144], axis=0).reshape(-1)
    part = jnp.sum(far[:, 0:128], axis=0).astype(bf16)
    total = spread(part, "grp", NEAR).reshape(rows, width).astype(f32)
    new_table = adagrad_step(row_table, squared_sums, total)
    return (new_table, logits, input_grad)


def solution(mesh):
    in_specs = (
        P(None, ("grp", "shard"), None, None),
        P(None, ("grp", "shard"), None),
        P(None, ("grp", "shard")),
        P("shard", None),
        P("shard", None),
        P(),
        P(),
        P(),
    )
    out_specs = (P("shard", None), P(None, ("grp", "shard")), P(("grp", "shard")))
    return jax.shard_map(local, mesh=mesh, in_specs=in_specs, out_specs=out_specs, check_vma=False)
```

time: 807 us -> 160 us (0.20)
  the two profiles are of different devices: /device:TPU:2 before, /device:TPU:32 now
where the time goes in v1:
time: 160 us; the launch traced here: 159 us
  blocking collectives  117 us (73%)
  Pallas kernels  21.5 us (13%)
  starting transfers between devices  7.28 us (5%)
  waiting for transfers between devices  4.85 us (3%)
  other arithmetic  3.15 us (2%)
  local copies, waits for them, and re-layouts  2.92 us (2%)
    all_to_all x5, blocking collectives, exchange(): lax.all_to_all(value, axis, split_axis=0, concat_axis=0, tiled=True, axis...  117 us
    pallas_call x1, Pallas kernels, run_main(): pl.pallas_call(main_kernel, out_shape=(jax.ShapeDtypeStruct((SHARDS, SENT...  17.8 us
    all_to_all x1, starting transfers between devices, exchange(): lax.all_to_all(value, axis, split_axis=0, concat_axis=0, tiled=True, axis...  5.37 us
    all_to_all x1, waiting for transfers between devices, exchange(): lax.all_to_all(value, axis, split_axis=0, concat_axis=0, tiled=True, axis...  4.57 us
    pallas_call x1, Pallas kernels, run_owner(): pl.pallas_call(owner_kernel, grid=(8,), out_shape=jax.ShapeDtypeStruct((4...  3.63 us
  transfers between devices with their start and end apart: 2, of which 2 were waited for; matrix products, arithmetic and copies ran while one was open for 3% of the time, Pallas kernels for 0%

profile of v1, /device:TPU:32, one launch (start us, length us, event | category | flops | bytes accessed | tf_op | source)
XLA Modules:
  0.0 159.4 jit_solution(7533922429894356837)
XLA Ops:
  0.6 1.0 convert_element_type.87
  1.7 12.2 %all_to_all.30 = bf16[4,512,128]{2,1,0:T(8,128)(2,1)S(1)} all-to-all(bf16[4,512,128]{2,1,0:T(8,128)(2,1)S(1)} %broadcast_in_dim.33), channel_id=1, replica_groups={{0,8,16,24},{2,10,18,26},{4,12,20,28},{6,14,22,30},{1,3,5,7},{9,11,13,1..., dimensions={0} | all-to-all | bytes 1048576 | tf_op jit(solution)/shard_map/all_to_all | solution.py:35
  13.9 0.3 broadcast_in_dim.35
  14.2 20.9 %all_to_all.31 = bf16[4,2048,128]{2,1,0:T(8,128)(2,1)S(1)} all-to-all(bf16[4,2048,128]{2,1,0:T(8,128)(2,1)S(1)} %broadcast_in_dim.35), channel_id=1, replica_groups={{0,2,4,6},{8,10,12,14},{16,18,20,22},{24,26,28,30},{1,9,17,25},{3,11,19..., dimensions={0} | all-to-all | bytes 4194304 | tf_op jit(solution)/shard_map/all_to_all | solution.py:35
  35.1 1.9 %collective-permute-start = (bf16[8192,128]{1,0:T(8,128)(2,1)S(1)}, bf16[8192,128]{1,0:T(8,128)(2,1)}, u32[]{:S(2)}, u32[]{:S(2)}) collective-permute-start(bf16[8192,128]{1,0:T(8,128)(2,1)S(1)} %bitcast.43), channel_id=1, source_target_pairs={{0,1},{1,0},{2,3},{3,2},{4,5},{5,4},{6,7},{7,6},{8,9},{9,8},{10,11... | collective-permute-start | bytes 6291464 | tf_op jit(solution)/shard_map/ppermute | solution.py:48
  37.1 0.2 convert_reduce_fusion
  37.3 0.1 select_reduce_fusion
  37.5 0.1 bitcast_compare_fusion
  37.7 0.3 bitcast_reduce_fusion
  38.5 0.1 copy.34
  38.6 0.1 mul.85
  38.9 0.1 mul.88
  39.9 1.0 fusion.3
  41.0 0.3 collective-permute-done.other_ref
  41.3 17.8 %shard_map.103 = (bf16[32,400,128]{2,1,0:T(8,128)(2,1)}, f32[2,128]{1,0:T(2,128)}) custom-call(s32[4096]{0:T(1024)S(1)} %reshape.93.index_ref, s32[4096]{0:T(1024)S(1)} %add_add_fusion.place_ref, bf16[8192,128]{1,0:T(8,128)(2,1)S(1)} %bitcast.44, bf16[8192,128]{1,0:T(8,128)(2,1)} %collective-permute-done.other_ref, ...), custom_call_target="tpu_custom_call" | custom-call | flops 2000000000 | bytes 12000000 | tf_op jit(solution)/shard_map/pallas_call | solution.py:161
  59.1 45.6 %all_to_all.32.got_ref = bf16[32,400,128]{2,1,0:T(8,128)(2,1)S(1)} all-to-all(bf16[32,400,128]{2,1,0:T(8,128)(2,1)} %get-tuple-element.5), channel_id=1, replica_groups=mesh['grp'=16,'shard'=32] {'shard'}, dimensions={0} | all-to-all | bytes 6553600 | tf_op jit(solution)/shard_map/all_to_all | solution.py:35
  104.7 3.6 %shard_map.104 = bf16[4,192,128]{2,1,0:T(8,128)(2,1)S(1)} custom-call(bf16[32,400,128]{2,1,0:T(8,128)(2,1)S(1)} %all_to_all.32.got_ref), custom_call_target="tpu_custom_call" | custom-call | flops 1100000000 | bytes 3500000 | tf_op jit(solution)/shard_map/pallas_call | solution.py:217
  108.4 12.1 %all_to_all.33 = bf16[4,192,128]{2,1,0:T(8,128)(2,1)S(1)} all-to-all(bf16[4,192,128]{2,1,0:T(8,128)(2,1)S(1)} %shard_map.104), channel_id=1, replica_groups={{0,32,64,96},{128,160,192,224},{256,288,320,352},{384,416,448,480},{1,3..., dimensions={0} | all-to-all | bytes 393216 | tf_op jit(solution)/shard_map/all_to_all | solution.py:35
  120.6 26.7 %all_to_all.34 = bf16[4,144,128]{2,1,0:T(8,128)(2,1)S(1)} all-to-all(bf16[4,144,128]{2,1,0:T(8,128)(2,1)S(1)} %pad_maximum_fusion), channel_id=1, replica_groups={{0,128,256,384},{32,160,288,416},{64,192,320,448},{96,224,352,480},{1,1..., dimensions={0} | all-to-all | bytes 294912 | tf_op jit(solution)/shard_map/all_to_all | solution.py:35
  147.4 0.7 broadcast_in_dim.60
  148.0 5.4 %all-to-all-start.5 = ((bf16[4,128,128]{2,1,0:T(8,128)(2,1)}), bf16[4,128,128]{2,1,0:T(8,128)(2,1)S(1)}, u32[]{:S(2)}, u32[]{:S(2)}) async-start(bf16[4,128,128]{2,1,0:T(8,128)(2,1)} %broadcast_in_dim.60), calls=%async_computation.5 | async-start | bytes 262144 | tf_op jit(solution)/shard_map/all_to_all | solution.py:35
  153.4 0.6 fusion.17
  154.0 4.6 %all-to-all-done.5 = bf16[4,128,128]{2,1,0:T(8,128)(2,1)S(1)} async-done(((bf16[4,128,128]{2,1,0:T(8,128)(2,1)}), bf16[4,128,128]{2,1,0:T(8,128)(2,1)S(1)}, u32[]{:S(2)}, u32[]{:S(2)}) %all-to-all-start.5) | async-done | bytes 131104 | tf_op jit(solution)/shard_map/all_to_all | solution.py:35
  158.6 0.8 fusion.13
  (52 shorter events, 1.9 us)
Async XLA Ops:
  14.1 23.0 %copy-start.2 = (s32[2,128,16,1]{1,3,2,0:T(1,128)S(1)}, s32[2,128,16,1]{1,3,2,0:T(1,128)}, u32[]{:S(2)}) copy-start(s32[2,128,16,1]{1,3,2,0:T(1,128)} %param.8) | copy-start | bytes 49156
  14.1 24.3 %copy-start.6 = (s32[2,128]{1,0:T(2,128)S(1)}, s32[2,128]{1,0:T(2,128)}, u32[]{:S(2)}) copy-start(s32[2,128]{1,0:T(2,128)} %param.10) | copy-start | bytes 3076
  14.2 24.3 %copy-start.5 = (bf16[1024]{0:T(1024)(128)(2,1)S(1)}, bf16[1024]{0:T(1024)(128)(2,1)}, u32[]{:S(2)}) copy-start(bf16[1024]{0:T(1024)(128)(2,1)} %param.15) | copy-start | bytes 6148
  14.2 24.3 %copy-start.4 = (s32[2,128,16]{1,2,0:T(8,128)S(1)}, s32[2,128,16]{1,2,0:T(8,128)}, u32[]{:S(2)}) copy-start(s32[2,128,16]{1,2,0:T(8,128)} %param.9) | copy-start | bytes 49156
  35.1 6.2 %collective-permute-start = (bf16[8192,128]{1,0:T(8,128)(2,1)S(1)}, bf16[8192,128]{1,0:T(8,128)(2,1)}, u32[]{:S(2)}, u32[]{:S(2)}) collective-permute-start(bf16[8192,128]{1,0:T(8,128)(2,1)S(1)} %bitcast.43), channel_id=1, source_target_pairs={{0,1},{1,0},{2,3},{3,2},{4,5},{5,4},{6,7},{7,6},{8,9},{9,8},{10,11... | collective-permute-start | bytes 6291464 | tf_op jit(solution)/shard_map/ppermute | solution.py:48
  38.5 2.8 %copy-start = (bf16[512,1024]{1,0:T(8,128)(2,1)S(1)}, bf16[512,1024]{1,0:T(8,128)(2,1)}, u32[]{:S(2)}) copy-start(bf16[512,1024]{1,0:T(8,128)(2,1)} %w_input_ref.1) | copy-start | bytes 3145732
  108.3 50.3 %copy-start.1 = (f32[512,128]{1,0:T(8,128)S(1)}, f32[512,128]{1,0:T(8,128)}, u32[]{:S(2)}) copy-start(f32[512,128]{1,0:T(8,128)} %param.11) | copy-start | bytes 786436
  108.4 50.3 %copy-start.3 = (f32[512,128]{1,0:T(8,128)S(1)}, f32[512,128]{1,0:T(8,128)}, u32[]{:S(2)}) copy-start(f32[512,128]{1,0:T(8,128)} %param.12) | copy-start | bytes 786436
  148.0 10.5 %all-to-all-start.5 = ((bf16[4,128,128]{2,1,0:T(8,128)(2,1)}), bf16[4,128,128]{2,1,0:T(8,128)(2,1)S(1)}, u32[]{:S(2)}, u32[]{:S(2)}) async-start(bf16[4,128,128]{2,1,0:T(8,128)(2,1)} %broadcast_in_dim.60), calls=%async_computation.5 | async-start | bytes 262144 | tf_op jit(solution)/shard_map/all_to_all | solution.py:35

commit v2 on v1

--- a/solution.py
+++ b/solution.py
@@ -60,30 +60,58 @@
 def main_kernel(
     index_ref,
     place_ref,
-    own_ref,
-    other_ref,
+    own_hbm,
+    other_hbm,
     label_ref,
+    w_input_hbm,
+    w_hidden_hbm,
+    w_output_ref,
+    ids_ref,
+    sent_hbm,
+    logit_ref,
+    half_ref,
     w_input_ref,
     w_hidden_ref,
-    w_output_ref,
-    ids_ref,
-    sent_ref,
-    logit_ref,
     table_ref,
     pooled_ref,
     slot_ref,
+    turn_ref,
     term_ref,
+    sent_ref,
+    half_sem,
+    weight_sem,
+    sent_sem,
 ):
-    half = own_ref.shape[0]
+    half = own_hbm.shape[0]
+    chunk = half // 2
     samples = pooled_ref.shape[0] // SLOTS
+    tables = []
+    for k in range(4):
+        source = (own_hbm, other_hbm)[k // 2].at[pl.ds((k % 2) * chunk, chunk)]
+        tables.append(
+            pltpu.make_async_copy(source, half_ref.at[pl.ds(k * chunk, chunk)], half_sem.at[k])
+        )
+    weights = [
+        pltpu.make_async_copy(w_input_hbm, w_input_ref, weight_sem.at[0]),
+        pltpu.make_async_copy(w_hidden_hbm, w_hidden_ref, weight_sem.at[1]),
+    ]
+    for copy in tables + weights:
+        copy.start()
+
+    def clear(step, carry):
+        slot_ref[pl.ds(pl.multiple_of(step * 256, 256), 256), :] = jnp.zeros((256, 128), f32)
+        return carry
+
+    lax.fori_loop(0, slot_ref.shape[0] // 256, clear, 0)
 
     def widen(step, carry):
         at = pl.multiple_of(step * 256, 256)
-        table_ref[pl.ds(at, 256), :] = own_ref[pl.ds(at, 256), :].astype(f32)
-        table_ref[pl.ds(half + at, 256), :] = other_ref[pl.ds(at, 256), :].astype(f32)
-        return carry
-
-    lax.fori_loop(0, half // 256, widen, 0)
+        table_ref[pl.ds(at, 256), :] = half_ref[pl.ds(at, 256), :].astype(f32)
+        return carry
+
+    for k in range(4):
+        tables[k].wait()
+        lax.fori_loop(k * chunk // 256, (k + 1) * chunk // 256, widen, 0)
 
     def look(sample, carry):
         for slot in range(SLOTS):
@@ -94,18 +122,29 @@
             pooled_ref[pl.ds(slot * samples + sample, 1), :] = total
         return carry
 
-    lax.fori_loop(0, samples, look, 0, unroll=4)
-
-    def clear(step, carry):
-        slot_ref[pl.ds(pl.multiple_of(step * 256, 256), 256), :] = jnp.zeros((256, 128), f32)
-        return carry
-
-    lax.fori_loop(0, slot_ref.shape[0] // 256, clear, 0)
-
+    lax.fori_loop(0, samples, look, 0, unroll=16)
+
+    features = SLOTS * 128
+    for slot in range(SLOTS):
+        for b in range(BATCHES):
+            block = pooled_ref[slot * samples + b * 128 : slot * samples + (b + 1) * 128, :]
+            turn_ref[b * features + slot * 128 : b * features + (slot + 1) * 128, :] = jnp.transpose(block)
+    turned = jnp.concatenate(
+        [
+            jnp.concatenate(
+                [turn_ref[pl.ds(b * features + s, 16, stride=SHARDS), :] for s in range(SHARDS)],
+                axis=0,
+            ).astype(bf16)
+            for b in range(BATCHES)
+        ],
+        axis=1,
+    )
     pooled = jnp.concatenate(
         [pooled_ref[slot * samples : (slot + 1) * samples, :].astype(bf16) for slot in range(SLOTS)],
         axis=1,
     )
+    for copy in weights:
+        copy.wait()
     w_input = w_input_ref[...]
     w_hidden = w_hidden_ref[...]
     w_output = w_output_ref[...].astype(f32)
@@ -125,11 +164,7 @@
     back_in = dot(back_one, w_input, ((1,), (1,))).astype(bf16).astype(f32)
     for slot in range(SLOTS):
         pooled_ref[slot * samples : (slot + 1) * samples, :] = back_in[:, slot * 128 : (slot + 1) * 128]
-    inner = pooled.shape[1]
-    for j in range(term_ref.shape[0] // inner):
-        term_ref[j * inner : (j + 1) * inner, :] = dot(
-            pooled, back_one[:, j * 128 : (j + 1) * 128], ((0,), (0,))
-        )
+    term_ref[...] = dot(turned, back_one, ((1,), (0,)))
 
     def scatter(sample, carry):
         for slot in range(SLOTS):
@@ -139,18 +174,31 @@
                 slot_ref[pl.ds(place_ref[first + hot], 1), :] = row
         return carry
 
-    lax.fori_loop(0, samples, scatter, 0, unroll=4)
+    lax.fori_loop(0, samples, scatter, 0, unroll=16)
 
     def pack(owner, carry):
         at = pl.multiple_of(owner * GRAD_ROWS, GRAD_ROWS)
         sent_ref[owner, 0:GRAD_ROWS, :] = slot_ref[pl.ds(at, GRAD_ROWS), :].astype(bf16)
-        sent_ref[owner, GRAD_ROWS : GRAD_ROWS + TERM_ROWS, :] = term_ref[
-            pl.ds(owner, TERM_ROWS, stride=SHARDS), :
-        ].astype(bf16)
+        piece = term_ref[pl.ds(pl.multiple_of(owner * 16, 16), 16), :].astype(bf16)
+        for j in range(8):
+            sent_ref[owner, GRAD_ROWS + j * 16 : GRAD_ROWS + (j + 1) * 16, :] = piece[
+                :, j * 128 : (j + 1) * 128
+            ]
         sent_ref[owner, GRAD_ROWS + TERM_ROWS : SENT_ROWS, :] = ids_ref[owner]
         return carry
 
-    lax.fori_loop(0, SHARDS, pack, 0)
+    parts = 4
+    step = SHARDS // parts
+    stores = []
+    for k in range(parts):
+        lax.fori_loop(k * step, (k + 1) * step, pack, 0, unroll=4)
+        piece = pl.ds(k * step, step)
+        stores.append(
+            pltpu.make_async_copy(sent_ref.at[piece], sent_hbm.at[piece], sent_sem.at[k])
+        )
+        stores[-1].start()
+    for copy in stores:
+        copy.wait()
 
 
 def run_main(index, place, own, other, labels, w_input, w_hidden, w_output, ids):
@@ -158,21 +206,30 @@
     samples = index.shape[0] // LOOK
     smem = pl.BlockSpec(memory_space=pltpu.SMEM)
     vmem = pl.BlockSpec(memory_space=pltpu.VMEM)
+    anywhere = pl.BlockSpec(memory_space=pl.ANY)
     return pl.pallas_call(
         main_kernel,
         out_shape=(
             jax.ShapeDtypeStruct((SHARDS, SENT_ROWS, width), bf16),
             jax.ShapeDtypeStruct((BATCHES, samples // BATCHES), f32),
         ),
-        in_specs=[smem, smem] + [vmem] * 7,
-        out_specs=(vmem, vmem),
+        in_specs=[smem, smem, anywhere, anywhere, vmem, anywhere, anywhere, vmem, vmem],
+        out_specs=(anywhere, vmem),
         scratch_shapes=[
+            pltpu.VMEM((2 * own.shape[0], width), bf16),
+            pltpu.VMEM(w_input.shape, bf16),
+            pltpu.VMEM(w_hidden.shape, bf16),
             pltpu.VMEM((2 * own.shape[0], width), f32),
             pltpu.VMEM((samples * SLOTS, width), f32),
             pltpu.VMEM((SHARDS * GRAD_ROWS, width), f32),
-            pltpu.VMEM((SHARDS * TERM_ROWS, width), f32),
+            pltpu.VMEM((BATCHES * SLOTS * width, samples // BATCHES), f32),
+            pltpu.VMEM(w_input.shape, f32),
+            pltpu.VMEM((SHARDS, SENT_ROWS, width), bf16),
+            pltpu.SemaphoreType.DMA((4,)),
+            pltpu.SemaphoreType.DMA((2,)),
+            pltpu.SemaphoreType.DMA((4,)),
         ],
-        compiler_params=pltpu.CompilerParams(vmem_limit_bytes=50 * 1024 * 1024),
+        compiler_params=pltpu.CompilerParams(vmem_limit_bytes=40 * 1024 * 1024),
         cost_estimate=pl.CostEstimate(
             flops=2_000_000_000, bytes_accessed=12_000_000, transcendentals=256
         ),
@@ -207,9 +264,7 @@
         for k in range(4):
             out_ref[k, 0:128, :] = sum_ref[k * 128 : (k + 1) * 128, :].astype(bf16)
             part = term_ref[pl.ds(k, 32, stride=4), :]
-            high = part.astype(bf16)
-            out_ref[k, 128:160, :] = high
-            out_ref[k, 160:192, :] = (part - high.astype(f32)).astype(bf16)
+            out_ref[k, 128:160, :] = part.astype(bf16)
 
 
 def run_owner(got, rows):
@@ -217,9 +272,9 @@
     return pl.pallas_call(
         owner_kernel,
         grid=(8,),
-        out_shape=jax.ShapeDtypeStruct((4, 192, width), bf16),
+        out_shape=jax.ShapeDtypeStruct((4, 160, width), bf16),
         in_specs=[pl.BlockSpec((SHARDS // 8, SENT_ROWS, width), lambda i: (i, 0, 0))],
-        out_specs=pl.BlockSpec((4, 192, width), lambda i: (0, 0, 0)),
+        out_specs=pl.BlockSpec((4, 160, width), lambda i: (0, 0, 0)),
         scratch_shapes=[
             pltpu.VMEM((rows, width), f32),
             pltpu.VMEM((TERM_ROWS, width), f32),
@@ -295,13 +350,11 @@
     )
     near = exchange(run_owner(exchange(sent, "shard"), rows), "grp", NEAR).astype(f32)
     grads = jnp.sum(near[:, 0:128], axis=0).astype(bf16)
-    term = jnp.sum(near[:, 128:160] + near[:, 160:192], axis=0)
-    term = term.reshape(8, 4, width).transpose(1, 0, 2)
-    high = term.astype(bf16)
-    low = (term - high.astype(f32)).astype(bf16)
-    far = jnp.concatenate([jnp.broadcast_to(grads[None], (4, 128, width)), high, low], axis=1)
+    term = jnp.sum(near[:, 128:160], axis=0)
+    term = term.reshape(8, 4, width).transpose(1, 0, 2).astype(bf16)
+    far = jnp.concatenate([jnp.broadcast_to(grads[None], (4, 128, width)), term], axis=1)
     far = exchange(far, "grp", FAR).astype(f32)
-    input_grad = jnp.sum(far[:, 128:136] + far[:, 136:144], axis=0).reshape(-1)
+    input_grad = jnp.sum(far[:, 128:136], axis=0).reshape(-1)
     part = jnp.sum(far[:, 0:128], axis=0).astype(bf16)
     total = spread(part, "grp", NEAR).reshape(rows, width).astype(f32)
     new_table = adagrad_step(row_table, squared_sums, total)

time: 160 us -> 155 us (0.969)
  Pallas kernels: 21.5 us -> 17.7 us
    pallas_call x1, Pallas kernels: 17.8 us -> 14.1 us  [run_main(): pl.pallas_call(main_kernel, out_shape=(jax.ShapeDtypeStruct((SHARDS, SENT...]
    all_to_all x5, blocking collectives: 117 us -> 116 us  [exchange(): lax.all_to_all(value, axis, split_axis=0, concat_axis=0, tiled=True, axis...]
where the time goes in v2:
time: 155 us; the launch traced here: 154 us
  blocking collectives  116 us (75%)
  Pallas kernels  17.7 us (11%)
  starting transfers between devices  7.64 us (5%)
  waiting for transfers between devices  4.84 us (3%)
  other arithmetic  3.13 us (2%)
  local copies, waits for them, and re-layouts  3.01 us (2%)
    all_to_all x5, blocking collectives, exchange(): lax.all_to_all(value, axis, split_axis=0, concat_axis=0, tiled=True, axis...  116 us
    pallas_call x1, Pallas kernels, run_main(): pl.pallas_call(main_kernel, out_shape=(jax.ShapeDtypeStruct((SHARDS, SENT...  14.1 us
    all_to_all x1, starting transfers between devices, exchange(): lax.all_to_all(value, axis, split_axis=0, concat_axis=0, tiled=True, axis...  5.73 us
    all_to_all x1, waiting for transfers between devices, exchange(): lax.all_to_all(value, axis, split_axis=0, concat_axis=0, tiled=True, axis...  4.57 us
    pallas_call x1, Pallas kernels, run_owner(): pl.pallas_call(owner_kernel, grid=(8,), out_shape=jax.ShapeDtypeStruct((4...  3.62 us
  transfers between devices with their start and end apart: 2, of which 2 were waited for; matrix products, arithmetic and copies ran while one was open for 3% of the time, Pallas kernels for 0%

profile of v2, /device:TPU:32, one launch (start us, length us, event | category | flops | bytes accessed | tf_op | source)
XLA Modules:
  0.0 154.4 jit_solution(4485967617550896202)
XLA Ops:
  0.6 1.0 convert_element_type.87
  1.7 12.2 %all_to_all.30 = bf16[4,512,128]{2,1,0:T(8,128)(2,1)S(1)} all-to-all(bf16[4,512,128]{2,1,0:T(8,128)(2,1)S(1)} %broadcast_in_dim.33), channel_id=1, replica_groups={{0,8,16,24},{2,10,18,26},{4,12,20,28},{6,14,22,30},{1,3,5,7},{9,11,13,1..., dimensions={0} | all-to-all | bytes 1048576 | tf_op jit(solution)/shard_map/all_to_all | solution.py:35
  13.9 0.3 broadcast_in_dim.35
  14.2 20.9 %all_to_all.31 = bf16[4,2048,128]{2,1,0:T(8,128)(2,1)S(1)} all-to-all(bf16[4,2048,128]{2,1,0:T(8,128)(2,1)S(1)} %broadcast_in_dim.35), channel_id=1, replica_groups={{0,2,4,6},{8,10,12,14},{16,18,20,22},{24,26,28,30},{1,9,17,25},{3,11,19..., dimensions={0} | all-to-all | bytes 4194304 | tf_op jit(solution)/shard_map/all_to_all | solution.py:35
  35.1 1.9 %collective-permute-start = (bf16[8192,128]{1,0:T(8,128)(2,1)S(1)}, bf16[8192,128]{1,0:T(8,128)(2,1)}, u32[]{:S(2)}, u32[]{:S(2)}) collective-permute-start(bf16[8192,128]{1,0:T(8,128)(2,1)S(1)} %bitcast.43), channel_id=1, source_target_pairs={{0,1},{1,0},{2,3},{3,2},{4,5},{5,4},{6,7},{7,6},{8,9},{9,8},{10,11... | collective-permute-start | bytes 6291464 | tf_op jit(solution)/shard_map/ppermute | solution.py:48
  37.1 0.2 convert_reduce_fusion
  37.3 0.1 select_reduce_fusion
  37.5 0.1 bitcast_compare_fusion
  37.7 0.3 bitcast_reduce_fusion
  38.5 0.1 copy.32
  38.6 0.1 mul.85
  38.9 0.1 mul.88
  39.9 1.0 fusion.3
  41.0 0.3 collective-permute-done.other_hbm
  41.4 14.1 %shard_map.103 = (bf16[32,400,128]{2,1,0:T(8,128)(2,1)S(1)}, f32[2,128]{1,0:T(2,128)}) custom-call(s32[4096]{0:T(1024)S(1)} %reshape.92.index_ref, s32[4096]{0:T(1024)S(1)} %add_add_fusion.place_ref, bf16[8192,128]{1,0:T(8,128)(2,1)S(1)} %bitcast.44, bf16[8192,128]{1,0:T(8,128)(2,1)} %collective-permute-done.other_hbm, ...), custom_call_target="tpu_custom_call" | custom-call | flops 2000000000 | bytes 12000000 | tf_op jit(solution)/shard_map/pallas_call | solution.py:210
  55.4 44.9 %all_to_all.32.got_ref = bf16[32,400,128]{2,1,0:T(8,128)(2,1)S(1)} all-to-all(bf16[32,400,128]{2,1,0:T(8,128)(2,1)S(1)} %get-tuple-element.5), channel_id=1, replica_groups=mesh['grp'=16,'shard'=32] {'shard'}, dimensions={0} | all-to-all | bytes 6553600 | tf_op jit(solution)/shard_map/all_to_all | solution.py:35
  100.3 3.6 %shard_map.104 = bf16[4,160,128]{2,1,0:T(8,128)(2,1)S(1)} custom-call(bf16[32,400,128]{2,1,0:T(8,128)(2,1)S(1)} %all_to_all.32.got_ref), custom_call_target="tpu_custom_call" | custom-call | flops 1100000000 | bytes 3500000 | tf_op jit(solution)/shard_map/pallas_call | solution.py:272
  104.0 11.5 %all_to_all.33 = bf16[4,160,128]{2,1,0:T(8,128)(2,1)S(1)} all-to-all(bf16[4,160,128]{2,1,0:T(8,128)(2,1)S(1)} %shard_map.104), channel_id=1, replica_groups={{0,32,64,96},{128,160,192,224},{256,288,320,352},{384,416,448,480},{1,3..., dimensions={0} | all-to-all | bytes 327680 | tf_op jit(solution)/shard_map/all_to_all | solution.py:35
  115.6 26.3 %all_to_all.34 = bf16[4,136,128]{2,1,0:T(8,128)(2,1)S(1)} all-to-all(bf16[4,136,128]{2,1,0:T(8,128)(2,1)S(1)} %pad_maximum_fusion), channel_id=1, replica_groups={{0,128,256,384},{32,160,288,416},{64,192,320,448},{96,224,352,480},{1,1..., dimensions={0} | all-to-all | bytes 278528 | tf_op jit(solution)/shard_map/all_to_all | solution.py:35
  142.0 0.7 broadcast_in_dim.60
  142.6 5.7 %all-to-all-start.5 = ((bf16[4,128,128]{2,1,0:T(8,128)(2,1)}), bf16[4,128,128]{2,1,0:T(8,128)(2,1)S(1)}, u32[]{:S(2)}, u32[]{:S(2)}) async-start(bf16[4,128,128]{2,1,0:T(8,128)(2,1)} %broadcast_in_dim.60), calls=%async_computation.5 | async-start | bytes 262144 | tf_op jit(solution)/shard_map/all_to_all | solution.py:35
  148.4 0.6 slice_reduce_fusion.3
  149.0 4.6 %all-to-all-done.5 = bf16[4,128,128]{2,1,0:T(8,128)(2,1)S(1)} async-done(((bf16[4,128,128]{2,1,0:T(8,128)(2,1)}), bf16[4,128,128]{2,1,0:T(8,128)(2,1)S(1)}, u32[]{:S(2)}, u32[]{:S(2)}) %all-to-all-start.5) | async-done | bytes 131104 | tf_op jit(solution)/shard_map/all_to_all | solution.py:35
  153.6 0.8 fusion.13
  (52 shorter events, 2.0 us)
Async XLA Ops:
  14.1 23.0 %copy-start.3 = (s32[2,128,16,1]{1,3,2,0:T(1,128)S(1)}, s32[2,128,16,1]{1,3,2,0:T(1,128)}, u32[]{:S(2)}) copy-start(s32[2,128,16,1]{1,3,2,0:T(1,128)} %param.8) | copy-start | bytes 49156
  14.1 24.3 %copy-start.7 = (s32[2,128]{1,0:T(2,128)S(1)}, s32[2,128]{1,0:T(2,128)}, u32[]{:S(2)}) copy-start(s32[2,128]{1,0:T(2,128)} %param.10) | copy-start | bytes 3076
  14.2 24.3 %copy-start.6 = (bf16[1024]{0:T(1024)(128)(2,1)S(1)}, bf16[1024]{0:T(1024)(128)(2,1)}, u32[]{:S(2)}) copy-start(bf16[1024]{0:T(1024)(128)(2,1)} %param.15) | copy-start | bytes 6148
  14.2 24.3 %copy-start.5 = (s32[2,128,16]{1,2,0:T(8,128)S(1)}, s32[2,128,16]{1,2,0:T(8,128)}, u32[]{:S(2)}) copy-start(s32[2,128,16]{1,2,0:T(8,128)} %param.9) | copy-start | bytes 49156
  35.1 6.2 %collective-permute-start = (bf16[8192,128]{1,0:T(8,128)(2,1)S(1)}, bf16[8192,128]{1,0:T(8,128)(2,1)}, u32[]{:S(2)}, u32[]{:S(2)}) collective-permute-start(bf16[8192,128]{1,0:T(8,128)(2,1)S(1)} %bitcast.43), channel_id=1, source_target_pairs={{0,1},{1,0},{2,3},{3,2},{4,5},{5,4},{6,7},{7,6},{8,9},{9,8},{10,11... | collective-permute-start | bytes 6291464 | tf_op jit(solution)/shard_map/ppermute | solution.py:48
  38.5 2.8 %copy-start.1 = (bf16[512,1024]{1,0:T(8,128)(2,1)S(1)}, bf16[512,1024]{1,0:T(8,128)(2,1)}, u32[]{:S(2)}) copy-start(bf16[512,1024]{1,0:T(8,128)(2,1)} %w_input_hbm.1) | copy-start | bytes 3145732
  39.8 1.6 %copy-start = (bf16[1024,1024]{1,0:T(8,128)(2,1)S(1)}, bf16[1024,1024]{1,0:T(8,128)(2,1)}, u32[]{:S(2)}) copy-start(bf16[1024,1024]{1,0:T(8,128)(2,1)} %w_hidden_hbm.1) | copy-start | bytes 6291460
  104.0 49.6 %copy-start.2 = (f32[512,128]{1,0:T(8,128)S(1)}, f32[512,128]{1,0:T(8,128)}, u32[]{:S(2)}) copy-start(f32[512,128]{1,0:T(8,128)} %param.11) | copy-start | bytes 786436
  104.0 49.6 %copy-start.4 = (f32[512,128]{1,0:T(8,128)S(1)}, f32[512,128]{1,0:T(8,128)}, u32[]{:S(2)}) copy-start(f32[512,128]{1,0:T(8,128)} %param.12) | copy-start | bytes 786436
  142.6 10.9 %all-to-all-start.5 = ((bf16[4,128,128]{2,1,0:T(8,128)(2,1)}), bf16[4,128,128]{2,1,0:T(8,128)(2,1)S(1)}, u32[]{:S(2)}, u32[]{:S(2)}) async-start(bf16[4,128,128]{2,1,0:T(8,128)(2,1)} %broadcast_in_dim.60), calls=%async_computation.5 | async-start | bytes 262144 | tf_op jit(solution)/shard_map/all_to_all | solution.py:35

commit v3 on v2

--- a/solution.py
+++ b/solution.py
@@ -60,6 +60,7 @@
 def main_kernel(
     index_ref,
     place_ref,
+    order_ref,
     own_hbm,
     other_hbm,
     label_ref,
@@ -67,6 +68,7 @@
     w_hidden_hbm,
     w_output_ref,
     ids_ref,
+    kept_hbm,
     sent_hbm,
     logit_ref,
     half_ref,
@@ -179,7 +181,7 @@
     def pack(owner, carry):
         at = pl.multiple_of(owner * GRAD_ROWS, GRAD_ROWS)
         sent_ref[owner, 0:GRAD_ROWS, :] = slot_ref[pl.ds(at, GRAD_ROWS), :].astype(bf16)
-        piece = term_ref[pl.ds(pl.multiple_of(owner * 16, 16), 16), :].astype(bf16)
+        piece = term_ref[pl.ds(pl.multiple_of(order_ref[owner] * 16, 16), 16), :].astype(bf16)
         for j in range(8):
             sent_ref[owner, GRAD_ROWS + j * 16 : GRAD_ROWS + (j + 1) * 16, :] = piece[
                 :, j * 128 : (j + 1) * 128
@@ -187,21 +189,23 @@
         sent_ref[owner, GRAD_ROWS + TERM_ROWS : SENT_ROWS, :] = ids_ref[owner]
         return carry
 
-    parts = 4
-    step = SHARDS // parts
+    step = SHARDS // 4
     stores = []
-    for k in range(parts):
+    for k, target in ((2, sent_hbm), (3, sent_hbm), (0, kept_hbm), (1, kept_hbm)):
         lax.fori_loop(k * step, (k + 1) * step, pack, 0, unroll=4)
-        piece = pl.ds(k * step, step)
         stores.append(
-            pltpu.make_async_copy(sent_ref.at[piece], sent_hbm.at[piece], sent_sem.at[k])
+            pltpu.make_async_copy(
+                sent_ref.at[pl.ds(k * step, step)],
+                target.at[pl.ds((k % 2) * step, step)],
+                sent_sem.at[k],
+            )
         )
         stores[-1].start()
     for copy in stores:
         copy.wait()
 
 
-def run_main(index, place, own, other, labels, w_input, w_hidden, w_output, ids):
+def run_main(index, place, order, own, other, labels, w_input, w_hidden, w_output, ids):
     width = own.shape[1]
     samples = index.shape[0] // LOOK
     smem = pl.BlockSpec(memory_space=pltpu.SMEM)
@@ -210,11 +214,12 @@
     return pl.pallas_call(
         main_kernel,
         out_shape=(
-            jax.ShapeDtypeStruct((SHARDS, SENT_ROWS, width), bf16),
+            jax.ShapeDtypeStruct((SHARDS // 2, SENT_ROWS, width), bf16),
+            jax.ShapeDtypeStruct((SHARDS // 2, SENT_ROWS, width), bf16),
             jax.ShapeDtypeStruct((BATCHES, samples // BATCHES), f32),
         ),
-        in_specs=[smem, smem, anywhere, anywhere, vmem, anywhere, anywhere, vmem, vmem],
-        out_specs=(anywhere, vmem),
+        in_specs=[smem, smem, smem, anywhere, anywhere, vmem, anywhere, anywhere, vmem, vmem],
+        out_specs=(anywhere, anywhere, vmem),
         scratch_shapes=[
             pltpu.VMEM((2 * own.shape[0], width), bf16),
             pltpu.VMEM(w_input.shape, bf16),
@@ -233,57 +238,88 @@
         cost_estimate=pl.CostEstimate(
             flops=2_000_000_000, bytes_accessed=12_000_000, transcendentals=256
         ),
-    )(index, place, own, other, labels, w_input, w_hidden, w_output, ids)
-
-
-def owner_kernel(got_ref, out_ref, sum_ref, term_ref):
-    step = pl.program_id(0)
-
-    @pl.when(step == 0)
-    def _():
-        sum_ref[...] = jnp.zeros_like(sum_ref)
-        term_ref[...] = jnp.zeros_like(term_ref)
-
-    names = lax.broadcasted_iota(jnp.int32, (sum_ref.shape[0], CAP), 0).astype(f32) + 1.0
-    total = sum_ref[...]
-    term = term_ref[...]
-    for source in range(got_ref.shape[0]):
-        coded = got_ref[source, GRAD_ROWS + TERM_ROWS : SENT_ROWS, :].astype(f32)
-        picks = []
-        for b in range(BATCHES):
-            named = coded[b : b + 1] * 256.0 + coded[BATCHES + b : BATCHES + b + 1]
-            picks.append(jnp.where(names == named, 1.0, 0.0).astype(bf16))
-        pick = jnp.concatenate(picks, axis=1)
-        total = total + dot(pick, got_ref[source, 0:GRAD_ROWS, :], ((1,), (0,)))
-        term = term + got_ref[source, GRAD_ROWS : GRAD_ROWS + TERM_ROWS, :].astype(f32)
-    sum_ref[...] = total
-    term_ref[...] = term
-
-    @pl.when(step == pl.num_programs(0) - 1)
-    def _():
-        for k in range(4):
-            out_ref[k, 0:128, :] = sum_ref[k * 128 : (k + 1) * 128, :].astype(bf16)
-            part = term_ref[pl.ds(k, 32, stride=4), :]
-            out_ref[k, 128:160, :] = part.astype(bf16)
-
-
-def run_owner(got, rows):
-    width = got.shape[2]
+    )(index, place, order, own, other, labels, w_input, w_hidden, w_output, ids)
+
+
+def owner_kernel(kept_ref, got_ref, out_ref):
+    rows = out_ref.shape[1] - TERM_ROWS
+    names = lax.broadcasted_iota(jnp.int32, (rows, CAP), 0).astype(f32) + 1.0
+    for owner in range(out_ref.shape[0]):
+        total = jnp.zeros((rows, out_ref.shape[2]), f32)
+        term = jnp.zeros((TERM_ROWS, out_ref.shape[2]), f32)
+        for source in (kept_ref, got_ref):
+            coded = source[owner, GRAD_ROWS + TERM_ROWS : SENT_ROWS, :].astype(f32)
+            picks = []
+            for b in range(BATCHES):
+                named = coded[b : b + 1] * 256.0 + coded[BATCHES + b : BATCHES + b + 1]
+                picks.append(jnp.where(names == named, 1.0, 0.0).astype(bf16))
+            pick = jnp.concatenate(picks, axis=1)
+            total = total + dot(pick, source[owner, 0:GRAD_ROWS, :], ((1,), (0,)))
+            term = term + source[owner, GRAD_ROWS : GRAD_ROWS + TERM_ROWS, :].astype(f32)
+        out_ref[owner, 0:rows, :] = total.astype(bf16)
+        out_ref[owner, rows : rows + TERM_ROWS, :] = term.astype(bf16)
+
+
+def run_owner(kept, got, rows):
+    owners, _, width = kept.shape
+    steps = 8
+    block = pl.BlockSpec((owners // steps, SENT_ROWS, width), lambda i: (i, 0, 0))
     return pl.pallas_call(
         owner_kernel,
-        grid=(8,),
-        out_shape=jax.ShapeDtypeStruct((4, 160, width), bf16),
-        in_specs=[pl.BlockSpec((SHARDS // 8, SENT_ROWS, width), lambda i: (i, 0, 0))],
-        out_specs=pl.BlockSpec((4, 160, width), lambda i: (0, 0, 0)),
-        scratch_shapes=[
-            pltpu.VMEM((rows, width), f32),
-            pltpu.VMEM((TERM_ROWS, width), f32),
-        ],
+        grid=(steps,),
+        out_shape=jax.ShapeDtypeStruct((owners, rows + TERM_ROWS, width), bf16),
+        in_specs=[block, block],
+        out_specs=pl.BlockSpec((owners // steps, rows + TERM_ROWS, width), lambda i: (i, 0, 0)),
         compiler_params=pltpu.CompilerParams(vmem_limit_bytes=32 * 1024 * 1024),
         cost_estimate=pl.CostEstimate(
-            flops=1_100_000_000, bytes_accessed=3_500_000, transcendentals=0
+            flops=1_100_000_000, bytes_accessed=6_000_000, transcendentals=0
         ),
+    )(kept, got)
+
+
+def near_kernel(got_ref, out_ref, term_ref):
+    rows = got_ref.shape[1] - TERM_ROWS
+    part = rows // 4
+    for k in range(4):
+        total = got_ref[0, k * part : (k + 1) * part, :].astype(f32)
+        for source in range(1, 4):
+            total = total + got_ref[source, k * part : (k + 1) * part, :].astype(f32)
+        out_ref[k, 0:part, :] = total.astype(bf16)
+    term = got_ref[0, rows : rows + TERM_ROWS, :].astype(f32)
+    for source in range(1, 4):
+        term = term + got_ref[source, rows : rows + TERM_ROWS, :].astype(f32)
+    term_ref[...] = term
+    for k in range(4):
+        out_ref[k, part : part + 32, :] = term_ref[pl.ds(k, 32, stride=4), :].astype(bf16)
+
+
+def run_near(got, rows):
+    width = got.shape[2]
+    vmem = pl.BlockSpec(memory_space=pltpu.VMEM)
+    return pl.pallas_call(
+        near_kernel,
+        out_shape=jax.ShapeDtypeStruct((4, rows // 4 + 32, width), bf16),
+        in_specs=[vmem],
+        out_specs=vmem,
+        scratch_shapes=[pltpu.VMEM((TERM_ROWS, width), f32)],
+        compiler_params=pltpu.CompilerParams(vmem_limit_bytes=32 * 1024 * 1024),
+        cost_estimate=pl.CostEstimate(flops=500_000, bytes_accessed=900_000, transcendentals=0),
     )(got)
+
+
+def owner_order():
+    core = lax.axis_index("shard") & 1
+    group = jnp.arange(SHARDS, dtype=jnp.int32)
+    c = (group >> 4) ^ core
+    slow, fast = (group >> 2) & 3, group & 3
+    x, y = jnp.where(c == 0, slow, fast), jnp.where(c == 0, fast, slow)
+    return x * 8 + y * 2 + c
+
+
+def group_of(owner):
+    core = lax.axis_index("shard") & 1
+    x, y, c = owner >> 3, (owner >> 1) & 3, owner & 1
+    return (c ^ core) * 16 + jnp.where(c == 0, x * 4 + y, y * 4 + x)
 
 
 def plan_slots(owner, row):
@@ -336,10 +372,11 @@
     owner = owner_shard[..., 0]
     own, other = gather_table(row_table.astype(bf16))
     index = table_index(owner, local_row, rows)
-    place, ids = plan_slots(owner, local_row)
-    sent, logits = run_main(
+    place, ids = plan_slots(group_of(owner), local_row)
+    kept, sent, logits = run_main(
         index,
         place,
+        owner_order(),
         own,
         other,
         click_label.astype(f32),
@@ -348,7 +385,11 @@
         w_output.reshape(1, -1),
         ids,
     )
-    near = exchange(run_owner(exchange(sent, "shard"), rows), "grp", NEAR).astype(f32)
+    got = lax.ppermute(sent, "shard", SWAP)
+    dense = run_owner(kept, got, rows).reshape(4, 4 * (rows + TERM_ROWS), width)
+    line = exchange(dense, "shard", FIRST).astype(f32)
+    line = jnp.sum(line, axis=0).astype(bf16).reshape(4, rows + TERM_ROWS, width)
+    near = exchange(run_near(exchange(line, "shard", SECOND), rows), "grp", NEAR).astype(f32)
     grads = jnp.sum(near[:, 0:128], axis=0).astype(bf16)
     term = jnp.sum(near[:, 128:160], axis=0)
     term = term.reshape(8, 4, width).transpose(1, 0, 2).astype(bf16)

time: 155 us -> 149 us (0.961)
  blocking collectives: 116 us -> 104 us
  waiting for transfers between devices: 4.84 us -> 7.68 us
    all_to_all x5 -> x6, blocking collectives: 116 us -> 104 us  [exchange(): lax.all_to_all(value, axis, split_axis=0, concat_axis=0, tiled=True, axis...]
    ppermute x0 -> x1, waiting for transfers between devices: none -> 3.11 us  [local(): got = lax.ppermute(sent, 'shard', SWAP)]
    ppermute x0 -> x1, starting transfers between devices: none -> 2.41 us  [local(): got = lax.ppermute(sent, 'shard', SWAP)]
    all_to_all x1, starting transfers between devices: 5.73 us -> 4.02 us  [exchange(): lax.all_to_all(value, axis, split_axis=0, concat_axis=0, tiled=True, axis...]
    pallas_call x2 -> x3, Pallas kernels: 17.7 us -> 17.8 us  [the longest x1 14.1 us: run_main(): pl.pallas_call(main_kernel, out_shape=(jax.ShapeDtypeStruct((SHARDS // 2,...]
  transfers between devices with their start and end apart: 2 -> 3, of which waited for: 2 -> 2; matrix products, arithmetic and copies ran while one was open for 3% -> 4% of each run, Pallas kernels for 0% -> 0%
where the time goes in v3:
time: 149 us
  blocking collectives  104 us (70%)
  Pallas kernels  17.8 us (12%)
  starting transfers between devices  8.34 us (6%)
  waiting for transfers between devices  7.68 us (5%)
  local copies, waits for them, and re-layouts  4.16 us (3%)
  other arithmetic  3.99 us (3%)
  matrix products  2.16 us (1%)
    all_to_all x6, blocking collectives, exchange(): lax.all_to_all(value, axis, split_axis=0, concat_axis=0, tiled=True, axis...  104 us
    pallas_call x1, Pallas kernels, run_main(): pl.pallas_call(main_kernel, out_shape=(jax.ShapeDtypeStruct((SHARDS // 2,...  14.1 us
    all_to_all x1, waiting for transfers between devices, exchange(): lax.all_to_all(value, axis, split_axis=0, concat_axis=0, tiled=True, axis...  4.57 us
    all_to_all x1, starting transfers between devices, exchange(): lax.all_to_all(value, axis, split_axis=0, concat_axis=0, tiled=True, axis...  4.02 us
    pallas_call x1, Pallas kernels, run_owner(): pl.pallas_call(owner_kernel, grid=(steps,), out_shape=jax.ShapeDtypeStruc...  3.6 us
    ppermute x1, waiting for transfers between devices, local(): got = lax.ppermute(sent, 'shard', SWAP)  3.11 us
  transfers between devices with their start and end apart: 3, of which 2 were waited for; matrix products, arithmetic and copies ran while one was open for 4% of the time, Pallas kernels for 0%

profile of v3, /device:TPU:32, one launch (start us, length us, event | category | flops | bytes accessed | tf_op | source)
XLA Modules:
  0.0 148.9 jit_solution(396400895060721534)
XLA Ops:
  0.6 1.0 convert_element_type.89
  1.7 12.2 %all_to_all.35 = bf16[4,512,128]{2,1,0:T(8,128)(2,1)S(1)} all-to-all(bf16[4,512,128]{2,1,0:T(8,128)(2,1)S(1)} %broadcast_in_dim.33), channel_id=1, replica_groups={{0,8,16,24},{2,10,18,26},{4,12,20,28},{6,14,22,30},{1,3,5,7},{9,11,13,1..., dimensions={0} | all-to-all | bytes 1048576 | tf_op jit(solution)/shard_map/all_to_all | solution.py:35
  13.9 0.3 broadcast_in_dim.35
  14.2 20.9 %all_to_all.36 = bf16[4,2048,128]{2,1,0:T(8,128)(2,1)S(1)} all-to-all(bf16[4,2048,128]{2,1,0:T(8,128)(2,1)S(1)} %broadcast_in_dim.35), channel_id=1, replica_groups={{0,2,4,6},{8,10,12,14},{16,18,20,22},{24,26,28,30},{1,9,17,25},{3,11,19..., dimensions={0} | all-to-all | bytes 4194304 | tf_op jit(solution)/shard_map/all_to_all | solution.py:35
  35.1 1.9 %collective-permute-start = (bf16[8192,128]{1,0:T(8,128)(2,1)S(1)}, bf16[8192,128]{1,0:T(8,128)(2,1)}, u32[]{:S(2)}, u32[]{:S(2)}) collective-permute-start(bf16[8192,128]{1,0:T(8,128)(2,1)S(1)} %bitcast.85), channel_id=1, source_target_pairs={{0,1},{1,0},{2,3},{3,2},{4,5},{5,4},{6,7},{7,6},{8,9},{9,8},{10,11... | collective-permute-start | bytes 6291464 | tf_op jit(solution)/shard_map/ppermute | solution.py:48
  37.1 0.2 convert_reduce_fusion
  37.6 0.1 bitcast_compare_fusion
  37.7 0.3 bitcast_reduce_fusion
  38.1 0.7 convert_element_type.93
  41.1 1.9 %fusion.3 = bf16[2,64,128]{2,1,0:T(8,128)(2,1)S(1)} fusion(s32[2,2048]{1,0:T(2,128)} %convert_element_type.93, bf16[2,2048,32]{1,2,0:T(8,128)(2,1)S(1)} %get-tuple-element.15, bf16[2,2048,32]{1,2,0:T(8,128)(2,1)S(1)} %get-tuple-element.14), kind=kOutput, calls=%fused_computation.5 | convolution fusion | flops 68698112 | bytes 573440 | tf_op jit(solution)/shard_map/bin,bip->bnp/dot_general | solution.py:350
  43.2 14.1 %shard_map.103 = (bf16[16,400,128]{2,1,0:T(8,128)(2,1)S(1)}, bf16[16,400,128]{2,1,0:T(8,128)(2,1)S(1)}, f32[2,128]{1,0:T(2,128)}) custom-call(s32[4096]{0:T(1024)S(1)} %reshape.124.index_ref, s32[4096]{0:T(1024)S(1)} %add_add_fusion.place_ref, s32[32]{0:T(128)S(1)} %fusion.23.order_ref, bf16[8192,128]{1,0:T(8,128)(2,1)S(1)} %bitcast.86, ...), custom_call_target="tpu_custom_call" | custom-call | flops 2000000000 | bytes 12000000 | tf_op jit(solution)/shard_map/pallas_call | solution.py:214
  57.2 2.4 %collective-permute-start.1 = (bf16[16,400,128]{2,1,0:T(8,128)(2,1)S(1)}, bf16[16,400,128]{2,1,0:T(8,128)(2,1)S(1)}, u32[]{:S(2)}, u32[]{:S(2)}) collective-permute-start(bf16[16,400,128]{2,1,0:T(8,128)(2,1)S(1)} %get-tuple-element.7), channel_id=1, source_target_pairs={{0,1},{1,0},{2,3},{3,2},{4,5},{5,4},{6,7},{7,6},{8,9},{9,8},{10,11... | collective-permute-start | bytes 4915208 | tf_op jit(solution)/shard_map/ppermute | solution.py:388
  59.7 3.1 %collective-permute-done.1.got_ref = bf16[16,400,128]{2,1,0:T(8,128)(2,1)S(1)} collective-permute-done((bf16[16,400,128]{2,1,0:T(8,128)(2,1)S(1)}, bf16[16,400,128]{2,1,0:T(8,128)(2,1)S(1)}, u32[]{:S(2)}, u32[]{:S(2)}) %collective-permute-start.1) | collective-permute-done | bytes 1638432 | tf_op jit(solution)/shard_map/ppermute | solution.py:388
  62.8 3.6 %shard_map.104 = bf16[16,640,128]{2,1,0:T(8,128)(2,1)S(1)} custom-call(bf16[16,400,128]{2,1,0:T(8,128)(2,1)S(1)} %get-tuple-element.6.kept_ref, bf16[16,400,128]{2,1,0:T(8,128)(2,1)S(1)} %collective-permute-done.1.got_ref), custom_call_target="tpu_custom_call" | custom-call | flops 1100000000 | bytes 6000000 | tf_op jit(solution)/shard_map/pallas_call | solution.py:267
  66.4 21.8 %all_to_all.37 = bf16[4,2560,128]{2,1,0:T(8,128)(2,1)S(1)} all-to-all(bf16[4,2560,128]{2,1,0:T(8,128)(2,1)S(1)} %bitcast.84), channel_id=1, replica_groups={{0,8,16,24},{2,10,18,26},{4,12,20,28},{6,14,22,30},{1,3,5,7},{9,11,13,1..., dimensions={0} | all-to-all | bytes 5242880 | tf_op jit(solution)/shard_map/all_to_all | solution.py:35
  88.2 0.8 reduce_sum.78
  89.0 11.2 %all_to_all.38.got_ref = bf16[4,640,128]{2,1,0:T(8,128)(2,1)S(1)} all-to-all(bf16[4,640,128]{2,1,0:T(8,128)(2,1)S(1)} %bitcast.87), channel_id=1, replica_groups={{0,2,4,6},{8,10,12,14},{16,18,20,22},{24,26,28,30},{1,9,17,25},{3,11,19..., dimensions={0} | all-to-all | bytes 1310720 | tf_op jit(solution)/shard_map/all_to_all | solution.py:35
  100.3 11.4 %all_to_all.39 = bf16[4,160,128]{2,1,0:T(8,128)(2,1)S(1)} all-to-all(bf16[4,160,128]{2,1,0:T(8,128)(2,1)S(1)} %shard_map.105), channel_id=1, replica_groups={{0,32,64,96},{128,160,192,224},{256,288,320,352},{384,416,448,480},{1,3..., dimensions={0} | all-to-all | bytes 327680 | tf_op jit(solution)/shard_map/all_to_all | solution.py:35
  111.8 26.3 %all_to_all.40 = bf16[4,136,128]{2,1,0:T(8,128)(2,1)S(1)} all-to-all(bf16[4,136,128]{2,1,0:T(8,128)(2,1)S(1)} %pad_maximum_fusion), channel_id=1, replica_groups={{0,128,256,384},{32,160,288,416},{64,192,320,448},{96,224,352,480},{1,1..., dimensions={0} | all-to-all | bytes 278528 | tf_op jit(solution)/shard_map/all_to_all | solution.py:35
  138.2 0.7 broadcast_in_dim.37
  138.8 4.0 %all-to-all-start.6 = ((bf16[4,128,128]{2,1,0:T(8,128)(2,1)}), bf16[4,128,128]{2,1,0:T(8,128)(2,1)S(1)}, u32[]{:S(2)}, u32[]{:S(2)}) async-start(bf16[4,128,128]{2,1,0:T(8,128)(2,1)} %broadcast_in_dim.37), calls=%async_computation.6 | async-start | bytes 262144 | tf_op jit(solution)/shard_map/all_to_all | solution.py:35
  142.9 0.6 slice_reduce_fusion.3
  143.4 4.6 %all-to-all-done.6 = bf16[4,128,128]{2,1,0:T(8,128)(2,1)S(1)} async-done(((bf16[4,128,128]{2,1,0:T(8,128)(2,1)}), bf16[4,128,128]{2,1,0:T(8,128)(2,1)S(1)}, u32[]{:S(2)}, u32[]{:S(2)}) %all-to-all-start.6) | async-done | bytes 131104 | tf_op jit(solution)/shard_map/all_to_all | solution.py:35
  148.1 0.8 fusion.13
  (64 shorter events, 3.0 us)
Async XLA Ops:
  14.1 23.0 %copy-start.4 = (s32[2,128,16,1]{1,3,2,0:T(1,128)S(1)}, s32[2,128,16,1]{1,3,2,0:T(1,128)}, u32[]{:S(2)}) copy-start(s32[2,128,16,1]{1,3,2,0:T(1,128)} %param.8) | copy-start | bytes 49156
  14.1 24.9 %copy-start.7 = (s32[2,128]{1,0:T(2,128)S(1)}, s32[2,128]{1,0:T(2,128)}, u32[]{:S(2)}) copy-start(s32[2,128]{1,0:T(2,128)} %param.10) | copy-start | bytes 3076
  14.2 24.9 %copy-start.6 = (bf16[1024]{0:T(1024)(128)(2,1)S(1)}, bf16[1024]{0:T(1024)(128)(2,1)}, u32[]{:S(2)}) copy-start(bf16[1024]{0:T(1024)(128)(2,1)} %param.15) | copy-start | bytes 6148
  14.2 25.3 %copy-start.5 = (s32[2,128,16]{1,2,0:T(8,128)S(1)}, s32[2,128,16]{1,2,0:T(8,128)}, u32[]{:S(2)}) copy-start(s32[2,128,16]{1,2,0:T(8,128)} %param.9) | copy-start | bytes 49156
  35.1 8.1 %collective-permute-start = (bf16[8192,128]{1,0:T(8,128)(2,1)S(1)}, bf16[8192,128]{1,0:T(8,128)(2,1)}, u32[]{:S(2)}, u32[]{:S(2)}) collective-permute-start(bf16[8192,128]{1,0:T(8,128)(2,1)S(1)} %bitcast.85), channel_id=1, source_target_pairs={{0,1},{1,0},{2,3},{3,2},{4,5},{5,4},{6,7},{7,6},{8,9},{9,8},{10,11... | collective-permute-start | bytes 6291464 | tf_op jit(solution)/shard_map/ppermute | solution.py:48
  40.1 3.1 %copy-start.1 = (bf16[512,1024]{1,0:T(8,128)(2,1)S(1)}, bf16[512,1024]{1,0:T(8,128)(2,1)}, u32[]{:S(2)}) copy-start(bf16[512,1024]{1,0:T(8,128)(2,1)} %w_input_hbm.1) | copy-start | bytes 3145732
  41.0 2.1 %copy-start = (bf16[1024,1024]{1,0:T(8,128)(2,1)S(1)}, bf16[1024,1024]{1,0:T(8,128)(2,1)}, u32[]{:S(2)}) copy-start(bf16[1024,1024]{1,0:T(8,128)(2,1)} %w_hidden_hbm.1) | copy-start | bytes 6291460
  57.2 5.5 %collective-permute-start.1 = (bf16[16,400,128]{2,1,0:T(8,128)(2,1)S(1)}, bf16[16,400,128]{2,1,0:T(8,128)(2,1)S(1)}, u32[]{:S(2)}, u32[]{:S(2)}) collective-permute-start(bf16[16,400,128]{2,1,0:T(8,128)(2,1)S(1)} %get-tuple-element.7), channel_id=1, source_target_pairs={{0,1},{1,0},{2,3},{3,2},{4,5},{5,4},{6,7},{7,6},{8,9},{9,8},{10,11... | collective-permute-start | bytes 4915208 | tf_op jit(solution)/shard_map/ppermute | solution.py:388
  100.2 47.8 %copy-start.2 = (f32[512,128]{1,0:T(8,128)S(1)}, f32[512,128]{1,0:T(8,128)}, u32[]{:S(2)}) copy-start(f32[512,128]{1,0:T(8,128)} %param.11) | copy-start | bytes 786436
  100.2 47.8 %copy-start.3 = (f32[512,128]{1,0:T(8,128)S(1)}, f32[512,128]{1,0:T(8,128)}, u32[]{:S(2)}) copy-start(f32[512,128]{1,0:T(8,128)} %param.12) | copy-start | bytes 786436
  138.8 9.2 %all-to-all-start.6 = ((bf16[4,128,128]{2,1,0:T(8,128)(2,1)}), bf16[4,128,128]{2,1,0:T(8,128)(2,1)S(1)}, u32[]{:S(2)}, u32[]{:S(2)}) async-start(bf16[4,128,128]{2,1,0:T(8,128)(2,1)} %broadcast_in_dim.37), calls=%async_computation.6 | async-start | bytes 262144 | tf_op jit(solution)/shard_map/all_to_all | solution.py:35

commit v4 on v3

--- a/solution.py
+++ b/solution.py
@@ -39,14 +39,6 @@
 
 def spread(value, axis, groups):
     return exchange(jnp.broadcast_to(value[None], (4,) + value.shape), axis, groups)
-
-
-def gather_table(table_low):
-    rows, width = table_low.shape
-    line = spread(table_low, "shard", FIRST).reshape(4 * rows, width)
-    own = spread(line, "shard", SECOND).reshape(16 * rows, width)
-    other = lax.ppermute(own, "shard", SWAP)
-    return own, other
 
 
 def dot(a, b, dims):
@@ -78,6 +70,8 @@
     pooled_ref,
     slot_ref,
     turn_ref,
+    turned_ref,
+    back_ref,
     term_ref,
     sent_ref,
     half_sem,
@@ -100,12 +94,6 @@
     for copy in tables + weights:
         copy.start()
 
-    def clear(step, carry):
-        slot_ref[pl.ds(pl.multiple_of(step * 256, 256), 256), :] = jnp.zeros((256, 128), f32)
-        return carry
-
-    lax.fori_loop(0, slot_ref.shape[0] // 256, clear, 0)
-
     def widen(step, carry):
         at = pl.multiple_of(step * 256, 256)
         table_ref[pl.ds(at, 256), :] = half_ref[pl.ds(at, 256), :].astype(f32)
@@ -115,23 +103,26 @@
         tables[k].wait()
         lax.fori_loop(k * chunk // 256, (k + 1) * chunk // 256, widen, 0)
 
-    def look(sample, carry):
-        for slot in range(SLOTS):
-            first = sample * LOOK + slot * HOT
-            total = table_ref[pl.ds(index_ref[first], 1), :]
-            for hot in range(1, HOT):
-                total = total + table_ref[pl.ds(index_ref[first + hot], 1), :]
-            pooled_ref[pl.ds(slot * samples + sample, 1), :] = total
+    def look(step, carry):
+        slot_ref[pl.ds(pl.multiple_of(step * 512, 512), 512), :] = jnp.zeros((512, 128), f32)
+        for turn in range(16):
+            sample = step * 16 + turn
+            for slot in range(SLOTS):
+                first = sample * LOOK + slot * HOT
+                total = table_ref[pl.ds(index_ref[first], 1), :]
+                for hot in range(1, HOT):
+                    total = total + table_ref[pl.ds(index_ref[first + hot], 1), :]
+                pooled_ref[pl.ds(slot * samples + sample, 1), :] = total
         return carry
 
-    lax.fori_loop(0, samples, look, 0, unroll=16)
+    lax.fori_loop(0, samples // 16, look, 0)
 
     features = SLOTS * 128
     for slot in range(SLOTS):
         for b in range(BATCHES):
             block = pooled_ref[slot * samples + b * 128 : slot * samples + (b + 1) * 128, :]
             turn_ref[b * features + slot * 128 : b * features + (slot + 1) * 128, :] = jnp.transpose(block)
-    turned = jnp.concatenate(
+    turned_ref[...] = jnp.concatenate(
         [
             jnp.concatenate(
                 [turn_ref[pl.ds(b * features + s, 16, stride=SHARDS), :] for s in range(SHARDS)],
@@ -166,26 +157,30 @@
     back_in = dot(back_one, w_input, ((1,), (1,))).astype(bf16).astype(f32)
     for slot in range(SLOTS):
         pooled_ref[slot * samples : (slot + 1) * samples, :] = back_in[:, slot * 128 : (slot + 1) * 128]
-    term_ref[...] = dot(turned, back_one, ((1,), (0,)))
-
-    def scatter(sample, carry):
-        for slot in range(SLOTS):
-            first = sample * LOOK + slot * HOT
-            row = pooled_ref[pl.ds(slot * samples + sample, 1), :]
-            for hot in range(HOT):
-                slot_ref[pl.ds(place_ref[first + hot], 1), :] = row
+    for j in range(8):
+        back_ref[j] = back_one[:, j * 128 : (j + 1) * 128]
+
+    def scatter(step, carry):
+        term_ref[step] = dot(turned_ref[...], back_ref[step], ((1,), (0,)))
+        for turn in range(32):
+            sample = step * 32 + turn
+            for slot in range(SLOTS):
+                first = sample * LOOK + slot * HOT
+                row = pooled_ref[pl.ds(slot * samples + sample, 1), :]
+                for hot in range(HOT):
+                    slot_ref[pl.ds(place_ref[first + hot], 1), :] = row
         return carry
 
-    lax.fori_loop(0, samples, scatter, 0, unroll=16)
+    lax.fori_loop(0, samples // 32, scatter, 0)
 
     def pack(owner, carry):
         at = pl.multiple_of(owner * GRAD_ROWS, GRAD_ROWS)
         sent_ref[owner, 0:GRAD_ROWS, :] = slot_ref[pl.ds(at, GRAD_ROWS), :].astype(bf16)
-        piece = term_ref[pl.ds(pl.multiple_of(order_ref[owner] * 16, 16), 16), :].astype(bf16)
+        piece = pl.ds(pl.multiple_of(order_ref[owner] * 16, 16), 16)
         for j in range(8):
-            sent_ref[owner, GRAD_ROWS + j * 16 : GRAD_ROWS + (j + 1) * 16, :] = piece[
-                :, j * 128 : (j + 1) * 128
-            ]
+            sent_ref[owner, GRAD_ROWS + j * 16 : GRAD_ROWS + (j + 1) * 16, :] = term_ref[
+                j, piece, :
+            ].astype(bf16)
         sent_ref[owner, GRAD_ROWS + TERM_ROWS : SENT_ROWS, :] = ids_ref[owner]
         return carry
 
@@ -211,6 +206,7 @@
     smem = pl.BlockSpec(memory_space=pltpu.SMEM)
     vmem = pl.BlockSpec(memory_space=pltpu.VMEM)
     anywhere = pl.BlockSpec(memory_space=pl.ANY)
+    hbm = pl.BlockSpec(memory_space=pltpu.HBM)
     return pl.pallas_call(
         main_kernel,
         out_shape=(
@@ -218,7 +214,7 @@
             jax.ShapeDtypeStruct((SHARDS // 2, SENT_ROWS, width), bf16),
             jax.ShapeDtypeStruct((BATCHES, samples // BATCHES), f32),
         ),
-        in_specs=[smem, smem, smem, anywhere, anywhere, vmem, anywhere, anywhere, vmem, vmem],
+        in_specs=[smem, smem, smem, anywhere, anywhere, vmem, hbm, hbm, vmem, vmem],
         out_specs=(anywhere, anywhere, vmem),
         scratch_shapes=[
             pltpu.VMEM((2 * own.shape[0], width), bf16),
@@ -228,7 +224,9 @@
             pltpu.VMEM((samples * SLOTS, width), f32),
             pltpu.VMEM((SHARDS * GRAD_ROWS, width), f32),
             pltpu.VMEM((BATCHES * SLOTS * width, samples // BATCHES), f32),
-            pltpu.VMEM(w_input.shape, f32),
+            pltpu.VMEM((SLOTS * width, samples), bf16),
+            pltpu.VMEM((8, samples, width), bf16),
+            pltpu.VMEM((8, SLOTS * width, width), f32),
             pltpu.VMEM((SHARDS, SENT_ROWS, width), bf16),
             pltpu.SemaphoreType.DMA((4,)),
             pltpu.SemaphoreType.DMA((2,)),
@@ -241,40 +239,57 @@
     )(index, place, order, own, other, labels, w_input, w_hidden, w_output, ids)
 
 
-def owner_kernel(kept_ref, got_ref, out_ref):
+def add_source(source, owner, total, term):
+    names = lax.broadcasted_iota(jnp.int32, (total.shape[0], CAP), 0).astype(f32) + 1.0
+    coded = source[owner, GRAD_ROWS + TERM_ROWS : SENT_ROWS, :].astype(f32)
+    picks = []
+    for b in range(BATCHES):
+        named = coded[b : b + 1] * 256.0 + coded[BATCHES + b : BATCHES + b + 1]
+        picks.append(jnp.where(names == named, 1.0, 0.0).astype(bf16))
+    pick = jnp.concatenate(picks, axis=1)
+    total = total + dot(pick, source[owner, 0:GRAD_ROWS, :], ((1,), (0,)))
+    return total, term + source[owner, GRAD_ROWS : GRAD_ROWS + TERM_ROWS, :].astype(f32)
+
+
+def kept_kernel(kept_ref, out_ref):
     rows = out_ref.shape[1] - TERM_ROWS
-    names = lax.broadcasted_iota(jnp.int32, (rows, CAP), 0).astype(f32) + 1.0
+    width = out_ref.shape[2]
     for owner in range(out_ref.shape[0]):
-        total = jnp.zeros((rows, out_ref.shape[2]), f32)
-        term = jnp.zeros((TERM_ROWS, out_ref.shape[2]), f32)
-        for source in (kept_ref, got_ref):
-            coded = source[owner, GRAD_ROWS + TERM_ROWS : SENT_ROWS, :].astype(f32)
-            picks = []
-            for b in range(BATCHES):
-                named = coded[b : b + 1] * 256.0 + coded[BATCHES + b : BATCHES + b + 1]
-                picks.append(jnp.where(names == named, 1.0, 0.0).astype(bf16))
-            pick = jnp.concatenate(picks, axis=1)
-            total = total + dot(pick, source[owner, 0:GRAD_ROWS, :], ((1,), (0,)))
-            term = term + source[owner, GRAD_ROWS : GRAD_ROWS + TERM_ROWS, :].astype(f32)
+        total = jnp.zeros((rows, width), f32)
+        term = jnp.zeros((TERM_ROWS, width), f32)
+        total, term = add_source(kept_ref, owner, total, term)
         out_ref[owner, 0:rows, :] = total.astype(bf16)
         out_ref[owner, rows : rows + TERM_ROWS, :] = term.astype(bf16)
 
 
-def run_owner(kept, got, rows):
-    owners, _, width = kept.shape
+def got_kernel(base_ref, got_ref, out_ref):
+    rows = out_ref.shape[1] - TERM_ROWS
+    for owner in range(out_ref.shape[0]):
+        total = base_ref[owner, 0:rows, :].astype(f32)
+        term = base_ref[owner, rows : rows + TERM_ROWS, :].astype(f32)
+        total, term = add_source(got_ref, owner, total, term)
+        out_ref[owner, 0:rows, :] = total.astype(bf16)
+        out_ref[owner, rows : rows + TERM_ROWS, :] = term.astype(bf16)
+
+
+def run_owner(kernel, rows, *operands):
+    owners, _, width = operands[0].shape
     steps = 8
-    block = pl.BlockSpec((owners // steps, SENT_ROWS, width), lambda i: (i, 0, 0))
+    blocks = [
+        pl.BlockSpec((owners // steps, each.shape[1], width), lambda i: (i, 0, 0))
+        for each in operands
+    ]
     return pl.pallas_call(
-        owner_kernel,
+        kernel,
         grid=(steps,),
         out_shape=jax.ShapeDtypeStruct((owners, rows + TERM_ROWS, width), bf16),
-        in_specs=[block, block],
+        in_specs=blocks,
         out_specs=pl.BlockSpec((owners // steps, rows + TERM_ROWS, width), lambda i: (i, 0, 0)),
         compiler_params=pltpu.CompilerParams(vmem_limit_bytes=32 * 1024 * 1024),
         cost_estimate=pl.CostEstimate(
-            flops=1_100_000_000, bytes_accessed=6_000_000, transcendentals=0
+            flops=550_000_000, bytes_accessed=5_000_000, transcendentals=0
         ),
-    )(kept, got)
+    )(*operands)
 
 
 def near_kernel(got_ref, out_ref, term_ref):
@@ -307,8 +322,7 @@
     )(got)
 
 
-def owner_order():
-    core = lax.axis_index("shard") & 1
+def owner_order(core):
     group = jnp.arange(SHARDS, dtype=jnp.int32)
     c = (group >> 4) ^ core
     slow, fast = (group >> 2) & 3, group & 3
@@ -316,29 +330,34 @@
     return x * 8 + y * 2 + c
 
 
-def group_of(owner):
-    core = lax.axis_index("shard") & 1
+def group_of(owner, core):
     x, y, c = owner >> 3, (owner >> 1) & 3, owner & 1
     return (c ^ core) * 16 + jnp.where(c == 0, x * 4 + y, y * 4 + x)
 
 
-def plan_slots(owner, row):
+def plan_slots(owner, row, after):
     batches, samples, looks = owner.shape
-    names = jnp.arange(SHARDS, dtype=jnp.int32)
+    names, steps, turn, batch, spots, after = lax.optimization_barrier(
+        (
+            jnp.arange(SHARDS, dtype=jnp.int32),
+            jnp.arange(samples),
+            jnp.arange(looks),
+            jnp.arange(batches, dtype=jnp.int32),
+            jnp.arange(CAP, dtype=jnp.int32),
+            after,
+        )
+    )
     hit = (owner[..., None] == names).astype(bf16).reshape(batches, samples, looks * SHARDS)
-    steps = jnp.arange(samples)
     before = (steps[None, :] < steps[:, None]).astype(bf16)
     rank = jnp.einsum("ts,bsn->btn", before, hit, preferred_element_type=f32)
     counts = jnp.sum(hit.astype(f32), axis=1).reshape(batches, looks, SHARDS)
-    turn = jnp.arange(looks)
     base = jnp.sum(
         jnp.where((turn[None, :] < turn[:, None])[None, :, :, None], counts[:, None], 0.0), axis=2
     ).reshape(batches, 1, looks * SHARDS)
     spot = jnp.sum(
         (hit.astype(f32) * (rank + base)).reshape(batches, samples, looks, SHARDS), axis=3
     ).astype(jnp.int32)
-    batch = jnp.arange(batches, dtype=jnp.int32)[:, None, None]
-    place = owner * GRAD_ROWS + batch * CAP + spot
+    place = owner * GRAD_ROWS + batch[:, None, None] * CAP + spot
     code = row + 1
     high = (code >> 8).astype(bf16)
     low = (code & 255).astype(bf16)
@@ -346,15 +365,14 @@
     coded = jnp.concatenate(
         [flat_hit * high.reshape(batches, -1, 1), flat_hit * low.reshape(batches, -1, 1)], axis=2
     )
-    where = (spot.reshape(batches, -1, 1) == jnp.arange(CAP, dtype=jnp.int32)).astype(bf16)
+    where = (spot.reshape(batches, -1, 1) == spots).astype(bf16)
     ids = jnp.einsum("bin,bip->bnp", coded, where, preferred_element_type=f32).astype(bf16)
     ids = ids.reshape(batches, 2, SHARDS, CAP).transpose(2, 1, 0, 3).reshape(SHARDS, 2 * batches, CAP)
     ids = jnp.pad(ids, ((0, 0), (0, ID_ROWS - 2 * batches), (0, 0)))
     return place.reshape(-1), ids
 
 
-def table_index(owner, row, rows):
-    core = lax.axis_index("shard") & 1
+def table_index(owner, row, rows, core):
     x, y, c = owner >> 3, (owner >> 1) & 3, owner & 1
     chip = jnp.where(c == 0, y * 4 + x, x * 4 + y)
     return (((c ^ core) * 16 + chip) * rows + row).reshape(-1)
@@ -370,23 +388,33 @@
 ):
     rows, width = row_table.shape
     owner = owner_shard[..., 0]
-    own, other = gather_table(row_table.astype(bf16))
-    index = table_index(owner, local_row, rows)
-    place, ids = plan_slots(group_of(owner), local_row)
+    core = lax.axis_index("shard") & 1
+    table_low, core = lax.optimization_barrier((row_table.astype(bf16), core))
+    line = spread(table_low, "shard", FIRST).reshape(4 * rows, width)
+    own = spread(line, "shard", SECOND).reshape(16 * rows, width)
+    own, owner, local_row, click_label, core = lax.optimization_barrier(
+        (own, owner, local_row, click_label, core)
+    )
+    other = lax.ppermute(own, "shard", SWAP)
+    index = table_index(owner, local_row, rows, core)
+    order = owner_order(core)
+    place, ids = plan_slots(group_of(owner, core), local_row, own)
+    labels = click_label.astype(f32)
     kept, sent, logits = run_main(
         index,
         place,
-        owner_order(),
+        order,
         own,
         other,
-        click_label.astype(f32),
+        labels,
         w_input,
         w_hidden,
         w_output.reshape(1, -1),
         ids,
     )
     got = lax.ppermute(sent, "shard", SWAP)
-    dense = run_owner(kept, got, rows).reshape(4, 4 * (rows + TERM_ROWS), width)
+    dense = run_owner(got_kernel, rows, run_owner(kept_kernel, rows, kept), got)
+    dense = dense.reshape(4, 4 * (rows + TERM_ROWS), width)
     line = exchange(dense, "shard", FIRST).astype(f32)
     line = jnp.sum(line, axis=0).astype(bf16).reshape(4, rows + TERM_ROWS, width)
     near = exchange(run_near(exchange(line, "shard", SECOND), rows), "grp", NEAR).astype(f32)
@@ -397,6 +425,7 @@
     far = exchange(far, "grp", FAR).astype(f32)
     input_grad = jnp.sum(far[:, 128:136], axis=0).reshape(-1)
     part = jnp.sum(far[:, 0:128], axis=0).astype(bf16)
+    part, input_grad = lax.optimization_barrier((part, input_grad))
     total = spread(part, "grp", NEAR).reshape(rows, width).astype(f32)
     new_table = adagrad_step(row_table, squared_sums, total)
     return (new_table, logits, input_grad)

time: 149 us -> 146 us (0.980)
  blocking collectives: 104 us -> 113 us
  waiting for transfers between devices: 7.68 us -> 0.81 us
  starting transfers between devices: 8.34 us -> 4.31 us
  local copies, waits for them, and re-layouts: 4.16 us -> 2.09 us
    all_to_all x6 -> x7, blocking collectives: 104 us -> 113 us  [exchange(): lax.all_to_all(value, axis, split_axis=0, concat_axis=0, tiled=True, axis...]
    all_to_all x1 -> x0, waiting for transfers between devices: 4.57 us -> none  [exchange(): lax.all_to_all(value, axis, split_axis=0, concat_axis=0, tiled=True, axis...]
    all_to_all x1 -> x0, starting transfers between devices: 4.02 us -> none  [exchange(): lax.all_to_all(value, axis, split_axis=0, concat_axis=0, tiled=True, axis...]
    ppermute x1, waiting for transfers between devices: 3.11 us -> 0.6 us  [local(): got = lax.ppermute(sent, 'shard', SWAP)]
    pallas_call x1 -> x2, Pallas kernels: 3.6 us -> 5.01 us  [run_owner(): pl.pallas_call(kernel, grid=(steps,), out_shape=jax.ShapeDtypeStruct((own...]
  transfers between devices with their start and end apart: 3 -> 2, of which waited for: 2 -> 2; matrix products, arithmetic and copies ran while one was open for 4% -> 3% of each run, Pallas kernels for 0% -> 2%
where the time goes in v4:
time: 146 us
  blocking collectives  113 us (77%)
  Pallas kernels  19.2 us (13%)
  starting transfers between devices  4.31 us (3%)
  other arithmetic  4.22 us (3%)
  local copies, waits for them, and re-layouts  2.09 us (1%)
    all_to_all x7, blocking collectives, exchange(): lax.all_to_all(value, axis, split_axis=0, concat_axis=0, tiled=True, axis...  113 us
    pallas_call x1, Pallas kernels, run_main(): pl.pallas_call(main_kernel, out_shape=(jax.ShapeDtypeStruct((SHARDS // 2,...  14.1 us
    pallas_call x2, Pallas kernels, run_owner(): pl.pallas_call(kernel, grid=(steps,), out_shape=jax.ShapeDtypeStruct((own...  5.01 us
  transfers between devices with their start and end apart: 2, of which 2 were waited for; matrix products, arithmetic and copies ran while one was open for 3% of the time, Pallas kernels for 2%

profile of v4, /device:TPU:32, one launch (start us, length us, event | category | flops | bytes accessed | tf_op | source)
XLA Modules:
  0.0 145.7 jit_solution(9504752317424758066)
XLA Ops:
  0.6 1.0 convert_element_type.75
  1.7 12.2 %all_to_all.35 = bf16[4,512,128]{2,1,0:T(8,128)(2,1)S(1)} all-to-all(bf16[4,512,128]{2,1,0:T(8,128)(2,1)S(1)} %broadcast_in_dim.30), channel_id=1, replica_groups={{0,8,16,24},{2,10,18,26},{4,12,20,28},{6,14,22,30},{1,3,5,7},{9,11,13,1..., dimensions={0} | all-to-all | bytes 1048576 | tf_op jit(solution)/shard_map/all_to_all | solution.py:35
  13.9 0.3 broadcast_in_dim.32
  14.2 20.9 %all_to_all.36 = bf16[4,2048,128]{2,1,0:T(8,128)(2,1)S(1)} all-to-all(bf16[4,2048,128]{2,1,0:T(8,128)(2,1)S(1)} %broadcast_in_dim.32), channel_id=1, replica_groups={{0,2,4,6},{8,10,12,14},{16,18,20,22},{24,26,28,30},{1,9,17,25},{3,11,19..., dimensions={0} | all-to-all | bytes 4194304 | tf_op jit(solution)/shard_map/all_to_all | solution.py:35
  35.1 1.9 %collective-permute-start = (bf16[8192,128]{1,0:T(8,128)(2,1)S(1)}, bf16[8192,128]{1,0:T(8,128)(2,1)}, u32[]{:S(2)}, u32[]{:S(2)}) collective-permute-start(bf16[8192,128]{1,0:T(8,128)(2,1)S(1)} %bitcast.38), channel_id=1, source_target_pairs={{0,1},{1,0},{2,3},{3,2},{4,5},{5,4},{6,7},{7,6},{8,9},{9,8},{10,11... | collective-permute-start | bytes 6291464 | tf_op jit(solution)/shard_map/ppermute | solution.py:398
  37.3 0.3 convert_reduce_fusion
  38.4 0.1 bitcast_compare_fusion
  38.6 0.3 bitcast_reduce_fusion
  39.8 0.1 compare_select_fusion.1
  39.9 1.0 fusion.4
  41.0 0.2 collective-permute-done.other_hbm
  41.4 14.1 %shard_map.103 = (bf16[16,400,128]{2,1,0:T(8,128)(2,1)S(1)}, bf16[16,400,128]{2,1,0:T(8,128)(2,1)S(1)}, f32[2,128]{1,0:T(2,128)}) custom-call(s32[4096]{0:T(1024)S(1)} %reshape.110.index_ref, s32[4096]{0:T(1024)S(1)} %reshape.112.place_ref, s32[32]{0:T(128)S(1)} %fusion.21.order_ref, bf16[8192,128]{1,0:T(8,128)(2,1)S(1)} %bitcast.39, ...), custom_call_target="tpu_custom_call" | custom-call | flops 2000000000 | bytes 12000000 | tf_op jit(solution)/shard_map/pallas_call | solution.py:210
  55.4 2.4 %collective-permute-start.1 = (bf16[16,400,128]{2,1,0:T(8,128)(2,1)S(1)}, bf16[16,400,128]{2,1,0:T(8,128)(2,1)S(1)}, u32[]{:S(2)}, u32[]{:S(2)}) collective-permute-start(bf16[16,400,128]{2,1,0:T(8,128)(2,1)S(1)} %get-tuple-element.33), channel_id=1, source_target_pairs={{0,1},{1,0},{2,3},{3,2},{4,5},{5,4},{6,7},{7,6},{8,9},{9,8},{10,11... | collective-permute-start | bytes 4915208 | tf_op jit(solution)/shard_map/ppermute | solution.py:415
  57.9 2.5 %shard_map.104.base_ref = bf16[16,640,128]{2,1,0:T(8,128)(2,1)S(1)} custom-call(bf16[16,400,128]{2,1,0:T(8,128)(2,1)S(1)} %get-tuple-element.32.kept_ref), custom_call_target="tpu_custom_call" | custom-call | flops 550000000 | bytes 5000000 | tf_op jit(solution)/shard_map/pallas_call | solution.py:282
  60.4 0.6 collective-permute-done.1.got_ref
  61.0 2.5 %shard_map.105 = bf16[16,640,128]{2,1,0:T(8,128)(2,1)S(1)} custom-call(bf16[16,640,128]{2,1,0:T(8,128)(2,1)S(1)} %shard_map.104.base_ref, bf16[16,400,128]{2,1,0:T(8,128)(2,1)S(1)} %collective-permute-done.1.got_ref), custom_call_target="tpu_custom_call" | custom-call | flops 550000000 | bytes 5000000 | tf_op jit(solution)/shard_map/pallas_call | solution.py:282
  63.5 21.8 %all_to_all.37 = bf16[4,2560,128]{2,1,0:T(8,128)(2,1)S(1)} all-to-all(bf16[4,2560,128]{2,1,0:T(8,128)(2,1)S(1)} %bitcast.37), channel_id=1, replica_groups={{0,8,16,24},{2,10,18,26},{4,12,20,28},{6,14,22,30},{1,3,5,7},{9,11,13,1..., dimensions={0} | all-to-all | bytes 5242880 | tf_op jit(solution)/shard_map/all_to_all | solution.py:35
  85.3 0.8 reduce_sum.78
  86.1 11.2 %all_to_all.38.got_ref = bf16[4,640,128]{2,1,0:T(8,128)(2,1)S(1)} all-to-all(bf16[4,640,128]{2,1,0:T(8,128)(2,1)S(1)} %bitcast.40), channel_id=1, replica_groups={{0,2,4,6},{8,10,12,14},{16,18,20,22},{24,26,28,30},{1,9,17,25},{3,11,19..., dimensions={0} | all-to-all | bytes 1310720 | tf_op jit(solution)/shard_map/all_to_all | solution.py:35
  97.4 11.4 %all_to_all.39 = bf16[4,160,128]{2,1,0:T(8,128)(2,1)S(1)} all-to-all(bf16[4,160,128]{2,1,0:T(8,128)(2,1)S(1)} %shard_map.106), channel_id=1, replica_groups={{0,32,64,96},{128,160,192,224},{256,288,320,352},{384,416,448,480},{1,3..., dimensions={0} | all-to-all | bytes 327680 | tf_op jit(solution)/shard_map/all_to_all | solution.py:35
  108.9 26.3 %all_to_all.40 = bf16[4,136,128]{2,1,0:T(8,128)(2,1)S(1)} all-to-all(bf16[4,136,128]{2,1,0:T(8,128)(2,1)S(1)} %pad_maximum_fusion), channel_id=1, replica_groups={{0,128,256,384},{32,160,288,416},{64,192,320,448},{96,224,352,480},{1,1..., dimensions={0} | all-to-all | bytes 278528 | tf_op jit(solution)/shard_map/all_to_all | solution.py:35
  135.2 0.6 slice_reduce_fusion.3
  135.9 9.0 %all_to_all.41 = bf16[4,128,128]{2,1,0:T(8,128)(2,1)S(1)} all-to-all(bf16[4,128,128]{2,1,0:T(8,128)(2,1)S(1)} %broadcast_in_dim.37), channel_id=1, replica_groups={{0,32,64,96},{128,160,192,224},{256,288,320,352},{384,416,448,480},{1,3..., dimensions={0} | all-to-all | bytes 262144 | tf_op jit(solution)/shard_map/all_to_all | solution.py:35
  144.9 0.8 fusion.14
  (58 shorter events, 2.4 us)
Async XLA Ops:
  14.1 22.9 %copy-start.6 = (bf16[1024]{0:T(1024)(128)(2,1)S(1)}, bf16[1024]{0:T(1024)(128)(2,1)}, u32[]{:S(2)}) copy-start(bf16[1024]{0:T(1024)(128)(2,1)} %param.15) | copy-start | bytes 6148
  14.1 22.9 %copy-start.7 = (s32[2,128]{1,0:T(2,128)S(1)}, s32[2,128]{1,0:T(2,128)}, u32[]{:S(2)}) copy-start(s32[2,128]{1,0:T(2,128)} %param.10) | copy-start | bytes 3076
  14.2 23.0 %copy-start.4 = (s32[2,128,16]{1,2,0:T(8,128)S(1)}, s32[2,128,16]{1,2,0:T(8,128)}, u32[]{:S(2)}) copy-start(s32[2,128,16]{1,2,0:T(8,128)} %param.9) | copy-start | bytes 49156
  14.2 23.0 %copy-start.5 = (s32[2,128,16,1]{1,3,2,0:T(1,128)S(1)}, s32[2,128,16,1]{1,3,2,0:T(1,128)}, u32[]{:S(2)}) copy-start(s32[2,128,16,1]{1,3,2,0:T(1,128)} %param.8) | copy-start | bytes 49156
  35.1 6.2 %collective-permute-start = (bf16[8192,128]{1,0:T(8,128)(2,1)S(1)}, bf16[8192,128]{1,0:T(8,128)(2,1)}, u32[]{:S(2)}, u32[]{:S(2)}) collective-permute-start(bf16[8192,128]{1,0:T(8,128)(2,1)S(1)} %bitcast.38), channel_id=1, source_target_pairs={{0,1},{1,0},{2,3},{3,2},{4,5},{5,4},{6,7},{7,6},{8,9},{9,8},{10,11... | collective-permute-start | bytes 6291464 | tf_op jit(solution)/shard_map/ppermute | solution.py:398
  38.5 2.7 %copy-start.1 = (bf16[512,1024]{1,0:T(8,128)(2,1)S(1)}, bf16[512,1024]{1,0:T(8,128)(2,1)}, u32[]{:S(2)}) copy-start(bf16[512,1024]{1,0:T(8,128)(2,1)} %w_input_hbm.1) | copy-start | bytes 3145732
  39.8 1.6 %copy-start = (bf16[1024,1024]{1,0:T(8,128)(2,1)S(1)}, bf16[1024,1024]{1,0:T(8,128)(2,1)}, u32[]{:S(2)}) copy-start(bf16[1024,1024]{1,0:T(8,128)(2,1)} %w_hidden_hbm.1) | copy-start | bytes 6291460
  55.4 5.5 %collective-permute-start.1 = (bf16[16,400,128]{2,1,0:T(8,128)(2,1)S(1)}, bf16[16,400,128]{2,1,0:T(8,128)(2,1)S(1)}, u32[]{:S(2)}, u32[]{:S(2)}) collective-permute-start(bf16[16,400,128]{2,1,0:T(8,128)(2,1)S(1)} %get-tuple-element.33), channel_id=1, source_target_pairs={{0,1},{1,0},{2,3},{3,2},{4,5},{5,4},{6,7},{7,6},{8,9},{9,8},{10,11... | collective-permute-start | bytes 4915208 | tf_op jit(solution)/shard_map/ppermute | solution.py:415
  97.3 47.6 %copy-start.2 = (f32[512,128]{1,0:T(8,128)S(1)}, f32[512,128]{1,0:T(8,128)}, u32[]{:S(2)}) copy-start(f32[512,128]{1,0:T(8,128)} %param.11) | copy-start | bytes 786436
  97.3 47.6 %copy-start.3 = (f32[512,128]{1,0:T(8,128)S(1)}, f32[512,128]{1,0:T(8,128)}, u32[]{:S(2)}) copy-start(f32[512,128]{1,0:T(8,128)} %param.12) | copy-start | bytes 786436

commit v5 on v4

--- a/solution.py
+++ b/solution.py
@@ -53,19 +53,16 @@
     index_ref,
     place_ref,
     order_ref,
-    own_hbm,
-    other_hbm,
+    own_ref,
+    other_ref,
     label_ref,
-    w_input_hbm,
-    w_hidden_hbm,
+    w_input_ref,
+    w_hidden_ref,
     w_output_ref,
     ids_ref,
-    kept_hbm,
-    sent_hbm,
+    kept_ref,
+    sent_ref,
     logit_ref,
-    half_ref,
-    w_input_ref,
-    w_hidden_ref,
     table_ref,
     pooled_ref,
     slot_ref,
@@ -73,35 +70,17 @@
     turned_ref,
     back_ref,
     term_ref,
-    sent_ref,
-    half_sem,
-    weight_sem,
-    sent_sem,
 ):
-    half = own_hbm.shape[0]
-    chunk = half // 2
+    half = own_ref.shape[0]
     samples = pooled_ref.shape[0] // SLOTS
-    tables = []
-    for k in range(4):
-        source = (own_hbm, other_hbm)[k // 2].at[pl.ds((k % 2) * chunk, chunk)]
-        tables.append(
-            pltpu.make_async_copy(source, half_ref.at[pl.ds(k * chunk, chunk)], half_sem.at[k])
-        )
-    weights = [
-        pltpu.make_async_copy(w_input_hbm, w_input_ref, weight_sem.at[0]),
-        pltpu.make_async_copy(w_hidden_hbm, w_hidden_ref, weight_sem.at[1]),
-    ]
-    for copy in tables + weights:
-        copy.start()
 
     def widen(step, carry):
         at = pl.multiple_of(step * 256, 256)
-        table_ref[pl.ds(at, 256), :] = half_ref[pl.ds(at, 256), :].astype(f32)
+        table_ref[pl.ds(at, 256), :] = own_ref[pl.ds(at, 256), :].astype(f32)
+        table_ref[pl.ds(half + at, 256), :] = other_ref[pl.ds(at, 256), :].astype(f32)
         return carry
 
-    for k in range(4):
-        tables[k].wait()
-        lax.fori_loop(k * chunk // 256, (k + 1) * chunk // 256, widen, 0)
+    lax.fori_loop(0, half // 256, widen, 0)
 
     def look(step, carry):
         slot_ref[pl.ds(pl.multiple_of(step * 512, 512), 512), :] = jnp.zeros((512, 128), f32)
@@ -136,8 +115,6 @@
         [pooled_ref[slot * samples : (slot + 1) * samples, :].astype(bf16) for slot in range(SLOTS)],
         axis=1,
     )
-    for copy in weights:
-        copy.wait()
     w_input = w_input_ref[...]
     w_hidden = w_hidden_ref[...]
     w_output = w_output_ref[...].astype(f32)
@@ -173,31 +150,20 @@
 
     lax.fori_loop(0, samples // 32, scatter, 0)
 
-    def pack(owner, carry):
-        at = pl.multiple_of(owner * GRAD_ROWS, GRAD_ROWS)
-        sent_ref[owner, 0:GRAD_ROWS, :] = slot_ref[pl.ds(at, GRAD_ROWS), :].astype(bf16)
-        piece = pl.ds(pl.multiple_of(order_ref[owner] * 16, 16), 16)
-        for j in range(8):
-            sent_ref[owner, GRAD_ROWS + j * 16 : GRAD_ROWS + (j + 1) * 16, :] = term_ref[
-                j, piece, :
-            ].astype(bf16)
-        sent_ref[owner, GRAD_ROWS + TERM_ROWS : SENT_ROWS, :] = ids_ref[owner]
-        return carry
-
-    step = SHARDS // 4
-    stores = []
-    for k, target in ((2, sent_hbm), (3, sent_hbm), (0, kept_hbm), (1, kept_hbm)):
-        lax.fori_loop(k * step, (k + 1) * step, pack, 0, unroll=4)
-        stores.append(
-            pltpu.make_async_copy(
-                sent_ref.at[pl.ds(k * step, step)],
-                target.at[pl.ds((k % 2) * step, step)],
-                sent_sem.at[k],
-            )
-        )
-        stores[-1].start()
-    for copy in stores:
-        copy.wait()
+    for target, base in ((sent_ref, SHARDS // 2), (kept_ref, 0)):
+
+        def pack(owner, carry):
+            at = pl.multiple_of((base + owner) * GRAD_ROWS, GRAD_ROWS)
+            target[owner, 0:GRAD_ROWS, :] = slot_ref[pl.ds(at, GRAD_ROWS), :].astype(bf16)
+            piece = pl.ds(pl.multiple_of(order_ref[base + owner] * 16, 16), 16)
+            for j in range(8):
+                target[owner, GRAD_ROWS + j * 16 : GRAD_ROWS + (j + 1) * 16, :] = term_ref[
+                    j, piece, :
+                ].astype(bf16)
+            target[owner, GRAD_ROWS + TERM_ROWS : SENT_ROWS, :] = ids_ref[base + owner]
+            return carry
+
+        lax.fori_loop(0, SHARDS // 2, pack, 0, unroll=4)
 
 
 def run_main(index, place, order, own, other, labels, w_input, w_hidden, w_output, ids):
@@ -205,8 +171,6 @@
     samples = index.shape[0] // LOOK
     smem = pl.BlockSpec(memory_space=pltpu.SMEM)
     vmem = pl.BlockSpec(memory_space=pltpu.VMEM)
-    anywhere = pl.BlockSpec(memory_space=pl.ANY)
-    hbm = pl.BlockSpec(memory_space=pltpu.HBM)
     return pl.pallas_call(
         main_kernel,
         out_shape=(
@@ -214,12 +178,9 @@
             jax.ShapeDtypeStruct((SHARDS // 2, SENT_ROWS, width), bf16),
             jax.ShapeDtypeStruct((BATCHES, samples // BATCHES), f32),
         ),
-        in_specs=[smem, smem, smem, anywhere, anywhere, vmem, hbm, hbm, vmem, vmem],
-        out_specs=(anywhere, anywhere, vmem),
+        in_specs=[smem] * 3 + [vmem] * 7,
+        out_specs=(vmem, vmem, vmem),
         scratch_shapes=[
-            pltpu.VMEM((2 * own.shape[0], width), bf16),
-            pltpu.VMEM(w_input.shape, bf16),
-            pltpu.VMEM(w_hidden.shape, bf16),
             pltpu.VMEM((2 * own.shape[0], width), f32),
             pltpu.VMEM((samples * SLOTS, width), f32),
             pltpu.VMEM((SHARDS * GRAD_ROWS, width), f32),
@@ -227,10 +188,6 @@
             pltpu.VMEM((SLOTS * width, samples), bf16),
             pltpu.VMEM((8, samples, width), bf16),
             pltpu.VMEM((8, SLOTS * width, width), f32),
-            pltpu.VMEM((SHARDS, SENT_ROWS, width), bf16),
-            pltpu.SemaphoreType.DMA((4,)),
-            pltpu.SemaphoreType.DMA((2,)),
-            pltpu.SemaphoreType.DMA((4,)),
         ],
         compiler_params=pltpu.CompilerParams(vmem_limit_bytes=40 * 1024 * 1024),
         cost_estimate=pl.CostEstimate(
@@ -239,14 +196,18 @@
     )(index, place, order, own, other, labels, w_input, w_hidden, w_output, ids)
 
 
+def row_code(row):
+    return jnp.where(row < 256, row + 1, 255 - row).astype(f32).astype(bf16)
+
+
 def add_source(source, owner, total, term):
-    names = lax.broadcasted_iota(jnp.int32, (total.shape[0], CAP), 0).astype(f32) + 1.0
-    coded = source[owner, GRAD_ROWS + TERM_ROWS : SENT_ROWS, :].astype(f32)
-    picks = []
-    for b in range(BATCHES):
-        named = coded[b : b + 1] * 256.0 + coded[BATCHES + b : BATCHES + b + 1]
-        picks.append(jnp.where(names == named, 1.0, 0.0).astype(bf16))
-    pick = jnp.concatenate(picks, axis=1)
+    rows = lax.broadcasted_iota(jnp.int32, (total.shape[0], CAP), 0)
+    names = row_code(rows)
+    coded = source[owner, GRAD_ROWS + TERM_ROWS : SENT_ROWS, :]
+    one, zero = jnp.ones((), bf16), jnp.zeros((), bf16)
+    pick = jnp.concatenate(
+        [jnp.where(names == coded[b : b + 1], one, zero) for b in range(BATCHES)], axis=1
+    )
     total = total + dot(pick, source[owner, 0:GRAD_ROWS, :], ((1,), (0,)))
     return total, term + source[owner, GRAD_ROWS : GRAD_ROWS + TERM_ROWS, :].astype(f32)
 
@@ -254,37 +215,40 @@
 def kept_kernel(kept_ref, out_ref):
     rows = out_ref.shape[1] - TERM_ROWS
     width = out_ref.shape[2]
-    for owner in range(out_ref.shape[0]):
+
+    def step(owner, carry):
         total = jnp.zeros((rows, width), f32)
         term = jnp.zeros((TERM_ROWS, width), f32)
         total, term = add_source(kept_ref, owner, total, term)
         out_ref[owner, 0:rows, :] = total.astype(bf16)
         out_ref[owner, rows : rows + TERM_ROWS, :] = term.astype(bf16)
+        return carry
+
+    lax.fori_loop(0, out_ref.shape[0], step, 0, unroll=2)
 
 
 def got_kernel(base_ref, got_ref, out_ref):
     rows = out_ref.shape[1] - TERM_ROWS
-    for owner in range(out_ref.shape[0]):
+
+    def step(owner, carry):
         total = base_ref[owner, 0:rows, :].astype(f32)
         term = base_ref[owner, rows : rows + TERM_ROWS, :].astype(f32)
         total, term = add_source(got_ref, owner, total, term)
         out_ref[owner, 0:rows, :] = total.astype(bf16)
         out_ref[owner, rows : rows + TERM_ROWS, :] = term.astype(bf16)
+        return carry
+
+    lax.fori_loop(0, out_ref.shape[0], step, 0, unroll=2)
 
 
 def run_owner(kernel, rows, *operands):
     owners, _, width = operands[0].shape
-    steps = 8
-    blocks = [
-        pl.BlockSpec((owners // steps, each.shape[1], width), lambda i: (i, 0, 0))
-        for each in operands
-    ]
+    vmem = pl.BlockSpec(memory_space=pltpu.VMEM)
     return pl.pallas_call(
         kernel,
-        grid=(steps,),
         out_shape=jax.ShapeDtypeStruct((owners, rows + TERM_ROWS, width), bf16),
-        in_specs=blocks,
-        out_specs=pl.BlockSpec((owners // steps, rows + TERM_ROWS, width), lambda i: (i, 0, 0)),
+        in_specs=[vmem] * len(operands),
+        out_specs=vmem,
         compiler_params=pltpu.CompilerParams(vmem_limit_bytes=32 * 1024 * 1024),
         cost_estimate=pl.CostEstimate(
             flops=550_000_000, bytes_accessed=5_000_000, transcendentals=0
@@ -322,6 +286,56 @@
     )(got)
 
 
+def sum_of(got_ref, first, last):
+    total = got_ref[0, first:last].astype(f32)
+    for source in range(1, 4):
+        total = total + got_ref[source, first:last].astype(f32)
+    return total
+
+
+def far_kernel(got_ref, out_ref):
+    total = sum_of(got_ref, 0, out_ref.shape[1]).astype(bf16)
+    for k in range(4):
+        out_ref[k] = total
+
+
+def run_far(got):
+    _, rows, width = got.shape
+    vmem = pl.BlockSpec(memory_space=pltpu.VMEM)
+    return pl.pallas_call(
+        far_kernel,
+        out_shape=jax.ShapeDtypeStruct((4, rows - 8, width), bf16),
+        in_specs=[vmem],
+        out_specs=vmem,
+        compiler_params=pltpu.CompilerParams(vmem_limit_bytes=16 * 1024 * 1024),
+        cost_estimate=pl.CostEstimate(flops=70_000, bytes_accessed=300_000, transcendentals=0),
+    )(got)
+
+
+def final_kernel(total_ref, table_ref, sums_ref, got_ref, new_ref, term_ref):
+    grad = total_ref[...].astype(f32)
+    new_sums = sums_ref[...] + grad * grad
+    new_ref[...] = table_ref[...] - learn_rate * grad / jnp.sqrt(new_sums)
+    term_ref[...] = sum_of(got_ref, got_ref.shape[1] - 8, got_ref.shape[1])
+
+
+def run_final(total, table, sums, got):
+    vmem = pl.BlockSpec(memory_space=pltpu.VMEM)
+    return pl.pallas_call(
+        final_kernel,
+        out_shape=(
+            jax.ShapeDtypeStruct(table.shape, f32),
+            jax.ShapeDtypeStruct((8, table.shape[1]), f32),
+        ),
+        in_specs=[vmem] * 4,
+        out_specs=(vmem, vmem),
+        compiler_params=pltpu.CompilerParams(vmem_limit_bytes=16 * 1024 * 1024),
+        cost_estimate=pl.CostEstimate(
+            flops=500_000, bytes_accessed=1_000_000, transcendentals=65536
+        ),
+    )(total, table, sums, got)
+
+
 def owner_order(core):
     group = jnp.arange(SHARDS, dtype=jnp.int32)
     c = (group >> 4) ^ core
@@ -358,17 +372,11 @@
         (hit.astype(f32) * (rank + base)).reshape(batches, samples, looks, SHARDS), axis=3
     ).astype(jnp.int32)
     place = owner * GRAD_ROWS + batch[:, None, None] * CAP + spot
-    code = row + 1
-    high = (code >> 8).astype(bf16)
-    low = (code & 255).astype(bf16)
     flat_hit = hit.reshape(batches, samples * looks, SHARDS)
-    coded = jnp.concatenate(
-        [flat_hit * high.reshape(batches, -1, 1), flat_hit * low.reshape(batches, -1, 1)], axis=2
-    )
+    coded = flat_hit * row_code(row).reshape(batches, -1, 1)
     where = (spot.reshape(batches, -1, 1) == spots).astype(bf16)
     ids = jnp.einsum("bin,bip->bnp", coded, where, preferred_element_type=f32).astype(bf16)
-    ids = ids.reshape(batches, 2, SHARDS, CAP).transpose(2, 1, 0, 3).reshape(SHARDS, 2 * batches, CAP)
-    ids = jnp.pad(ids, ((0, 0), (0, ID_ROWS - 2 * batches), (0, 0)))
+    ids = jnp.pad(ids.transpose(1, 0, 2), ((0, 0), (0, ID_ROWS - batches), (0, 0)))
     return place.reshape(-1), ids
 
 
@@ -376,11 +384,6 @@
     x, y, c = owner >> 3, (owner >> 1) & 3, owner & 1
     chip = jnp.where(c == 0, y * 4 + x, x * 4 + y)
     return (((c ^ core) * 16 + chip) * rows + row).reshape(-1)
-
-
-def adagrad_step(table_part, sums_part, grad_part):
-    new_sums = sums_part + grad_part * grad_part
-    return table_part - learn_rate * grad_part / jnp.sqrt(new_sums)
 
 
 def local(
@@ -422,13 +425,10 @@
     term = jnp.sum(near[:, 128:160], axis=0)
     term = term.reshape(8, 4, width).transpose(1, 0, 2).astype(bf16)
     far = jnp.concatenate([jnp.broadcast_to(grads[None], (4, 128, width)), term], axis=1)
-    far = exchange(far, "grp", FAR).astype(f32)
-    input_grad = jnp.sum(far[:, 128:136], axis=0).reshape(-1)
-    part = jnp.sum(far[:, 0:128], axis=0).astype(bf16)
-    part, input_grad = lax.optimization_barrier((part, input_grad))
-    total = spread(part, "grp", NEAR).reshape(rows, width).astype(f32)
-    new_table = adagrad_step(row_table, squared_sums, total)
-    return (new_table, logits, input_grad)
+    far = exchange(far, "grp", FAR)
+    total = exchange(run_far(far), "grp", NEAR).reshape(rows, width)
+    new_table, input_grad = run_final(total, row_table, squared_sums, far)
+    return (new_table, logits, input_grad.reshape(-1))
 
 
 def solution(mesh):

time: 146 us -> 146 us (level)
  other arithmetic: 4.22 us -> 2.62 us
    pallas_call x1, Pallas kernels: 14.1 us -> 12.5 us  [run_main(): pl.pallas_call(main_kernel, out_shape=(jax.ShapeDtypeStruct((SHARDS // 2,...]
    unnamed x16 -> x17, local copies, waits for them, and re-layouts: 0.14 us -> 1.65 us
    pallas_call x2 -> x4, Pallas kernels: 5.01 us -> 5.7 us  [the longest x2 4.85 us: run_owner(): pl.pallas_call(kernel, out_shape=jax.ShapeDtypeStruct((owners, rows + TER...]
  transfers between devices with their start and end apart: 2 -> 2, of which waited for: 2 -> 2; matrix products, arithmetic and copies ran while one was open for 3% -> 2% of each run, Pallas kernels for 2% -> 2%
where the time goes in v5:
time: 146 us; the launch traced here: 145 us
  blocking collectives  113 us (77%)
  Pallas kernels  18.3 us (13%)
  starting transfers between devices  4.06 us (3%)
  local copies, waits for them, and re-layouts  3.3 us (2%)
  other arithmetic  2.62 us (2%)
  waiting for transfers between devices  1.87 us (1%)
    all_to_all x7, blocking collectives, exchange(): lax.all_to_all(value, axis, split_axis=0, concat_axis=0, tiled=True, axis...  113 us
    pallas_call x1, Pallas kernels, run_main(): pl.pallas_call(main_kernel, out_shape=(jax.ShapeDtypeStruct((SHARDS // 2,...  12.5 us
    pallas_call x2, Pallas kernels, run_owner(): pl.pallas_call(kernel, out_shape=jax.ShapeDtypeStruct((owners, rows + TER...  4.85 us
  transfers between devices with their start and end apart: 2, of which 2 were waited for; matrix products, arithmetic and copies ran while one was open for 2% of the time, Pallas kernels for 2%

profile of v5, /device:TPU:32, one launch (start us, length us, event | category | flops | bytes accessed | tf_op | source)
XLA Modules:
  0.0 145.2 jit_solution(7628393538325592575)
XLA Ops:
  0.6 1.0 convert_element_type.69
  1.7 12.2 %all_to_all.35 = bf16[4,512,128]{2,1,0:T(8,128)(2,1)S(1)} all-to-all(bf16[4,512,128]{2,1,0:T(8,128)(2,1)S(1)} %broadcast_in_dim.28), channel_id=1, replica_groups={{0,8,16,24},{2,10,18,26},{4,12,20,28},{6,14,22,30},{1,3,5,7},{9,11,13,1..., dimensions={0} | all-to-all | bytes 1048576 | tf_op jit(solution)/shard_map/all_to_all | solution.py:35
  13.9 0.3 broadcast_in_dim.30
  14.2 20.9 %all_to_all.36 = bf16[4,2048,128]{2,1,0:T(8,128)(2,1)S(1)} all-to-all(bf16[4,2048,128]{2,1,0:T(8,128)(2,1)S(1)} %broadcast_in_dim.30), channel_id=1, replica_groups={{0,2,4,6},{8,10,12,14},{16,18,20,22},{24,26,28,30},{1,9,17,25},{3,11,19..., dimensions={0} | all-to-all | bytes 4194304 | tf_op jit(solution)/shard_map/all_to_all | solution.py:35
  35.1 2.0 %collective-permute-start = (bf16[8192,128]{1,0:T(8,128)(2,1)S(1)}, bf16[8192,128]{1,0:T(8,128)(2,1)}, u32[]{:S(2)}, u32[]{:S(2)}) collective-permute-start(bf16[8192,128]{1,0:T(8,128)(2,1)S(1)} %bitcast.29), channel_id=1, source_target_pairs={{0,1},{1,0},{2,3},{3,2},{4,5},{5,4},{6,7},{7,6},{8,9},{9,8},{10,11... | collective-permute-start | bytes 6291464 | tf_op jit(solution)/shard_map/ppermute | solution.py:401
  37.4 0.3 convert_reduce_fusion
  37.8 0.1 select_reduce_fusion
  38.3 0.1 bitcast_compare_fusion
  38.4 0.3 bitcast_reduce_fusion
  39.1 0.8 fusion.4
  40.4 0.9 collective-permute-done.other_ref
  41.4 1.6 %copy-done = bf16[1024,1024]{1,0:T(8,128)(2,1)S(1)} copy-done((bf16[1024,1024]{1,0:T(8,128)(2,1)S(1)}, bf16[1024,1024]{1,0:T(8,128)(2,1)}, u32[]{:S(2)}) %copy-start) | copy-done | bytes 2097176
  43.0 12.5 %shard_map.103 = (bf16[16,400,128]{2,1,0:T(8,128)(2,1)S(1)}, bf16[16,400,128]{2,1,0:T(8,128)(2,1)S(1)}, f32[2,128]{1,0:T(2,128)}) custom-call(s32[4096]{0:T(1024)S(1)} %reshape.99.index_ref, s32[4096]{0:T(1024)S(1)} %reshape.101.place_ref, s32[32]{0:T(128)S(1)} %fusion.19.order_ref, bf16[8192,128]{1,0:T(8,128)(2,1)S(1)} %bitcast.30, ...), custom_call_target="tpu_custom_call" | custom-call | flops 2000000000 | bytes 12000000 | tf_op jit(solution)/shard_map/pallas_call | solution.py:174
  55.5 2.0 %collective-permute-start.1 = (bf16[16,400,128]{2,1,0:T(8,128)(2,1)S(1)}, bf16[16,400,128]{2,1,0:T(8,128)(2,1)S(1)}, u32[]{:S(2)}, u32[]{:S(2)}) collective-permute-start(bf16[16,400,128]{2,1,0:T(8,128)(2,1)S(1)} %get-tuple-element.33), channel_id=1, source_target_pairs={{0,1},{1,0},{2,3},{3,2},{4,5},{5,4},{6,7},{7,6},{8,9},{9,8},{10,11... | collective-permute-start | bytes 4915208 | tf_op jit(solution)/shard_map/ppermute | solution.py:418
  57.5 2.4 %shard_map.104.base_ref = bf16[16,640,128]{2,1,0:T(8,128)(2,1)S(1)} custom-call(bf16[16,400,128]{2,1,0:T(8,128)(2,1)S(1)} %get-tuple-element.32.kept_ref), custom_call_target="tpu_custom_call" | custom-call | flops 550000000 | bytes 5000000 | tf_op jit(solution)/shard_map/pallas_call | solution.py:247
  59.9 0.9 collective-permute-done.1.got_ref
  60.9 2.4 %shard_map.105 = bf16[16,640,128]{2,1,0:T(8,128)(2,1)S(1)} custom-call(bf16[16,640,128]{2,1,0:T(8,128)(2,1)S(1)} %shard_map.104.base_ref, bf16[16,400,128]{2,1,0:T(8,128)(2,1)S(1)} %collective-permute-done.1.got_ref), custom_call_target="tpu_custom_call" | custom-call | flops 550000000 | bytes 5000000 | tf_op jit(solution)/shard_map/pallas_call | solution.py:247
  63.3 21.8 %all_to_all.37 = bf16[4,2560,128]{2,1,0:T(8,128)(2,1)S(1)} all-to-all(bf16[4,2560,128]{2,1,0:T(8,128)(2,1)S(1)} %bitcast.28), channel_id=1, replica_groups={{0,8,16,24},{2,10,18,26},{4,12,20,28},{6,14,22,30},{1,3,5,7},{9,11,13,1..., dimensions={0} | all-to-all | bytes 5242880 | tf_op jit(solution)/shard_map/all_to_all | solution.py:35
  85.1 0.8 reduce_sum.60
  86.0 11.3 %all_to_all.38.got_ref = bf16[4,640,128]{2,1,0:T(8,128)(2,1)S(1)} all-to-all(bf16[4,640,128]{2,1,0:T(8,128)(2,1)S(1)} %bitcast.32), channel_id=1, replica_groups={{0,2,4,6},{8,10,12,14},{16,18,20,22},{24,26,28,30},{1,9,17,25},{3,11,19..., dimensions={0} | all-to-all | bytes 1310720 | tf_op jit(solution)/shard_map/all_to_all | solution.py:35
  97.4 11.3 %all_to_all.39 = bf16[4,160,128]{2,1,0:T(8,128)(2,1)S(1)} all-to-all(bf16[4,160,128]{2,1,0:T(8,128)(2,1)S(1)} %shard_map.106), channel_id=1, replica_groups={{0,32,64,96},{128,160,192,224},{256,288,320,352},{384,416,448,480},{1,3..., dimensions={0} | all-to-all | bytes 327680 | tf_op jit(solution)/shard_map/all_to_all | solution.py:35
  108.8 26.2 %all_to_all.40.got_ref = bf16[4,136,128]{2,1,0:T(8,128)(2,1)S(1)} all-to-all(bf16[4,136,128]{2,1,0:T(8,128)(2,1)S(1)} %pad_maximum_fusion), channel_id=1, replica_groups={{0,128,256,384},{32,160,288,416},{64,192,320,448},{96,224,352,480},{1,1..., dimensions={0} | all-to-all | bytes 278528 | tf_op jit(solution)/shard_map/all_to_all | solution.py:35
  135.1 9.3 %all_to_all.41 = bf16[4,128,128]{2,1,0:T(8,128)(2,1)S(1)} all-to-all(bf16[4,128,128]{2,1,0:T(8,128)(2,1)S(1)} %shard_map.107), channel_id=1, replica_groups={{0,32,64,96},{128,160,192,224},{256,288,320,352},{384,416,448,480},{1,3..., dimensions={0} | all-to-all | bytes 262144 | tf_op jit(solution)/shard_map/all_to_all | solution.py:35
  144.4 0.8 shard_map.108
  (51 shorter events, 1.8 us)
Async XLA Ops:
  14.1 23.0 %copy-start.6 = (bf16[1024]{0:T(1024)(128)(2,1)S(1)}, bf16[1024]{0:T(1024)(128)(2,1)}, u32[]{:S(2)}) copy-start(bf16[1024]{0:T(1024)(128)(2,1)} %param.15) | copy-start | bytes 6148
  14.1 23.1 %copy-start.7 = (s32[2,128]{1,0:T(2,128)S(1)}, s32[2,128]{1,0:T(2,128)}, u32[]{:S(2)}) copy-start(s32[2,128]{1,0:T(2,128)} %param.10) | copy-start | bytes 3076
  14.2 23.2 %copy-start.4 = (s32[2,128,16]{1,2,0:T(8,128)S(1)}, s32[2,128,16]{1,2,0:T(8,128)}, u32[]{:S(2)}) copy-start(s32[2,128,16]{1,2,0:T(8,128)} %param.9) | copy-start | bytes 49156
  14.2 23.1 %copy-start.5 = (s32[2,128,16,1]{1,3,2,0:T(1,128)S(1)}, s32[2,128,16,1]{1,3,2,0:T(1,128)}, u32[]{:S(2)}) copy-start(s32[2,128,16,1]{1,3,2,0:T(1,128)} %param.8) | copy-start | bytes 49156
  35.1 6.3 %copy-start.2 = (bf16[512,1024]{1,0:T(8,128)(2,1)S(1)}, bf16[512,1024]{1,0:T(8,128)(2,1)}, u32[]{:S(2)}) copy-start(bf16[512,1024]{1,0:T(8,128)(2,1)} %w_input_ref.1) | copy-start | bytes 3145732
  35.1 6.3 %collective-permute-start = (bf16[8192,128]{1,0:T(8,128)(2,1)S(1)}, bf16[8192,128]{1,0:T(8,128)(2,1)}, u32[]{:S(2)}, u32[]{:S(2)}) collective-permute-start(bf16[8192,128]{1,0:T(8,128)(2,1)S(1)} %bitcast.29), channel_id=1, source_target_pairs={{0,1},{1,0},{2,3},{3,2},{4,5},{5,4},{6,7},{7,6},{8,9},{9,8},{10,11... | collective-permute-start | bytes 6291464 | tf_op jit(solution)/shard_map/ppermute | solution.py:401
  41.4 1.6 %copy-start = (bf16[1024,1024]{1,0:T(8,128)(2,1)S(1)}, bf16[1024,1024]{1,0:T(8,128)(2,1)}, u32[]{:S(2)}) copy-start(bf16[1024,1024]{1,0:T(8,128)(2,1)} %w_hidden_ref.1) | copy-start | bytes 6291460
  55.5 5.4 %collective-permute-start.1 = (bf16[16,400,128]{2,1,0:T(8,128)(2,1)S(1)}, bf16[16,400,128]{2,1,0:T(8,128)(2,1)S(1)}, u32[]{:S(2)}, u32[]{:S(2)}) collective-permute-start(bf16[16,400,128]{2,1,0:T(8,128)(2,1)S(1)} %get-tuple-element.33), channel_id=1, source_target_pairs={{0,1},{1,0},{2,3},{3,2},{4,5},{5,4},{6,7},{7,6},{8,9},{9,8},{10,11... | collective-permute-start | bytes 4915208 | tf_op jit(solution)/shard_map/ppermute | solution.py:418
  86.0 58.4 %copy-start.1 = (f32[512,128]{1,0:T(8,128)S(1)}, f32[512,128]{1,0:T(8,128)}, u32[]{:S(2)}) copy-start(f32[512,128]{1,0:T(8,128)} %table_ref.1) | copy-start | bytes 786436
  86.0 58.4 %copy-start.3 = (f32[512,128]{1,0:T(8,128)S(1)}, f32[512,128]{1,0:T(8,128)}, u32[]{:S(2)}) copy-start(f32[512,128]{1,0:T(8,128)} %sums_ref.1) | copy-start | bytes 786436

commit v6 on v5

--- a/solution.py
+++ b/solution.py
@@ -189,7 +189,7 @@
             pltpu.VMEM((8, samples, width), bf16),
             pltpu.VMEM((8, SLOTS * width, width), f32),
         ],
-        compiler_params=pltpu.CompilerParams(vmem_limit_bytes=40 * 1024 * 1024),
+        compiler_params=pltpu.CompilerParams(vmem_limit_bytes=24 * 1024 * 1024),
         cost_estimate=pl.CostEstimate(
             flops=2_000_000_000, bytes_accessed=12_000_000, transcendentals=256
         ),
@@ -224,7 +224,7 @@
         out_ref[owner, rows : rows + TERM_ROWS, :] = term.astype(bf16)
         return carry
 
-    lax.fori_loop(0, out_ref.shape[0], step, 0, unroll=2)
+    lax.fori_loop(0, out_ref.shape[0], step, 0, unroll=8)
 
 
 def got_kernel(base_ref, got_ref, out_ref):
@@ -238,7 +238,7 @@
         out_ref[owner, rows : rows + TERM_ROWS, :] = term.astype(bf16)
         return carry
 
-    lax.fori_loop(0, out_ref.shape[0], step, 0, unroll=2)
+    lax.fori_loop(0, out_ref.shape[0], step, 0, unroll=8)
 
 
 def run_owner(kernel, rows, *operands):

time: 146 us -> 145 us (level)
  Pallas kernels: 18.3 us -> 16.3 us
    pallas_call x2, Pallas kernels: 4.85 us -> 2.87 us  [run_owner(): pl.pallas_call(kernel, out_shape=jax.ShapeDtypeStruct((owners, rows + TER...]
  transfers between devices with their start and end apart: 2 -> 2, of which waited for: 2 -> 2; matrix products, arithmetic and copies ran while one was open for 2% -> 2% of each run, Pallas kernels for 2% -> 1%
where the time goes in v6:
time: 145 us; the launch traced here: 144 us
  blocking collectives  113 us (78%)
  Pallas kernels  16.3 us (11%)
  starting transfers between devices  4.07 us (3%)
  local copies, waits for them, and re-layouts  3.3 us (2%)
  waiting for transfers between devices  2.85 us (2%)
  other arithmetic  2.62 us (2%)
    all_to_all x7, blocking collectives, exchange(): lax.all_to_all(value, axis, split_axis=0, concat_axis=0, tiled=True, axis...  113 us
    pallas_call x1, Pallas kernels, run_main(): pl.pallas_call(main_kernel, out_shape=(jax.ShapeDtypeStruct((SHARDS // 2,...  12.5 us
  transfers between devices with their start and end apart: 2, of which 2 were waited for; matrix products, arithmetic and copies ran while one was open for 2% of the time, Pallas kernels for 1%

profile of v6, /device:TPU:32, one launch (start us, length us, event | category | flops | bytes accessed | tf_op | source)
XLA Modules:
  0.0 144.2 jit_solution(4428361912042722134)
XLA Ops:
  0.6 1.0 convert_element_type.69
  1.7 12.2 %all_to_all.35 = bf16[4,512,128]{2,1,0:T(8,128)(2,1)S(1)} all-to-all(bf16[4,512,128]{2,1,0:T(8,128)(2,1)S(1)} %broadcast_in_dim.28), channel_id=1, replica_groups={{0,8,16,24},{2,10,18,26},{4,12,20,28},{6,14,22,30},{1,3,5,7},{9,11,13,1..., dimensions={0} | all-to-all | bytes 1048576 | tf_op jit(solution)/shard_map/all_to_all | solution.py:35
  13.9 0.3 broadcast_in_dim.30
  14.2 20.9 %all_to_all.36 = bf16[4,2048,128]{2,1,0:T(8,128)(2,1)S(1)} all-to-all(bf16[4,2048,128]{2,1,0:T(8,128)(2,1)S(1)} %broadcast_in_dim.30), channel_id=1, replica_groups={{0,2,4,6},{8,10,12,14},{16,18,20,22},{24,26,28,30},{1,9,17,25},{3,11,19..., dimensions={0} | all-to-all | bytes 4194304 | tf_op jit(solution)/shard_map/all_to_all | solution.py:35
  35.1 2.0 %collective-permute-start = (bf16[8192,128]{1,0:T(8,128)(2,1)S(1)}, bf16[8192,128]{1,0:T(8,128)(2,1)}, u32[]{:S(2)}, u32[]{:S(2)}) collective-permute-start(bf16[8192,128]{1,0:T(8,128)(2,1)S(1)} %bitcast.29), channel_id=1, source_target_pairs={{0,1},{1,0},{2,3},{3,2},{4,5},{5,4},{6,7},{7,6},{8,9},{9,8},{10,11... | collective-permute-start | bytes 6291464 | tf_op jit(solution)/shard_map/ppermute | solution.py:401
  37.4 0.3 convert_reduce_fusion
  37.8 0.1 select_reduce_fusion
  38.3 0.1 bitcast_compare_fusion
  38.4 0.3 bitcast_reduce_fusion
  39.1 0.8 fusion.4
  40.4 0.9 collective-permute-done.other_ref
  41.4 1.6 %copy-done = bf16[1024,1024]{1,0:T(8,128)(2,1)S(1)} copy-done((bf16[1024,1024]{1,0:T(8,128)(2,1)S(1)}, bf16[1024,1024]{1,0:T(8,128)(2,1)}, u32[]{:S(2)}) %copy-start) | copy-done | bytes 2097176
  43.0 12.5 %shard_map.103 = (bf16[16,400,128]{2,1,0:T(8,128)(2,1)S(1)}, bf16[16,400,128]{2,1,0:T(8,128)(2,1)S(1)}, f32[2,128]{1,0:T(2,128)}) custom-call(s32[4096]{0:T(1024)S(1)} %reshape.99.index_ref, s32[4096]{0:T(1024)S(1)} %reshape.101.place_ref, s32[32]{0:T(128)S(1)} %fusion.19.order_ref, bf16[8192,128]{1,0:T(8,128)(2,1)S(1)} %bitcast.30, ...), custom_call_target="tpu_custom_call" | custom-call | flops 2000000000 | bytes 12000000 | tf_op jit(solution)/shard_map/pallas_call | solution.py:174
  55.5 2.0 %collective-permute-start.1 = (bf16[16,400,128]{2,1,0:T(8,128)(2,1)S(1)}, bf16[16,400,128]{2,1,0:T(8,128)(2,1)S(1)}, u32[]{:S(2)}, u32[]{:S(2)}) collective-permute-start(bf16[16,400,128]{2,1,0:T(8,128)(2,1)S(1)} %get-tuple-element.33), channel_id=1, source_target_pairs={{0,1},{1,0},{2,3},{3,2},{4,5},{5,4},{6,7},{7,6},{8,9},{9,8},{10,11... | collective-permute-start | bytes 4915208 | tf_op jit(solution)/shard_map/ppermute | solution.py:418
  57.5 1.4 shard_map.104.base_ref
  59.0 1.9 %collective-permute-done.1.got_ref = bf16[16,400,128]{2,1,0:T(8,128)(2,1)S(1)} collective-permute-done((bf16[16,400,128]{2,1,0:T(8,128)(2,1)S(1)}, bf16[16,400,128]{2,1,0:T(8,128)(2,1)S(1)}, u32[]{:S(2)}, u32[]{:S(2)}) %collective-permute-start.1) | collective-permute-done | bytes 1638432 | tf_op jit(solution)/shard_map/ppermute | solution.py:418
  60.9 1.4 shard_map.105
  62.3 21.8 %all_to_all.37 = bf16[4,2560,128]{2,1,0:T(8,128)(2,1)S(1)} all-to-all(bf16[4,2560,128]{2,1,0:T(8,128)(2,1)S(1)} %bitcast.28), channel_id=1, replica_groups={{0,8,16,24},{2,10,18,26},{4,12,20,28},{6,14,22,30},{1,3,5,7},{9,11,13,1..., dimensions={0} | all-to-all | bytes 5242880 | tf_op jit(solution)/shard_map/all_to_all | solution.py:35
  84.1 0.8 reduce_sum.60
  85.0 11.3 %all_to_all.38.got_ref = bf16[4,640,128]{2,1,0:T(8,128)(2,1)S(1)} all-to-all(bf16[4,640,128]{2,1,0:T(8,128)(2,1)S(1)} %bitcast.32), channel_id=1, replica_groups={{0,2,4,6},{8,10,12,14},{16,18,20,22},{24,26,28,30},{1,9,17,25},{3,11,19..., dimensions={0} | all-to-all | bytes 1310720 | tf_op jit(solution)/shard_map/all_to_all | solution.py:35
  96.4 11.2 %all_to_all.39 = bf16[4,160,128]{2,1,0:T(8,128)(2,1)S(1)} all-to-all(bf16[4,160,128]{2,1,0:T(8,128)(2,1)S(1)} %shard_map.106), channel_id=1, replica_groups={{0,32,64,96},{128,160,192,224},{256,288,320,352},{384,416,448,480},{1,3..., dimensions={0} | all-to-all | bytes 327680 | tf_op jit(solution)/shard_map/all_to_all | solution.py:35
  107.8 26.3 %all_to_all.40.got_ref = bf16[4,136,128]{2,1,0:T(8,128)(2,1)S(1)} all-to-all(bf16[4,136,128]{2,1,0:T(8,128)(2,1)S(1)} %pad_maximum_fusion), channel_id=1, replica_groups={{0,128,256,384},{32,160,288,416},{64,192,320,448},{96,224,352,480},{1,1..., dimensions={0} | all-to-all | bytes 278528 | tf_op jit(solution)/shard_map/all_to_all | solution.py:35
  134.1 9.3 %all_to_all.41 = bf16[4,128,128]{2,1,0:T(8,128)(2,1)S(1)} all-to-all(bf16[4,128,128]{2,1,0:T(8,128)(2,1)S(1)} %shard_map.107), channel_id=1, replica_groups={{0,32,64,96},{128,160,192,224},{256,288,320,352},{384,416,448,480},{1,3..., dimensions={0} | all-to-all | bytes 262144 | tf_op jit(solution)/shard_map/all_to_all | solution.py:35
  143.4 0.8 shard_map.108
  (51 shorter events, 1.8 us)
Async XLA Ops:
  14.1 23.0 %copy-start.6 = (bf16[1024]{0:T(1024)(128)(2,1)S(1)}, bf16[1024]{0:T(1024)(128)(2,1)}, u32[]{:S(2)}) copy-start(bf16[1024]{0:T(1024)(128)(2,1)} %param.15) | copy-start | bytes 6148
  14.1 23.1 %copy-start.7 = (s32[2,128]{1,0:T(2,128)S(1)}, s32[2,128]{1,0:T(2,128)}, u32[]{:S(2)}) copy-start(s32[2,128]{1,0:T(2,128)} %param.10) | copy-start | bytes 3076
  14.2 23.2 %copy-start.4 = (s32[2,128,16]{1,2,0:T(8,128)S(1)}, s32[2,128,16]{1,2,0:T(8,128)}, u32[]{:S(2)}) copy-start(s32[2,128,16]{1,2,0:T(8,128)} %param.9) | copy-start | bytes 49156
  14.2 23.1 %copy-start.5 = (s32[2,128,16,1]{1,3,2,0:T(1,128)S(1)}, s32[2,128,16,1]{1,3,2,0:T(1,128)}, u32[]{:S(2)}) copy-start(s32[2,128,16,1]{1,3,2,0:T(1,128)} %param.8) | copy-start | bytes 49156
  35.1 6.3 %copy-start.2 = (bf16[512,1024]{1,0:T(8,128)(2,1)S(1)}, bf16[512,1024]{1,0:T(8,128)(2,1)}, u32[]{:S(2)}) copy-start(bf16[512,1024]{1,0:T(8,128)(2,1)} %w_input_ref.1) | copy-start | bytes 3145732
  35.1 6.3 %collective-permute-start = (bf16[8192,128]{1,0:T(8,128)(2,1)S(1)}, bf16[8192,128]{1,0:T(8,128)(2,1)}, u32[]{:S(2)}, u32[]{:S(2)}) collective-permute-start(bf16[8192,128]{1,0:T(8,128)(2,1)S(1)} %bitcast.29), channel_id=1, source_target_pairs={{0,1},{1,0},{2,3},{3,2},{4,5},{5,4},{6,7},{7,6},{8,9},{9,8},{10,11... | collective-permute-start | bytes 6291464 | tf_op jit(solution)/shard_map/ppermute | solution.py:401
  41.4 1.6 %copy-start = (bf16[1024,1024]{1,0:T(8,128)(2,1)S(1)}, bf16[1024,1024]{1,0:T(8,128)(2,1)}, u32[]{:S(2)}) copy-start(bf16[1024,1024]{1,0:T(8,128)(2,1)} %w_hidden_ref.1) | copy-start | bytes 6291460
  55.5 5.4 %collective-permute-start.1 = (bf16[16,400,128]{2,1,0:T(8,128)(2,1)S(1)}, bf16[16,400,128]{2,1,0:T(8,128)(2,1)S(1)}, u32[]{:S(2)}, u32[]{:S(2)}) collective-permute-start(bf16[16,400,128]{2,1,0:T(8,128)(2,1)S(1)} %get-tuple-element.33), channel_id=1, source_target_pairs={{0,1},{1,0},{2,3},{3,2},{4,5},{5,4},{6,7},{7,6},{8,9},{9,8},{10,11... | collective-permute-start | bytes 4915208 | tf_op jit(solution)/shard_map/ppermute | solution.py:418
  85.0 58.4 %copy-start.1 = (f32[512,128]{1,0:T(8,128)S(1)}, f32[512,128]{1,0:T(8,128)}, u32[]{:S(2)}) copy-start(f32[512,128]{1,0:T(8,128)} %table_ref.1) | copy-start | bytes 786436
  85.0 58.4 %copy-start.3 = (f32[512,128]{1,0:T(8,128)S(1)}, f32[512,128]{1,0:T(8,128)}, u32[]{:S(2)}) copy-start(f32[512,128]{1,0:T(8,128)} %sums_ref.1) | copy-start | bytes 786436

commit v7 on v6

--- a/solution.py
+++ b/solution.py
@@ -54,15 +54,17 @@
     place_ref,
     order_ref,
     own_ref,
-    other_ref,
+    other_hbm,
     label_ref,
     w_input_ref,
-    w_hidden_ref,
+    w_hidden_hbm,
     w_output_ref,
     ids_ref,
     kept_ref,
     sent_ref,
     logit_ref,
+    other_ref,
+    w_hidden_ref,
     table_ref,
     pooled_ref,
     slot_ref,
@@ -70,17 +72,26 @@
     turned_ref,
     back_ref,
     term_ref,
+    other_sem,
+    weight_sem,
 ):
     half = own_ref.shape[0]
     samples = pooled_ref.shape[0] // SLOTS
-
-    def widen(step, carry):
-        at = pl.multiple_of(step * 256, 256)
-        table_ref[pl.ds(at, 256), :] = own_ref[pl.ds(at, 256), :].astype(f32)
-        table_ref[pl.ds(half + at, 256), :] = other_ref[pl.ds(at, 256), :].astype(f32)
-        return carry
-
-    lax.fori_loop(0, half // 256, widen, 0)
+    swap = pltpu.make_async_copy(other_hbm, other_ref, other_sem)
+    swap.start()
+    fetch = pltpu.make_async_copy(w_hidden_hbm, w_hidden_ref, weight_sem)
+    fetch.start()
+
+    for source, base in ((own_ref, 0), (other_ref, half)):
+        if base:
+            swap.wait()
+
+        def widen(step, carry):
+            at = pl.multiple_of(step * 256, 256)
+            table_ref[pl.ds(base + at, 256), :] = source[pl.ds(at, 256), :].astype(f32)
+            return carry
+
+        lax.fori_loop(0, half // 256, widen, 0, unroll=2)
 
     def look(step, carry):
         slot_ref[pl.ds(pl.multiple_of(step * 512, 512), 512), :] = jnp.zeros((512, 128), f32)
@@ -115,6 +126,7 @@
         [pooled_ref[slot * samples : (slot + 1) * samples, :].astype(bf16) for slot in range(SLOTS)],
         axis=1,
     )
+    fetch.wait()
     w_input = w_input_ref[...]
     w_hidden = w_hidden_ref[...]
     w_output = w_output_ref[...].astype(f32)
@@ -171,6 +183,7 @@
     samples = index.shape[0] // LOOK
     smem = pl.BlockSpec(memory_space=pltpu.SMEM)
     vmem = pl.BlockSpec(memory_space=pltpu.VMEM)
+    anywhere = pl.BlockSpec(memory_space=pl.ANY)
     return pl.pallas_call(
         main_kernel,
         out_shape=(
@@ -178,9 +191,11 @@
             jax.ShapeDtypeStruct((SHARDS // 2, SENT_ROWS, width), bf16),
             jax.ShapeDtypeStruct((BATCHES, samples // BATCHES), f32),
         ),
-        in_specs=[smem] * 3 + [vmem] * 7,
+        in_specs=[smem] * 3 + [vmem, anywhere, vmem, vmem, anywhere, vmem, vmem],
         out_specs=(vmem, vmem, vmem),
         scratch_shapes=[
+            pltpu.VMEM(other.shape, bf16),
+            pltpu.VMEM(w_hidden.shape, bf16),
             pltpu.VMEM((2 * own.shape[0], width), f32),
             pltpu.VMEM((samples * SLOTS, width), f32),
             pltpu.VMEM((SHARDS * GRAD_ROWS, width), f32),
@@ -188,8 +203,10 @@
             pltpu.VMEM((SLOTS * width, samples), bf16),
             pltpu.VMEM((8, samples, width), bf16),
             pltpu.VMEM((8, SLOTS * width, width), f32),
+            pltpu.SemaphoreType.DMA(()),
+            pltpu.SemaphoreType.DMA(()),
         ],
-        compiler_params=pltpu.CompilerParams(vmem_limit_bytes=24 * 1024 * 1024),
+        compiler_params=pltpu.CompilerParams(vmem_limit_bytes=44 * 1024 * 1024),
         cost_estimate=pl.CostEstimate(
             flops=2_000_000_000, bytes_accessed=12_000_000, transcendentals=256
         ),

time: 145 us -> 144 us (level)
  local copies, waits for them, and re-layouts: 3.3 us -> 1.71 us
    unnamed x17 -> x15, local copies, waits for them, and re-layouts: 1.65 us -> 0.06 us
where the time goes in v7:
time: 144 us
  blocking collectives  113 us (78%)
  Pallas kernels  17.3 us (12%)
  starting transfers between devices  4.08 us (3%)
  waiting for transfers between devices  2.85 us (2%)
  other arithmetic  2.62 us (2%)
  local copies, waits for them, and re-layouts  1.71 us (1%)
    all_to_all x7, blocking collectives, exchange(): lax.all_to_all(value, axis, split_axis=0, concat_axis=0, tiled=True, axis...  113 us
    pallas_call x1, Pallas kernels, run_main(): pl.pallas_call(main_kernel, out_shape=(jax.ShapeDtypeStruct((SHARDS // 2,...  13.5 us
    pallas_call x2, Pallas kernels, run_owner(): pl.pallas_call(kernel, out_shape=jax.ShapeDtypeStruct((owners, rows + TER...  2.88 us
  transfers between devices with their start and end apart: 2, of which 2 were waited for; matrix products, arithmetic and copies ran while one was open for 2% of the time, Pallas kernels for 1%

profile of v7, /device:TPU:32, one launch (start us, length us, event | category | flops | bytes accessed | tf_op | source)
XLA Modules:
  0.0 143.7 jit_solution(9375651252284458825)
XLA Ops:
  0.6 1.0 convert_element_type.69
  1.7 12.2 %all_to_all.35 = bf16[4,512,128]{2,1,0:T(8,128)(2,1)S(1)} all-to-all(bf16[4,512,128]{2,1,0:T(8,128)(2,1)S(1)} %broadcast_in_dim.28), channel_id=1, replica_groups={{0,8,16,24},{2,10,18,26},{4,12,20,28},{6,14,22,30},{1,3,5,7},{9,11,13,1..., dimensions={0} | all-to-all | bytes 1048576 | tf_op jit(solution)/shard_map/all_to_all | solution.py:35
  13.9 0.3 broadcast_in_dim.30
  14.2 20.9 %all_to_all.36 = bf16[4,2048,128]{2,1,0:T(8,128)(2,1)S(1)} all-to-all(bf16[4,2048,128]{2,1,0:T(8,128)(2,1)S(1)} %broadcast_in_dim.30), channel_id=1, replica_groups={{0,2,4,6},{8,10,12,14},{16,18,20,22},{24,26,28,30},{1,9,17,25},{3,11,19..., dimensions={0} | all-to-all | bytes 4194304 | tf_op jit(solution)/shard_map/all_to_all | solution.py:35
  35.1 2.0 %collective-permute-start = (bf16[8192,128]{1,0:T(8,128)(2,1)S(1)}, bf16[8192,128]{1,0:T(8,128)(2,1)}, u32[]{:S(2)}, u32[]{:S(2)}) collective-permute-start(bf16[8192,128]{1,0:T(8,128)(2,1)S(1)} %bitcast.29), channel_id=1, source_target_pairs={{0,1},{1,0},{2,3},{3,2},{4,5},{5,4},{6,7},{7,6},{8,9},{9,8},{10,11... | collective-permute-start | bytes 6291464 | tf_op jit(solution)/shard_map/ppermute | solution.py:418
  37.4 0.3 convert_reduce_fusion
  37.8 0.1 select_reduce_fusion
  38.2 0.1 mul.58
  38.3 0.1 bitcast_compare_fusion
  38.4 0.3 bitcast_reduce_fusion
  39.1 0.8 fusion.4
  40.4 0.9 collective-permute-done.other_hbm
  41.4 13.5 %shard_map.103 = (bf16[16,400,128]{2,1,0:T(8,128)(2,1)S(1)}, bf16[16,400,128]{2,1,0:T(8,128)(2,1)S(1)}, f32[2,128]{1,0:T(2,128)}) custom-call(s32[4096]{0:T(1024)S(1)} %reshape.99.index_ref, s32[4096]{0:T(1024)S(1)} %reshape.101.place_ref, s32[32]{0:T(128)S(1)} %fusion.19.order_ref, bf16[8192,128]{1,0:T(8,128)(2,1)S(1)} %bitcast.30, ...), custom_call_target="tpu_custom_call" | custom-call | flops 2000000000 | bytes 12000000 | tf_op jit(solution)/shard_map/pallas_call | solution.py:187
  54.9 2.0 %collective-permute-start.1 = (bf16[16,400,128]{2,1,0:T(8,128)(2,1)S(1)}, bf16[16,400,128]{2,1,0:T(8,128)(2,1)S(1)}, u32[]{:S(2)}, u32[]{:S(2)}) collective-permute-start(bf16[16,400,128]{2,1,0:T(8,128)(2,1)S(1)} %get-tuple-element.33), channel_id=1, source_target_pairs={{0,1},{1,0},{2,3},{3,2},{4,5},{5,4},{6,7},{7,6},{8,9},{9,8},{10,11... | collective-permute-start | bytes 4915208 | tf_op jit(solution)/shard_map/ppermute | solution.py:435
  57.0 1.4 %shard_map.104.base_ref = bf16[16,640,128]{2,1,0:T(8,128)(2,1)S(1)} custom-call(bf16[16,400,128]{2,1,0:T(8,128)(2,1)S(1)} %get-tuple-element.32.kept_ref), custom_call_target="tpu_custom_call" | custom-call | flops 550000000 | bytes 5000000 | tf_op jit(solution)/shard_map/pallas_call | solution.py:264
  58.4 1.9 %collective-permute-done.1.got_ref = bf16[16,400,128]{2,1,0:T(8,128)(2,1)S(1)} collective-permute-done((bf16[16,400,128]{2,1,0:T(8,128)(2,1)S(1)}, bf16[16,400,128]{2,1,0:T(8,128)(2,1)S(1)}, u32[]{:S(2)}, u32[]{:S(2)}) %collective-permute-start.1) | collective-permute-done | bytes 1638432 | tf_op jit(solution)/shard_map/ppermute | solution.py:435
  60.3 1.4 shard_map.105
  61.8 21.8 %all_to_all.37 = bf16[4,2560,128]{2,1,0:T(8,128)(2,1)S(1)} all-to-all(bf16[4,2560,128]{2,1,0:T(8,128)(2,1)S(1)} %bitcast.28), channel_id=1, replica_groups={{0,8,16,24},{2,10,18,26},{4,12,20,28},{6,14,22,30},{1,3,5,7},{9,11,13,1..., dimensions={0} | all-to-all | bytes 5242880 | tf_op jit(solution)/shard_map/all_to_all | solution.py:35
  83.6 0.8 reduce_sum.60
  84.4 11.3 %all_to_all.38.got_ref = bf16[4,640,128]{2,1,0:T(8,128)(2,1)S(1)} all-to-all(bf16[4,640,128]{2,1,0:T(8,128)(2,1)S(1)} %bitcast.32), channel_id=1, replica_groups={{0,2,4,6},{8,10,12,14},{16,18,20,22},{24,26,28,30},{1,9,17,25},{3,11,19..., dimensions={0} | all-to-all | bytes 1310720 | tf_op jit(solution)/shard_map/all_to_all | solution.py:35
  95.9 11.2 %all_to_all.39 = bf16[4,160,128]{2,1,0:T(8,128)(2,1)S(1)} all-to-all(bf16[4,160,128]{2,1,0:T(8,128)(2,1)S(1)} %shard_map.106), channel_id=1, replica_groups={{0,32,64,96},{128,160,192,224},{256,288,320,352},{384,416,448,480},{1,3..., dimensions={0} | all-to-all | bytes 327680 | tf_op jit(solution)/shard_map/all_to_all | solution.py:35
  107.2 26.3 %all_to_all.40.got_ref = bf16[4,136,128]{2,1,0:T(8,128)(2,1)S(1)} all-to-all(bf16[4,136,128]{2,1,0:T(8,128)(2,1)S(1)} %pad_maximum_fusion), channel_id=1, replica_groups={{0,128,256,384},{32,160,288,416},{64,192,320,448},{96,224,352,480},{1,1..., dimensions={0} | all-to-all | bytes 278528 | tf_op jit(solution)/shard_map/all_to_all | solution.py:35
  133.5 9.3 %all_to_all.41 = bf16[4,128,128]{2,1,0:T(8,128)(2,1)S(1)} all-to-all(bf16[4,128,128]{2,1,0:T(8,128)(2,1)S(1)} %shard_map.107), channel_id=1, replica_groups={{0,32,64,96},{128,160,192,224},{256,288,320,352},{384,416,448,480},{1,3..., dimensions={0} | all-to-all | bytes 262144 | tf_op jit(solution)/shard_map/all_to_all | solution.py:35
  142.8 0.8 shard_map.108
  (49 shorter events, 1.7 us)
Async XLA Ops:
  14.1 23.0 %copy-start.5 = (bf16[1024]{0:T(1024)(128)(2,1)S(1)}, bf16[1024]{0:T(1024)(128)(2,1)}, u32[]{:S(2)}) copy-start(bf16[1024]{0:T(1024)(128)(2,1)} %param.15) | copy-start | bytes 6148
  14.1 23.1 %copy-start.6 = (s32[2,128]{1,0:T(2,128)S(1)}, s32[2,128]{1,0:T(2,128)}, u32[]{:S(2)}) copy-start(s32[2,128]{1,0:T(2,128)} %param.10) | copy-start | bytes 3076
  14.2 23.2 %copy-start.3 = (s32[2,128,16]{1,2,0:T(8,128)S(1)}, s32[2,128,16]{1,2,0:T(8,128)}, u32[]{:S(2)}) copy-start(s32[2,128,16]{1,2,0:T(8,128)} %param.9) | copy-start | bytes 49156
  14.2 23.1 %copy-start.4 = (s32[2,128,16,1]{1,3,2,0:T(1,128)S(1)}, s32[2,128,16,1]{1,3,2,0:T(1,128)}, u32[]{:S(2)}) copy-start(s32[2,128,16,1]{1,3,2,0:T(1,128)} %param.8) | copy-start | bytes 49156
  35.1 6.3 %copy-start.1 = (bf16[512,1024]{1,0:T(8,128)(2,1)S(1)}, bf16[512,1024]{1,0:T(8,128)(2,1)}, u32[]{:S(2)}) copy-start(bf16[512,1024]{1,0:T(8,128)(2,1)} %w_input_ref.1) | copy-start | bytes 3145732
  35.1 6.3 %collective-permute-start = (bf16[8192,128]{1,0:T(8,128)(2,1)S(1)}, bf16[8192,128]{1,0:T(8,128)(2,1)}, u32[]{:S(2)}, u32[]{:S(2)}) collective-permute-start(bf16[8192,128]{1,0:T(8,128)(2,1)S(1)} %bitcast.29), channel_id=1, source_target_pairs={{0,1},{1,0},{2,3},{3,2},{4,5},{5,4},{6,7},{7,6},{8,9},{9,8},{10,11... | collective-permute-start | bytes 6291464 | tf_op jit(solution)/shard_map/ppermute | solution.py:418
  54.9 5.4 %collective-permute-start.1 = (bf16[16,400,128]{2,1,0:T(8,128)(2,1)S(1)}, bf16[16,400,128]{2,1,0:T(8,128)(2,1)S(1)}, u32[]{:S(2)}, u32[]{:S(2)}) collective-permute-start(bf16[16,400,128]{2,1,0:T(8,128)(2,1)S(1)} %get-tuple-element.33), channel_id=1, source_target_pairs={{0,1},{1,0},{2,3},{3,2},{4,5},{5,4},{6,7},{7,6},{8,9},{9,8},{10,11... | collective-permute-start | bytes 4915208 | tf_op jit(solution)/shard_map/ppermute | solution.py:435
  84.4 58.4 %copy-start = (f32[512,128]{1,0:T(8,128)S(1)}, f32[512,128]{1,0:T(8,128)}, u32[]{:S(2)}) copy-start(f32[512,128]{1,0:T(8,128)} %table_ref.1) | copy-start | bytes 786436
  84.4 58.4 %copy-start.2 = (f32[512,128]{1,0:T(8,128)S(1)}, f32[512,128]{1,0:T(8,128)}, u32[]{:S(2)}) copy-start(f32[512,128]{1,0:T(8,128)} %sums_ref.1) | copy-start | bytes 786436

commit v8 on v6

--- a/solution.py
+++ b/solution.py
@@ -57,12 +57,13 @@
     other_ref,
     label_ref,
     w_input_ref,
-    w_hidden_ref,
+    w_hidden_hbm,
     w_output_ref,
     ids_ref,
     kept_ref,
     sent_ref,
     logit_ref,
+    w_hidden_ref,
     table_ref,
     pooled_ref,
     slot_ref,
@@ -70,9 +71,12 @@
     turned_ref,
     back_ref,
     term_ref,
+    weight_sem,
 ):
     half = own_ref.shape[0]
     samples = pooled_ref.shape[0] // SLOTS
+    fetch = pltpu.make_async_copy(w_hidden_hbm, w_hidden_ref, weight_sem)
+    fetch.start()
 
     def widen(step, carry):
         at = pl.multiple_of(step * 256, 256)
@@ -115,6 +119,7 @@
         [pooled_ref[slot * samples : (slot + 1) * samples, :].astype(bf16) for slot in range(SLOTS)],
         axis=1,
     )
+    fetch.wait()
     w_input = w_input_ref[...]
     w_hidden = w_hidden_ref[...]
     w_output = w_output_ref[...].astype(f32)
@@ -178,9 +183,10 @@
             jax.ShapeDtypeStruct((SHARDS // 2, SENT_ROWS, width), bf16),
             jax.ShapeDtypeStruct((BATCHES, samples // BATCHES), f32),
         ),
-        in_specs=[smem] * 3 + [vmem] * 7,
+        in_specs=[smem] * 3 + [vmem] * 4 + [pl.BlockSpec(memory_space=pl.ANY)] + [vmem] * 2,
         out_specs=(vmem, vmem, vmem),
         scratch_shapes=[
+            pltpu.VMEM(w_hidden.shape, bf16),
             pltpu.VMEM((2 * own.shape[0], width), f32),
             pltpu.VMEM((samples * SLOTS, width), f32),
             pltpu.VMEM((SHARDS * GRAD_ROWS, width), f32),
@@ -188,8 +194,9 @@
             pltpu.VMEM((SLOTS * width, samples), bf16),
             pltpu.VMEM((8, samples, width), bf16),
             pltpu.VMEM((8, SLOTS * width, width), f32),
+            pltpu.SemaphoreType.DMA(()),
         ],
-        compiler_params=pltpu.CompilerParams(vmem_limit_bytes=24 * 1024 * 1024),
+        compiler_params=pltpu.CompilerParams(vmem_limit_bytes=44 * 1024 * 1024),
         cost_estimate=pl.CostEstimate(
             flops=2_000_000_000, bytes_accessed=12_000_000, transcendentals=256
         ),

time: 145 us -> 143 us (0.986)
  local copies, waits for them, and re-layouts: 3.3 us -> 1.71 us
    unnamed x17 -> x15, local copies, waits for them, and re-layouts: 1.65 us -> 0.06 us
where the time goes in v8:
time: 143 us
  blocking collectives  113 us (79%)
  Pallas kernels  16.6 us (12%)
  starting transfers between devices  4.08 us (3%)
  waiting for transfers between devices  2.85 us (2%)
  other arithmetic  2.62 us (2%)
  local copies, waits for them, and re-layouts  1.71 us (1%)
    all_to_all x7, blocking collectives, exchange(): lax.all_to_all(value, axis, split_axis=0, concat_axis=0, tiled=True, axis...  113 us
    pallas_call x1, Pallas kernels, run_main(): pl.pallas_call(main_kernel, out_shape=(jax.ShapeDtypeStruct((SHARDS // 2,...  12.8 us
    pallas_call x2, Pallas kernels, run_owner(): pl.pallas_call(kernel, out_shape=jax.ShapeDtypeStruct((owners, rows + TER...  2.88 us
  transfers between devices with their start and end apart: 2, of which 2 were waited for; matrix products, arithmetic and copies ran while one was open for 2% of the time, Pallas kernels for 1%

profile of v8, /device:TPU:32, one launch (start us, length us, event | category | flops | bytes accessed | tf_op | source)
XLA Modules:
  0.0 142.9 jit_solution(15578348623663329607)
XLA Ops:
  0.6 1.0 convert_element_type.69
  1.7 12.2 %all_to_all.35 = bf16[4,512,128]{2,1,0:T(8,128)(2,1)S(1)} all-to-all(bf16[4,512,128]{2,1,0:T(8,128)(2,1)S(1)} %broadcast_in_dim.28), channel_id=1, replica_groups={{0,8,16,24},{2,10,18,26},{4,12,20,28},{6,14,22,30},{1,3,5,7},{9,11,13,1..., dimensions={0} | all-to-all | bytes 1048576 | tf_op jit(solution)/shard_map/all_to_all | solution.py:35
  13.9 0.3 broadcast_in_dim.30
  14.2 20.9 %all_to_all.36 = bf16[4,2048,128]{2,1,0:T(8,128)(2,1)S(1)} all-to-all(bf16[4,2048,128]{2,1,0:T(8,128)(2,1)S(1)} %broadcast_in_dim.30), channel_id=1, replica_groups={{0,2,4,6},{8,10,12,14},{16,18,20,22},{24,26,28,30},{1,9,17,25},{3,11,19..., dimensions={0} | all-to-all | bytes 4194304 | tf_op jit(solution)/shard_map/all_to_all | solution.py:35
  35.1 2.0 %collective-permute-start = (bf16[8192,128]{1,0:T(8,128)(2,1)S(1)}, bf16[8192,128]{1,0:T(8,128)(2,1)}, u32[]{:S(2)}, u32[]{:S(2)}) collective-permute-start(bf16[8192,128]{1,0:T(8,128)(2,1)S(1)} %bitcast.29), channel_id=1, source_target_pairs={{0,1},{1,0},{2,3},{3,2},{4,5},{5,4},{6,7},{7,6},{8,9},{9,8},{10,11... | collective-permute-start | bytes 6291464 | tf_op jit(solution)/shard_map/ppermute | solution.py:408
  37.4 0.3 convert_reduce_fusion
  37.8 0.1 select_reduce_fusion
  38.2 0.1 mul.58
  38.3 0.1 bitcast_compare_fusion
  38.4 0.3 bitcast_reduce_fusion
  39.1 0.8 fusion.4
  40.4 0.9 collective-permute-done.other_ref
  41.4 12.8 %shard_map.103 = (bf16[16,400,128]{2,1,0:T(8,128)(2,1)S(1)}, bf16[16,400,128]{2,1,0:T(8,128)(2,1)S(1)}, f32[2,128]{1,0:T(2,128)}) custom-call(s32[4096]{0:T(1024)S(1)} %reshape.99.index_ref, s32[4096]{0:T(1024)S(1)} %reshape.101.place_ref, s32[32]{0:T(128)S(1)} %fusion.19.order_ref, bf16[8192,128]{1,0:T(8,128)(2,1)S(1)} %bitcast.30, ...), custom_call_target="tpu_custom_call" | custom-call | flops 2000000000 | bytes 12000000 | tf_op jit(solution)/shard_map/pallas_call | solution.py:179
  54.2 2.0 %collective-permute-start.1 = (bf16[16,400,128]{2,1,0:T(8,128)(2,1)S(1)}, bf16[16,400,128]{2,1,0:T(8,128)(2,1)S(1)}, u32[]{:S(2)}, u32[]{:S(2)}) collective-permute-start(bf16[16,400,128]{2,1,0:T(8,128)(2,1)S(1)} %get-tuple-element.33), channel_id=1, source_target_pairs={{0,1},{1,0},{2,3},{3,2},{4,5},{5,4},{6,7},{7,6},{8,9},{9,8},{10,11... | collective-permute-start | bytes 4915208 | tf_op jit(solution)/shard_map/ppermute | solution.py:425
  56.2 1.4 %shard_map.104.base_ref = bf16[16,640,128]{2,1,0:T(8,128)(2,1)S(1)} custom-call(bf16[16,400,128]{2,1,0:T(8,128)(2,1)S(1)} %get-tuple-element.32.kept_ref), custom_call_target="tpu_custom_call" | custom-call | flops 550000000 | bytes 5000000 | tf_op jit(solution)/shard_map/pallas_call | solution.py:254
  57.7 1.9 %collective-permute-done.1.got_ref = bf16[16,400,128]{2,1,0:T(8,128)(2,1)S(1)} collective-permute-done((bf16[16,400,128]{2,1,0:T(8,128)(2,1)S(1)}, bf16[16,400,128]{2,1,0:T(8,128)(2,1)S(1)}, u32[]{:S(2)}, u32[]{:S(2)}) %collective-permute-start.1) | collective-permute-done | bytes 1638432 | tf_op jit(solution)/shard_map/ppermute | solution.py:425
  59.6 1.4 %shard_map.105 = bf16[16,640,128]{2,1,0:T(8,128)(2,1)S(1)} custom-call(bf16[16,640,128]{2,1,0:T(8,128)(2,1)S(1)} %shard_map.104.base_ref, bf16[16,400,128]{2,1,0:T(8,128)(2,1)S(1)} %collective-permute-done.1.got_ref), custom_call_target="tpu_custom_call" | custom-call | flops 550000000 | bytes 5000000 | tf_op jit(solution)/shard_map/pallas_call | solution.py:254
  61.0 21.8 %all_to_all.37 = bf16[4,2560,128]{2,1,0:T(8,128)(2,1)S(1)} all-to-all(bf16[4,2560,128]{2,1,0:T(8,128)(2,1)S(1)} %bitcast.28), channel_id=1, replica_groups={{0,8,16,24},{2,10,18,26},{4,12,20,28},{6,14,22,30},{1,3,5,7},{9,11,13,1..., dimensions={0} | all-to-all | bytes 5242880 | tf_op jit(solution)/shard_map/all_to_all | solution.py:35
  82.8 0.8 reduce_sum.60
  83.7 11.3 %all_to_all.38.got_ref = bf16[4,640,128]{2,1,0:T(8,128)(2,1)S(1)} all-to-all(bf16[4,640,128]{2,1,0:T(8,128)(2,1)S(1)} %bitcast.32), channel_id=1, replica_groups={{0,2,4,6},{8,10,12,14},{16,18,20,22},{24,26,28,30},{1,9,17,25},{3,11,19..., dimensions={0} | all-to-all | bytes 1310720 | tf_op jit(solution)/shard_map/all_to_all | solution.py:35
  95.1 11.2 %all_to_all.39 = bf16[4,160,128]{2,1,0:T(8,128)(2,1)S(1)} all-to-all(bf16[4,160,128]{2,1,0:T(8,128)(2,1)S(1)} %shard_map.106), channel_id=1, replica_groups={{0,32,64,96},{128,160,192,224},{256,288,320,352},{384,416,448,480},{1,3..., dimensions={0} | all-to-all | bytes 327680 | tf_op jit(solution)/shard_map/all_to_all | solution.py:35
  106.5 26.3 %all_to_all.40.got_ref = bf16[4,136,128]{2,1,0:T(8,128)(2,1)S(1)} all-to-all(bf16[4,136,128]{2,1,0:T(8,128)(2,1)S(1)} %pad_maximum_fusion), channel_id=1, replica_groups={{0,128,256,384},{32,160,288,416},{64,192,320,448},{96,224,352,480},{1,1..., dimensions={0} | all-to-all | bytes 278528 | tf_op jit(solution)/shard_map/all_to_all | solution.py:35
  132.8 9.3 %all_to_all.41 = bf16[4,128,128]{2,1,0:T(8,128)(2,1)S(1)} all-to-all(bf16[4,128,128]{2,1,0:T(8,128)(2,1)S(1)} %shard_map.107), channel_id=1, replica_groups={{0,32,64,96},{128,160,192,224},{256,288,320,352},{384,416,448,480},{1,3..., dimensions={0} | all-to-all | bytes 262144 | tf_op jit(solution)/shard_map/all_to_all | solution.py:35
  142.1 0.8 shard_map.108
  (49 shorter events, 1.7 us)
Async XLA Ops:
  14.1 23.0 %copy-start.5 = (bf16[1024]{0:T(1024)(128)(2,1)S(1)}, bf16[1024]{0:T(1024)(128)(2,1)}, u32[]{:S(2)}) copy-start(bf16[1024]{0:T(1024)(128)(2,1)} %param.15) | copy-start | bytes 6148
  14.1 23.1 %copy-start.6 = (s32[2,128]{1,0:T(2,128)S(1)}, s32[2,128]{1,0:T(2,128)}, u32[]{:S(2)}) copy-start(s32[2,128]{1,0:T(2,128)} %param.10) | copy-start | bytes 3076
  14.2 23.2 %copy-start.3 = (s32[2,128,16]{1,2,0:T(8,128)S(1)}, s32[2,128,16]{1,2,0:T(8,128)}, u32[]{:S(2)}) copy-start(s32[2,128,16]{1,2,0:T(8,128)} %param.9) | copy-start | bytes 49156
  14.2 23.1 %copy-start.4 = (s32[2,128,16,1]{1,3,2,0:T(1,128)S(1)}, s32[2,128,16,1]{1,3,2,0:T(1,128)}, u32[]{:S(2)}) copy-start(s32[2,128,16,1]{1,3,2,0:T(1,128)} %param.8) | copy-start | bytes 49156
  35.1 6.3 %copy-start.1 = (bf16[512,1024]{1,0:T(8,128)(2,1)S(1)}, bf16[512,1024]{1,0:T(8,128)(2,1)}, u32[]{:S(2)}) copy-start(bf16[512,1024]{1,0:T(8,128)(2,1)} %w_input_ref.1) | copy-start | bytes 3145732
  35.1 6.3 %collective-permute-start = (bf16[8192,128]{1,0:T(8,128)(2,1)S(1)}, bf16[8192,128]{1,0:T(8,128)(2,1)}, u32[]{:S(2)}, u32[]{:S(2)}) collective-permute-start(bf16[8192,128]{1,0:T(8,128)(2,1)S(1)} %bitcast.29), channel_id=1, source_target_pairs={{0,1},{1,0},{2,3},{3,2},{4,5},{5,4},{6,7},{7,6},{8,9},{9,8},{10,11... | collective-permute-start | bytes 6291464 | tf_op jit(solution)/shard_map/ppermute | solution.py:408
  54.2 5.4 %collective-permute-start.1 = (bf16[16,400,128]{2,1,0:T(8,128)(2,1)S(1)}, bf16[16,400,128]{2,1,0:T(8,128)(2,1)S(1)}, u32[]{:S(2)}, u32[]{:S(2)}) collective-permute-start(bf16[16,400,128]{2,1,0:T(8,128)(2,1)S(1)} %get-tuple-element.33), channel_id=1, source_target_pairs={{0,1},{1,0},{2,3},{3,2},{4,5},{5,4},{6,7},{7,6},{8,9},{9,8},{10,11... | collective-permute-start | bytes 4915208 | tf_op jit(solution)/shard_map/ppermute | solution.py:425
  83.7 58.4 %copy-start = (f32[512,128]{1,0:T(8,128)S(1)}, f32[512,128]{1,0:T(8,128)}, u32[]{:S(2)}) copy-start(f32[512,128]{1,0:T(8,128)} %table_ref.1) | copy-start | bytes 786436
  83.7 58.4 %copy-start.2 = (f32[512,128]{1,0:T(8,128)S(1)}, f32[512,128]{1,0:T(8,128)}, u32[]{:S(2)}) copy-start(f32[512,128]{1,0:T(8,128)} %sums_ref.1) | copy-start | bytes 786436

commit v9 on v8

--- a/solution.py
+++ b/solution.py
@@ -68,6 +68,10 @@
     pooled_ref,
     slot_ref,
     turn_ref,
+    pool_ref,
+    act_ref,
+    one_ref,
+    two_ref,
     turned_ref,
     back_ref,
     term_ref,
@@ -86,74 +90,101 @@
 
     lax.fori_loop(0, half // 256, widen, 0)
 
-    def look(step, carry):
-        slot_ref[pl.ds(pl.multiple_of(step * 512, 512), 512), :] = jnp.zeros((512, 128), f32)
+    def look(sample):
+        for slot in range(SLOTS):
+            first = sample * LOOK + slot * HOT
+            total = table_ref[pl.ds(index_ref[first], 1), :]
+            for hot in range(1, HOT):
+                total = total + table_ref[pl.ds(index_ref[first + hot], 1), :]
+            pooled_ref[pl.ds(slot * samples + sample, 1), :] = total
+
+    def put(sample):
+        for slot in range(SLOTS):
+            first = sample * LOOK + slot * HOT
+            row = pooled_ref[pl.ds(slot * samples + sample, 1), :]
+            for hot in range(HOT):
+                slot_ref[pl.ds(place_ref[first + hot], 1), :] = row
+
+    def first_look(step, carry):
+        slot_ref[pl.ds(pl.multiple_of(step * 1024, 1024), 1024), :] = jnp.zeros((1024, 128), f32)
         for turn in range(16):
-            sample = step * 16 + turn
-            for slot in range(SLOTS):
-                first = sample * LOOK + slot * HOT
-                total = table_ref[pl.ds(index_ref[first], 1), :]
-                for hot in range(1, HOT):
-                    total = total + table_ref[pl.ds(index_ref[first + hot], 1), :]
-                pooled_ref[pl.ds(slot * samples + sample, 1), :] = total
+            look(step * 16 + turn)
         return carry
 
-    lax.fori_loop(0, samples // 16, look, 0)
+    lax.fori_loop(0, 8, first_look, 0)
 
     features = SLOTS * 128
-    for slot in range(SLOTS):
-        for b in range(BATCHES):
+
+    def dense(b, work, start):
+        rows = slice(b * 128, (b + 1) * 128)
+        for slot in range(SLOTS):
             block = pooled_ref[slot * samples + b * 128 : slot * samples + (b + 1) * 128, :]
-            turn_ref[b * features + slot * 128 : b * features + (slot + 1) * 128, :] = jnp.transpose(block)
-    turned_ref[...] = jnp.concatenate(
-        [
-            jnp.concatenate(
-                [turn_ref[pl.ds(b * features + s, 16, stride=SHARDS), :] for s in range(SHARDS)],
-                axis=0,
+            turn_ref[slot * 128 : (slot + 1) * 128, :] = jnp.transpose(block)
+            pool_ref[:, slot * 128 : (slot + 1) * 128] = block.astype(bf16)
+        turned_ref[:, rows] = jnp.concatenate(
+            [turn_ref[pl.ds(s, 16, stride=SHARDS), :] for s in range(SHARDS)], axis=0
+        ).astype(bf16)
+
+        def one(c, carry):
+            cols = pl.ds(pl.multiple_of(c * 1024, 1024), 1024)
+            pre = dot(pool_ref[...], w_input_ref[:, cols], ((1,), (0,)))
+            one_ref[c] = pre
+            act_ref[:, cols] = jnp.maximum(pre, 0.0).astype(bf16)
+            for turn in range(32):
+                work(start + c * 32 + turn)
+            return carry
+
+        lax.fori_loop(0, 1, one, 0)
+
+        def two(c, carry):
+            cols = pl.ds(pl.multiple_of(c * 1024, 1024), 1024)
+            pre = dot(act_ref[...], w_hidden_ref[:, cols], ((1,), (0,)))
+            two_ref[c] = pre
+            act = jnp.maximum(pre, 0.0).astype(bf16).astype(f32)
+            part = act * w_output_ref[:, cols].astype(f32)
+            for turn in range(48):
+                work(start + 32 + c * 48 + turn)
+            return carry + part
+
+        part = lax.fori_loop(0, 1, two, jnp.zeros((128, 1024), f32))
+        logits = jnp.sum(part, axis=1, keepdims=True)
+        logit_ref[b : b + 1, :] = jnp.transpose(jnp.broadcast_to(logits, (128, 128)))[0:1, :]
+        slope = jax.nn.sigmoid(logits) - column(label_ref[b : b + 1, :])
+        for c in range(1):
+            cols = slice(c * 1024, (c + 1) * 1024)
+            act_ref[:, cols] = jnp.where(
+                two_ref[c] > 0, slope * w_output_ref[:, cols].astype(f32), 0.0
             ).astype(bf16)
-            for b in range(BATCHES)
-        ],
-        axis=1,
-    )
-    pooled = jnp.concatenate(
-        [pooled_ref[slot * samples : (slot + 1) * samples, :].astype(bf16) for slot in range(SLOTS)],
-        axis=1,
-    )
+
+        def back(c, carry):
+            lines = pl.ds(pl.multiple_of(c * 1024, 1024), 1024)
+            grad = dot(act_ref[...], w_hidden_ref[lines, :], ((1,), (1,)))
+            grad = jnp.where(one_ref[c] > 0, grad, 0.0).astype(bf16)
+            for h in range(8):
+                back_ref[8 * c + h, rows, :] = grad[:, h * 128 : (h + 1) * 128]
+            for turn in range(48):
+                work(start + 80 + c * 48 + turn)
+            return carry
+
+        lax.fori_loop(0, 1, back, 0)
+        back_one = jnp.concatenate([back_ref[j, rows, :] for j in range(8)], axis=1)
+        back_in = dot(back_one, w_input_ref[...], ((1,), (1,))).astype(bf16).astype(f32)
+        for slot in range(SLOTS):
+            pooled_ref[slot * samples + b * 128 : slot * samples + (b + 1) * 128, :] = back_in[
+                :, slot * 128 : (slot + 1) * 128
+            ]
+
     fetch.wait()
-    w_input = w_input_ref[...]
-    w_hidden = w_hidden_ref[...]
-    w_output = w_output_ref[...].astype(f32)
-    labels = jnp.concatenate([column(label_ref[b : b + 1, :]) for b in range(BATCHES)], axis=0)
-    pre_one = dot(pooled, w_input, ((1,), (0,)))
-    act_one = jnp.maximum(pre_one, 0.0).astype(bf16)
-    pre_two = dot(act_one, w_hidden, ((1,), (0,)))
-    act_two = jnp.maximum(pre_two, 0.0).astype(bf16).astype(f32)
-    logits = jnp.sum(act_two * w_output, axis=1, keepdims=True)
-    for b in range(BATCHES):
-        part = jnp.broadcast_to(logits[b * 128 : (b + 1) * 128], (128, 128))
-        logit_ref[b : b + 1, :] = jnp.transpose(part)[0:1, :]
-    slope = jax.nn.sigmoid(logits) - labels
-    back_two = jnp.where(pre_two > 0, slope * w_output, 0.0).astype(bf16)
-    back_one = dot(back_two, w_hidden, ((1,), (1,)))
-    back_one = jnp.where(pre_one > 0, back_one, 0.0).astype(bf16)
-    back_in = dot(back_one, w_input, ((1,), (1,))).astype(bf16).astype(f32)
-    for slot in range(SLOTS):
-        pooled_ref[slot * samples : (slot + 1) * samples, :] = back_in[:, slot * 128 : (slot + 1) * 128]
-    for j in range(8):
-        back_ref[j] = back_one[:, j * 128 : (j + 1) * 128]
-
-    def scatter(step, carry):
+    dense(0, look, 128)
+    dense(1, put, 0)
+
+    def last_put(step, carry):
         term_ref[step] = dot(turned_ref[...], back_ref[step], ((1,), (0,)))
-        for turn in range(32):
-            sample = step * 32 + turn
-            for slot in range(SLOTS):
-                first = sample * LOOK + slot * HOT
-                row = pooled_ref[pl.ds(slot * samples + sample, 1), :]
-                for hot in range(HOT):
-                    slot_ref[pl.ds(place_ref[first + hot], 1), :] = row
+        for turn in range(16):
+            put(128 + step * 16 + turn)
         return carry
 
-    lax.fori_loop(0, samples // 32, scatter, 0)
+    lax.fori_loop(0, 8, last_put, 0)
 
     for target, base in ((sent_ref, SHARDS // 2), (kept_ref, 0)):
 
@@ -190,7 +221,11 @@
             pltpu.VMEM((2 * own.shape[0], width), f32),
             pltpu.VMEM((samples * SLOTS, width), f32),
             pltpu.VMEM((SHARDS * GRAD_ROWS, width), f32),
-            pltpu.VMEM((BATCHES * SLOTS * width, samples // BATCHES), f32),
+            pltpu.VMEM((SLOTS * width, 128), f32),
+            pltpu.VMEM((128, SLOTS * width), bf16),
+            pltpu.VMEM((128, 1024), bf16),
+            pltpu.VMEM((1, 128, 1024), f32),
+            pltpu.VMEM((1, 128, 1024), f32),
             pltpu.VMEM((SLOTS * width, samples), bf16),
             pltpu.VMEM((8, samples, width), bf16),
             pltpu.VMEM((8, SLOTS * width, width), f32),

time: 143 us -> 142 us (level)
  no operation moved by 1% of the time
where the time goes in v9:
time: 142 us
  blocking collectives  113 us (80%)
  Pallas kernels  15.6 us (11%)
  starting transfers between devices  4.07 us (3%)
  waiting for transfers between devices  2.86 us (2%)
  other arithmetic  2.62 us (2%)
  local copies, waits for them, and re-layouts  1.71 us (1%)
    all_to_all x7, blocking collectives, exchange(): lax.all_to_all(value, axis, split_axis=0, concat_axis=0, tiled=True, axis...  113 us
    pallas_call x1, Pallas kernels, run_main(): pl.pallas_call(main_kernel, out_shape=(jax.ShapeDtypeStruct((SHARDS // 2,...  11.8 us
    pallas_call x2, Pallas kernels, run_owner(): pl.pallas_call(kernel, out_shape=jax.ShapeDtypeStruct((owners, rows + TER...  2.87 us
  transfers between devices with their start and end apart: 2, of which 2 were waited for; matrix products, arithmetic and copies ran while one was open for 2% of the time, Pallas kernels for 1%

profile of v9, /device:TPU:32, one launch (start us, length us, event | category | flops | bytes accessed | tf_op | source)
XLA Modules:
  0.0 142.0 jit_solution(2868354556810153050)
XLA Ops:
  0.6 1.0 convert_element_type.69
  1.7 12.2 %all_to_all.35 = bf16[4,512,128]{2,1,0:T(8,128)(2,1)S(1)} all-to-all(bf16[4,512,128]{2,1,0:T(8,128)(2,1)S(1)} %broadcast_in_dim.28), channel_id=1, replica_groups={{0,8,16,24},{2,10,18,26},{4,12,20,28},{6,14,22,30},{1,3,5,7},{9,11,13,1..., dimensions={0} | all-to-all | bytes 1048576 | tf_op jit(solution)/shard_map/all_to_all | solution.py:35
  13.9 0.3 broadcast_in_dim.30
  14.2 20.9 %all_to_all.36 = bf16[4,2048,128]{2,1,0:T(8,128)(2,1)S(1)} all-to-all(bf16[4,2048,128]{2,1,0:T(8,128)(2,1)S(1)} %broadcast_in_dim.30), channel_id=1, replica_groups={{0,2,4,6},{8,10,12,14},{16,18,20,22},{24,26,28,30},{1,9,17,25},{3,11,19..., dimensions={0} | all-to-all | bytes 4194304 | tf_op jit(solution)/shard_map/all_to_all | solution.py:35
  35.1 2.0 %collective-permute-start = (bf16[8192,128]{1,0:T(8,128)(2,1)S(1)}, bf16[8192,128]{1,0:T(8,128)(2,1)}, u32[]{:S(2)}, u32[]{:S(2)}) collective-permute-start(bf16[8192,128]{1,0:T(8,128)(2,1)S(1)} %bitcast.29), channel_id=1, source_target_pairs={{0,1},{1,0},{2,3},{3,2},{4,5},{5,4},{6,7},{7,6},{8,9},{9,8},{10,11... | collective-permute-start | bytes 6291464 | tf_op jit(solution)/shard_map/ppermute | solution.py:443
  37.4 0.3 convert_reduce_fusion
  37.8 0.1 select_reduce_fusion
  38.2 0.1 mul.58
  38.3 0.1 bitcast_compare_fusion
  38.4 0.3 bitcast_reduce_fusion
  39.1 0.8 fusion.4
  40.4 0.9 collective-permute-done.other_ref
  41.4 11.8 %shard_map.103 = (bf16[16,400,128]{2,1,0:T(8,128)(2,1)S(1)}, bf16[16,400,128]{2,1,0:T(8,128)(2,1)S(1)}, f32[2,128]{1,0:T(2,128)}) custom-call(s32[4096]{0:T(1024)S(1)} %reshape.99.index_ref, s32[4096]{0:T(1024)S(1)} %reshape.101.place_ref, s32[32]{0:T(128)S(1)} %fusion.19.order_ref, bf16[8192,128]{1,0:T(8,128)(2,1)S(1)} %bitcast.30, ...), custom_call_target="tpu_custom_call" | custom-call | flops 2000000000 | bytes 12000000 | tf_op jit(solution)/shard_map/pallas_call | solution.py:210
  53.2 2.0 %collective-permute-start.1 = (bf16[16,400,128]{2,1,0:T(8,128)(2,1)S(1)}, bf16[16,400,128]{2,1,0:T(8,128)(2,1)S(1)}, u32[]{:S(2)}, u32[]{:S(2)}) collective-permute-start(bf16[16,400,128]{2,1,0:T(8,128)(2,1)S(1)} %get-tuple-element.33), channel_id=1, source_target_pairs={{0,1},{1,0},{2,3},{3,2},{4,5},{5,4},{6,7},{7,6},{8,9},{9,8},{10,11... | collective-permute-start | bytes 4915208 | tf_op jit(solution)/shard_map/ppermute | solution.py:460
  55.3 1.4 %shard_map.104.base_ref = bf16[16,640,128]{2,1,0:T(8,128)(2,1)S(1)} custom-call(bf16[16,400,128]{2,1,0:T(8,128)(2,1)S(1)} %get-tuple-element.32.kept_ref), custom_call_target="tpu_custom_call" | custom-call | flops 550000000 | bytes 5000000 | tf_op jit(solution)/shard_map/pallas_call | solution.py:289
  56.7 1.9 %collective-permute-done.1.got_ref = bf16[16,400,128]{2,1,0:T(8,128)(2,1)S(1)} collective-permute-done((bf16[16,400,128]{2,1,0:T(8,128)(2,1)S(1)}, bf16[16,400,128]{2,1,0:T(8,128)(2,1)S(1)}, u32[]{:S(2)}, u32[]{:S(2)}) %collective-permute-start.1) | collective-permute-done | bytes 1638432 | tf_op jit(solution)/shard_map/ppermute | solution.py:460
  58.6 1.4 %shard_map.105 = bf16[16,640,128]{2,1,0:T(8,128)(2,1)S(1)} custom-call(bf16[16,640,128]{2,1,0:T(8,128)(2,1)S(1)} %shard_map.104.base_ref, bf16[16,400,128]{2,1,0:T(8,128)(2,1)S(1)} %collective-permute-done.1.got_ref), custom_call_target="tpu_custom_call" | custom-call | flops 550000000 | bytes 5000000 | tf_op jit(solution)/shard_map/pallas_call | solution.py:289
  60.1 21.8 %all_to_all.37 = bf16[4,2560,128]{2,1,0:T(8,128)(2,1)S(1)} all-to-all(bf16[4,2560,128]{2,1,0:T(8,128)(2,1)S(1)} %bitcast.28), channel_id=1, replica_groups={{0,8,16,24},{2,10,18,26},{4,12,20,28},{6,14,22,30},{1,3,5,7},{9,11,13,1..., dimensions={0} | all-to-all | bytes 5242880 | tf_op jit(solution)/shard_map/all_to_all | solution.py:35
  81.9 0.8 reduce_sum.60
  82.7 11.3 %all_to_all.38.got_ref = bf16[4,640,128]{2,1,0:T(8,128)(2,1)S(1)} all-to-all(bf16[4,640,128]{2,1,0:T(8,128)(2,1)S(1)} %bitcast.32), channel_id=1, replica_groups={{0,2,4,6},{8,10,12,14},{16,18,20,22},{24,26,28,30},{1,9,17,25},{3,11,19..., dimensions={0} | all-to-all | bytes 1310720 | tf_op jit(solution)/shard_map/all_to_all | solution.py:35
  94.2 11.2 %all_to_all.39 = bf16[4,160,128]{2,1,0:T(8,128)(2,1)S(1)} all-to-all(bf16[4,160,128]{2,1,0:T(8,128)(2,1)S(1)} %shard_map.106), channel_id=1, replica_groups={{0,32,64,96},{128,160,192,224},{256,288,320,352},{384,416,448,480},{1,3..., dimensions={0} | all-to-all | bytes 327680 | tf_op jit(solution)/shard_map/all_to_all | solution.py:35
  105.5 26.3 %all_to_all.40.got_ref = bf16[4,136,128]{2,1,0:T(8,128)(2,1)S(1)} all-to-all(bf16[4,136,128]{2,1,0:T(8,128)(2,1)S(1)} %pad_maximum_fusion), channel_id=1, replica_groups={{0,128,256,384},{32,160,288,416},{64,192,320,448},{96,224,352,480},{1,1..., dimensions={0} | all-to-all | bytes 278528 | tf_op jit(solution)/shard_map/all_to_all | solution.py:35
  131.8 9.3 %all_to_all.41 = bf16[4,128,128]{2,1,0:T(8,128)(2,1)S(1)} all-to-all(bf16[4,128,128]{2,1,0:T(8,128)(2,1)S(1)} %shard_map.107), channel_id=1, replica_groups={{0,32,64,96},{128,160,192,224},{256,288,320,352},{384,416,448,480},{1,3..., dimensions={0} | all-to-all | bytes 262144 | tf_op jit(solution)/shard_map/all_to_all | solution.py:35
  141.1 0.8 shard_map.108
  (49 shorter events, 1.7 us)
Async XLA Ops:
  14.1 23.0 %copy-start.5 = (bf16[1024]{0:T(1024)(128)(2,1)S(1)}, bf16[1024]{0:T(1024)(128)(2,1)}, u32[]{:S(2)}) copy-start(bf16[1024]{0:T(1024)(128)(2,1)} %param.15) | copy-start | bytes 6148
  14.1 23.1 %copy-start.6 = (s32[2,128]{1,0:T(2,128)S(1)}, s32[2,128]{1,0:T(2,128)}, u32[]{:S(2)}) copy-start(s32[2,128]{1,0:T(2,128)} %param.10) | copy-start | bytes 3076
  14.2 23.2 %copy-start.3 = (s32[2,128,16]{1,2,0:T(8,128)S(1)}, s32[2,128,16]{1,2,0:T(8,128)}, u32[]{:S(2)}) copy-start(s32[2,128,16]{1,2,0:T(8,128)} %param.9) | copy-start | bytes 49156
  14.2 23.1 %copy-start.4 = (s32[2,128,16,1]{1,3,2,0:T(1,128)S(1)}, s32[2,128,16,1]{1,3,2,0:T(1,128)}, u32[]{:S(2)}) copy-start(s32[2,128,16,1]{1,3,2,0:T(1,128)} %param.8) | copy-start | bytes 49156
  35.1 6.3 %copy-start.1 = (bf16[512,1024]{1,0:T(8,128)(2,1)S(1)}, bf16[512,1024]{1,0:T(8,128)(2,1)}, u32[]{:S(2)}) copy-start(bf16[512,1024]{1,0:T(8,128)(2,1)} %w_input_ref.1) | copy-start | bytes 3145732
  35.1 6.3 %collective-permute-start = (bf16[8192,128]{1,0:T(8,128)(2,1)S(1)}, bf16[8192,128]{1,0:T(8,128)(2,1)}, u32[]{:S(2)}, u32[]{:S(2)}) collective-permute-start(bf16[8192,128]{1,0:T(8,128)(2,1)S(1)} %bitcast.29), channel_id=1, source_target_pairs={{0,1},{1,0},{2,3},{3,2},{4,5},{5,4},{6,7},{7,6},{8,9},{9,8},{10,11... | collective-permute-start | bytes 6291464 | tf_op jit(solution)/shard_map/ppermute | solution.py:443
  53.2 5.4 %collective-permute-start.1 = (bf16[16,400,128]{2,1,0:T(8,128)(2,1)S(1)}, bf16[16,400,128]{2,1,0:T(8,128)(2,1)S(1)}, u32[]{:S(2)}, u32[]{:S(2)}) collective-permute-start(bf16[16,400,128]{2,1,0:T(8,128)(2,1)S(1)} %get-tuple-element.33), channel_id=1, source_target_pairs={{0,1},{1,0},{2,3},{3,2},{4,5},{5,4},{6,7},{7,6},{8,9},{9,8},{10,11... | collective-permute-start | bytes 4915208 | tf_op jit(solution)/shard_map/ppermute | solution.py:460
  82.7 58.4 %copy-start = (f32[512,128]{1,0:T(8,128)S(1)}, f32[512,128]{1,0:T(8,128)}, u32[]{:S(2)}) copy-start(f32[512,128]{1,0:T(8,128)} %table_ref.1) | copy-start | bytes 786436
  82.7 58.4 %copy-start.2 = (f32[512,128]{1,0:T(8,128)S(1)}, f32[512,128]{1,0:T(8,128)}, u32[]{:S(2)}) copy-start(f32[512,128]{1,0:T(8,128)} %sums_ref.1) | copy-start | bytes 786436

commit v10 on v9

--- a/solution.py
+++ b/solution.py
@@ -88,7 +88,7 @@
         table_ref[pl.ds(half + at, 256), :] = other_ref[pl.ds(at, 256), :].astype(f32)
         return carry
 
-    lax.fori_loop(0, half // 256, widen, 0)
+    lax.fori_loop(0, half // 256, widen, 0, unroll=4)
 
     def look(sample):
         for slot in range(SLOTS):
@@ -111,7 +111,7 @@
             look(step * 16 + turn)
         return carry
 
-    lax.fori_loop(0, 8, first_look, 0)
+    lax.fori_loop(0, 8, first_look, 0, unroll=2)
 
     features = SLOTS * 128
 
@@ -184,7 +184,7 @@
             put(128 + step * 16 + turn)
         return carry
 
-    lax.fori_loop(0, 8, last_put, 0)
+    lax.fori_loop(0, 8, last_put, 0, unroll=2)
 
     for target, base in ((sent_ref, SHARDS // 2), (kept_ref, 0)):
 
@@ -199,7 +199,7 @@
             target[owner, GRAD_ROWS + TERM_ROWS : SENT_ROWS, :] = ids_ref[base + owner]
             return carry
 
-        lax.fori_loop(0, SHARDS // 2, pack, 0, unroll=4)
+        lax.fori_loop(0, SHARDS // 2, pack, 0, unroll=16)
 
 
 def run_main(index, place, order, own, other, labels, w_input, w_hidden, w_output, ids):

time: 142 us -> 142 us (level)
  no operation moved by 1% of the time
where the time goes in v10:
time: 142 us
  blocking collectives  113 us (80%)
  Pallas kernels  15.3 us (11%)
  starting transfers between devices  4.07 us (3%)
  waiting for transfers between devices  2.86 us (2%)
  other arithmetic  2.62 us (2%)
  local copies, waits for them, and re-layouts  1.71 us (1%)
    all_to_all x7, blocking collectives, exchange(): lax.all_to_all(value, axis, split_axis=0, concat_axis=0, tiled=True, axis...  113 us
    pallas_call x1, Pallas kernels, run_main(): pl.pallas_call(main_kernel, out_shape=(jax.ShapeDtypeStruct((SHARDS // 2,...  11.5 us
    pallas_call x2, Pallas kernels, run_owner(): pl.pallas_call(kernel, out_shape=jax.ShapeDtypeStruct((owners, rows + TER...  2.87 us
  transfers between devices with their start and end apart: 2, of which 2 were waited for; matrix products, arithmetic and copies ran while one was open for 2% of the time, Pallas kernels for 1%

profile of v10, /device:TPU:32, one launch (start us, length us, event | category | flops | bytes accessed | tf_op | source)
XLA Modules:
  0.0 141.7 jit_solution(16090219871918258473)
XLA Ops:
  0.6 1.0 convert_element_type.69
  1.7 12.2 %all_to_all.35 = bf16[4,512,128]{2,1,0:T(8,128)(2,1)S(1)} all-to-all(bf16[4,512,128]{2,1,0:T(8,128)(2,1)S(1)} %broadcast_in_dim.28), channel_id=1, replica_groups={{0,8,16,24},{2,10,18,26},{4,12,20,28},{6,14,22,30},{1,3,5,7},{9,11,13,1..., dimensions={0} | all-to-all | bytes 1048576 | tf_op jit(solution)/shard_map/all_to_all | solution.py:35
  13.9 0.3 broadcast_in_dim.30
  14.2 20.9 %all_to_all.36 = bf16[4,2048,128]{2,1,0:T(8,128)(2,1)S(1)} all-to-all(bf16[4,2048,128]{2,1,0:T(8,128)(2,1)S(1)} %broadcast_in_dim.30), channel_id=1, replica_groups={{0,2,4,6},{8,10,12,14},{16,18,20,22},{24,26,28,30},{1,9,17,25},{3,11,19..., dimensions={0} | all-to-all | bytes 4194304 | tf_op jit(solution)/shard_map/all_to_all | solution.py:35
  35.1 2.0 %collective-permute-start = (bf16[8192,128]{1,0:T(8,128)(2,1)S(1)}, bf16[8192,128]{1,0:T(8,128)(2,1)}, u32[]{:S(2)}, u32[]{:S(2)}) collective-permute-start(bf16[8192,128]{1,0:T(8,128)(2,1)S(1)} %bitcast.29), channel_id=1, source_target_pairs={{0,1},{1,0},{2,3},{3,2},{4,5},{5,4},{6,7},{7,6},{8,9},{9,8},{10,11... | collective-permute-start | bytes 6291464 | tf_op jit(solution)/shard_map/ppermute | solution.py:443
  37.4 0.3 convert_reduce_fusion
  37.8 0.1 select_reduce_fusion
  38.2 0.1 mul.58
  38.3 0.1 bitcast_compare_fusion
  38.4 0.3 bitcast_reduce_fusion
  39.1 0.8 fusion.4
  40.4 0.9 collective-permute-done.other_ref
  41.4 11.5 %shard_map.103 = (bf16[16,400,128]{2,1,0:T(8,128)(2,1)S(1)}, bf16[16,400,128]{2,1,0:T(8,128)(2,1)S(1)}, f32[2,128]{1,0:T(2,128)}) custom-call(s32[4096]{0:T(1024)S(1)} %reshape.99.index_ref, s32[4096]{0:T(1024)S(1)} %reshape.101.place_ref, s32[32]{0:T(128)S(1)} %fusion.19.order_ref, bf16[8192,128]{1,0:T(8,128)(2,1)S(1)} %bitcast.30, ...), custom_call_target="tpu_custom_call" | custom-call | flops 2000000000 | bytes 12000000 | tf_op jit(solution)/shard_map/pallas_call | solution.py:210
  52.9 2.0 %collective-permute-start.1 = (bf16[16,400,128]{2,1,0:T(8,128)(2,1)S(1)}, bf16[16,400,128]{2,1,0:T(8,128)(2,1)S(1)}, u32[]{:S(2)}, u32[]{:S(2)}) collective-permute-start(bf16[16,400,128]{2,1,0:T(8,128)(2,1)S(1)} %get-tuple-element.33), channel_id=1, source_target_pairs={{0,1},{1,0},{2,3},{3,2},{4,5},{5,4},{6,7},{7,6},{8,9},{9,8},{10,11... | collective-permute-start | bytes 4915208 | tf_op jit(solution)/shard_map/ppermute | solution.py:460
  55.0 1.4 %shard_map.104.base_ref = bf16[16,640,128]{2,1,0:T(8,128)(2,1)S(1)} custom-call(bf16[16,400,128]{2,1,0:T(8,128)(2,1)S(1)} %get-tuple-element.32.kept_ref), custom_call_target="tpu_custom_call" | custom-call | flops 550000000 | bytes 5000000 | tf_op jit(solution)/shard_map/pallas_call | solution.py:289
  56.4 1.9 %collective-permute-done.1.got_ref = bf16[16,400,128]{2,1,0:T(8,128)(2,1)S(1)} collective-permute-done((bf16[16,400,128]{2,1,0:T(8,128)(2,1)S(1)}, bf16[16,400,128]{2,1,0:T(8,128)(2,1)S(1)}, u32[]{:S(2)}, u32[]{:S(2)}) %collective-permute-start.1) | collective-permute-done | bytes 1638432 | tf_op jit(solution)/shard_map/ppermute | solution.py:460
  58.3 1.4 %shard_map.105 = bf16[16,640,128]{2,1,0:T(8,128)(2,1)S(1)} custom-call(bf16[16,640,128]{2,1,0:T(8,128)(2,1)S(1)} %shard_map.104.base_ref, bf16[16,400,128]{2,1,0:T(8,128)(2,1)S(1)} %collective-permute-done.1.got_ref), custom_call_target="tpu_custom_call" | custom-call | flops 550000000 | bytes 5000000 | tf_op jit(solution)/shard_map/pallas_call | solution.py:289
  59.8 21.8 %all_to_all.37 = bf16[4,2560,128]{2,1,0:T(8,128)(2,1)S(1)} all-to-all(bf16[4,2560,128]{2,1,0:T(8,128)(2,1)S(1)} %bitcast.28), channel_id=1, replica_groups={{0,8,16,24},{2,10,18,26},{4,12,20,28},{6,14,22,30},{1,3,5,7},{9,11,13,1..., dimensions={0} | all-to-all | bytes 5242880 | tf_op jit(solution)/shard_map/all_to_all | solution.py:35
  81.6 0.8 reduce_sum.60
  82.4 11.3 %all_to_all.38.got_ref = bf16[4,640,128]{2,1,0:T(8,128)(2,1)S(1)} all-to-all(bf16[4,640,128]{2,1,0:T(8,128)(2,1)S(1)} %bitcast.32), channel_id=1, replica_groups={{0,2,4,6},{8,10,12,14},{16,18,20,22},{24,26,28,30},{1,9,17,25},{3,11,19..., dimensions={0} | all-to-all | bytes 1310720 | tf_op jit(solution)/shard_map/all_to_all | solution.py:35
  93.8 11.2 %all_to_all.39 = bf16[4,160,128]{2,1,0:T(8,128)(2,1)S(1)} all-to-all(bf16[4,160,128]{2,1,0:T(8,128)(2,1)S(1)} %shard_map.106), channel_id=1, replica_groups={{0,32,64,96},{128,160,192,224},{256,288,320,352},{384,416,448,480},{1,3..., dimensions={0} | all-to-all | bytes 327680 | tf_op jit(solution)/shard_map/all_to_all | solution.py:35
  105.2 26.3 %all_to_all.40.got_ref = bf16[4,136,128]{2,1,0:T(8,128)(2,1)S(1)} all-to-all(bf16[4,136,128]{2,1,0:T(8,128)(2,1)S(1)} %pad_maximum_fusion), channel_id=1, replica_groups={{0,128,256,384},{32,160,288,416},{64,192,320,448},{96,224,352,480},{1,1..., dimensions={0} | all-to-all | bytes 278528 | tf_op jit(solution)/shard_map/all_to_all | solution.py:35
  131.5 9.3 %all_to_all.41 = bf16[4,128,128]{2,1,0:T(8,128)(2,1)S(1)} all-to-all(bf16[4,128,128]{2,1,0:T(8,128)(2,1)S(1)} %shard_map.107), channel_id=1, replica_groups={{0,32,64,96},{128,160,192,224},{256,288,320,352},{384,416,448,480},{1,3..., dimensions={0} | all-to-all | bytes 262144 | tf_op jit(solution)/shard_map/all_to_all | solution.py:35
  140.8 0.8 shard_map.108
  (49 shorter events, 1.7 us)
Async XLA Ops:
  14.1 23.0 %copy-start.5 = (bf16[1024]{0:T(1024)(128)(2,1)S(1)}, bf16[1024]{0:T(1024)(128)(2,1)}, u32[]{:S(2)}) copy-start(bf16[1024]{0:T(1024)(128)(2,1)} %param.15) | copy-start | bytes 6148
  14.1 23.1 %copy-start.6 = (s32[2,128]{1,0:T(2,128)S(1)}, s32[2,128]{1,0:T(2,128)}, u32[]{:S(2)}) copy-start(s32[2,128]{1,0:T(2,128)} %param.10) | copy-start | bytes 3076
  14.2 23.2 %copy-start.3 = (s32[2,128,16]{1,2,0:T(8,128)S(1)}, s32[2,128,16]{1,2,0:T(8,128)}, u32[]{:S(2)}) copy-start(s32[2,128,16]{1,2,0:T(8,128)} %param.9) | copy-start | bytes 49156
  14.2 23.1 %copy-start.4 = (s32[2,128,16,1]{1,3,2,0:T(1,128)S(1)}, s32[2,128,16,1]{1,3,2,0:T(1,128)}, u32[]{:S(2)}) copy-start(s32[2,128,16,1]{1,3,2,0:T(1,128)} %param.8) | copy-start | bytes 49156
  35.1 6.3 %copy-start.1 = (bf16[512,1024]{1,0:T(8,128)(2,1)S(1)}, bf16[512,1024]{1,0:T(8,128)(2,1)}, u32[]{:S(2)}) copy-start(bf16[512,1024]{1,0:T(8,128)(2,1)} %w_input_ref.1) | copy-start | bytes 3145732
  35.1 6.3 %collective-permute-start = (bf16[8192,128]{1,0:T(8,128)(2,1)S(1)}, bf16[8192,128]{1,0:T(8,128)(2,1)}, u32[]{:S(2)}, u32[]{:S(2)}) collective-permute-start(bf16[8192,128]{1,0:T(8,128)(2,1)S(1)} %bitcast.29), channel_id=1, source_target_pairs={{0,1},{1,0},{2,3},{3,2},{4,5},{5,4},{6,7},{7,6},{8,9},{9,8},{10,11... | collective-permute-start | bytes 6291464 | tf_op jit(solution)/shard_map/ppermute | solution.py:443
  52.9 5.4 %collective-permute-start.1 = (bf16[16,400,128]{2,1,0:T(8,128)(2,1)S(1)}, bf16[16,400,128]{2,1,0:T(8,128)(2,1)S(1)}, u32[]{:S(2)}, u32[]{:S(2)}) collective-permute-start(bf16[16,400,128]{2,1,0:T(8,128)(2,1)S(1)} %get-tuple-element.33), channel_id=1, source_target_pairs={{0,1},{1,0},{2,3},{3,2},{4,5},{5,4},{6,7},{7,6},{8,9},{9,8},{10,11... | collective-permute-start | bytes 4915208 | tf_op jit(solution)/shard_map/ppermute | solution.py:460
  82.4 58.4 %copy-start = (f32[512,128]{1,0:T(8,128)S(1)}, f32[512,128]{1,0:T(8,128)}, u32[]{:S(2)}) copy-start(f32[512,128]{1,0:T(8,128)} %table_ref.1) | copy-start | bytes 786436
  82.4 58.4 %copy-start.2 = (f32[512,128]{1,0:T(8,128)S(1)}, f32[512,128]{1,0:T(8,128)}, u32[]{:S(2)}) copy-start(f32[512,128]{1,0:T(8,128)} %sums_ref.1) | copy-start | bytes 786436
